TPU v7x, 256 devices: a whole 4x4x8 slice. The times are simulated.
256 devices in a mesh: mem: 64 (over z, x, y_hi), grp: 4 (over y_lo, core).
Axes of the slice: x: 4, y: 4 (y_hi: 2, y_lo: 2; y = y_hi * 2 + y_lo), z: 8, core: 2. Of those that a mesh axis runs over, the one named last changes fastest.
Arguments:
- fields: bfloat16 [4, 1024, 4, 64, 256], P('grp', 'mem'), may hold values from -6 to 6
- centres: bfloat16 [4, 64, 1024, 1024], P('grp', 'mem'), may hold values from -0.03125 to 1
- sides: int32 [4, 64, 4, 2], P('grp', 'mem'), may hold values from 0 to 1
- quarters: int32 [4, 64, 4, 2], P('grp', 'mem'), may hold values from 0 to 4
Outputs:
- analysis: bfloat16 [4, 1024, 4, 64, 256], P('grp', 'mem')
All inputs are finite; a program needn't handle non-finite values.
Results may differ from a plain program's by a relative error of at most 0.006.
Values may be sent and summed in bfloat16 or wider, within the bound.
No kernel may reach another device: no remote copies, remote signals or barrier semaphores. Data moves between devices by JAX's collectives and lax.ppermute only.
A program may use at most 128 MiB of HBM per device.

v0:
```python
import jax
import jax.numpy as jnp
from jax import lax
from jax.sharding import PartitionSpec as P


def with_halo(block, sides, width):
    for axis, dim in sides:
        count = lax.axis_size(axis)
        forward = [(i, i + 1) for i in range(count - 1)]
        forward.append((count - 1, 0))
        backward = [(target, source) for source, target in forward]
        low = lax.ppermute(
            lax.slice_in_dim(block, block.shape[dim] - width, None, axis=dim), axis, forward
        )
        high = lax.ppermute(lax.slice_in_dim(block, 0, width, axis=dim), axis, backward)
        block = jnp.concatenate([low, block, high], axis=dim)
    return block


def body(fields, centres, sides, quarters):
    patch_field = lax.all_to_all(
        lax.all_to_all(fields, "mem", split_axis=3, concat_axis=1, tiled=True),
        "grp",
        split_axis=2,
        concat_axis=0,
        tiled=True,
    )
    levels = patch_field.shape[0]
    members = patch_field.shape[1]
    col_width = patch_field.shape[4]
    blocks = col_width // 64
    neighbours = with_halo(centres, (("grp", 0), ("mem", 1)), 1)
    centre_table = neighbours.reshape(9, members, members)
    side_row = sides[0, 0, :, 0]
    side_col = sides[0, 0, :, 1]
    own_index = jnp.zeros_like(side_row) + 4
    row_index = 6 * side_row + 1
    col_index = 3 + 2 * side_col
    diag_index = 6 * side_row + 2 * side_col
    frac_row = quarters[0, 0, :, 0].astype(jnp.float32) / 4.0
    frac_col = quarters[0, 0, :, 1].astype(jnp.float32) / 4.0
    weight_list = (
        (1.0 - frac_row) * (1.0 - frac_col),
        frac_row * (1.0 - frac_col),
        (1.0 - frac_row) * frac_col,
        frac_row * frac_col,
    )
    index_list = (own_index, row_index, col_index, diag_index)
    block_field = patch_field.reshape(levels, members, blocks, 64)
    blend = jnp.zeros((blocks, members, members), jnp.float32)
    for weight, index in zip(weight_list, index_list):
        blend = blend + weight[:, None, None] * jnp.take(centre_table, index, axis=0).astype(
            jnp.float32
        )
    blend_high = blend.astype(jnp.bfloat16)
    blend_rest = (blend - blend_high.astype(jnp.float32)).astype(jnp.bfloat16)
    analysed = jnp.einsum(
        "lksc,skj->ljsc", block_field, blend_high, preferred_element_type=jnp.float32
    )
    analysed = analysed + jnp.einsum(
        "lksc,skj->ljsc", block_field, blend_rest, preferred_element_type=jnp.float32
    )
    result = analysed.reshape(levels, members, 1, 1, col_width).astype(jnp.bfloat16)
    return lax.all_to_all(
        lax.all_to_all(result, "mem", split_axis=1, concat_axis=3, tiled=True),
        "grp",
        split_axis=0,
        concat_axis=2,
        tiled=True,
    )


def solution(mesh):
    return jax.shard_map(
        body,
        mesh=mesh,
        in_specs=(
            P("grp", "mem", None, None, None),
            P("grp", "mem", None, None),
            P("grp", "mem", None, None),
            P("grp", "mem", None, None),
        ),
        out_specs=P("grp", "mem", None, None, None),
        check_vma=False,
    )
```

profile of v0, /device:TPU:1, one launch (start us, length us, event | category | flops | bytes accessed | tf_op | source)
XLA Modules:
  0.0 578.9 jit_solution(4104387037001293739)
XLA Ops:
  0.0 2.7 collective-permute-start
  3.2 42.7 %collective-permute-done = bf16[1,1,1024,1024]{3,2,1,0:T(8,128)(2,1)S(1)} collective-permute-done((bf16[1,1,1024,1024]{3,2,1,0:T(8,128)(2,1)}, bf16[1,1,1024,1024]{3,2,1,0:T(8,128)(2,1)S(1)}, u32[]{:S(2)}, u32[]{:S(2)}) %collective-permute-start) | collective-permute-done | bytes 2097184 | tf_op jit(solution)/shard_map/ppermute | solution.py:13
  47.4 3.1 constant_dynamic-update-slice_fusion.1
  52.4 3.7 collective-permute-start.2
  56.1 7.5 %collective-permute-start.3 = (bf16[3,1,1024,1024]{3,2,1,0:T(8,128)(2,1)}, bf16[3,1,1024,1024]{3,2,1,0:T(8,128)(2,1)}, u32[]{:S(2)}, u32[]{:S(2)}) collective-permute-start(bf16[3,1,1024,1024]{3,2,1,0:T(8,128)(2,1)} %constant_dynamic-update-slice_fusion), channel_id=1, source_target_pairs={{4,0},{8,4},{12,8},{16,12},{20,16},{24,20},{28,24},{32,28},{36,32}... | collective-permute-start | bytes 18874376 | tf_op jit(solution)/shard_map/ppermute | solution.py:16
  64.8 286.2 %all_to_all.69 = bf16[1,16,4,64,256]{4,1,2,0,3:T(8,128)(2,1)S(1)} all-to-all(bf16[1,16,4,64,256]{4,1,2,0,3:T(8,128)(2,1)S(1)} %copy.12), channel_id=1, replica_groups=mesh['mem'=64,'grp'=4] {'mem'}, dimensions={3} | all-to-all | bytes 4194304 | tf_op jit(solution)/shard_map/all_to_all | solution.py:23
  352.5 5.6 all-to-all-start.1
  358.2 24.8 %all-to-all-done.1 = bf16[1,1024,4,1,256]{4,1,3,0,2:T(8,128)(2,1)S(1)} async-done(((bf16[1,1024,4,1,256]{4,1,3,0,2:T(8,128)(2,1)}), bf16[1,1024,4,1,256]{4,1,3,0,2:T(8,128)(2,1)S(1)}, u32[]{:S(2)}, u32[]{:S(2)}) %all-to-all-start.1) | async-done | bytes 2097184 | tf_op jit(solution)/shard_map/all_to_all | solution.py:22
  387.2 10.0 %pad_maximum_fusion = bf16[3,3,1024,1024]{3,2,1,0:T(8,128)(2,1)S(1)} fusion(bf16[3,1,1024,1024]{3,2,1,0:T(8,128)(2,1)} %collective-permute-done.3, bf16[3,1,1024,1024]{3,2,1,0:T(8,128)(2,1)} %constant_dynamic-update-slice_fusion, bf16[3,1,1024,1024]{3,2,1,0:T(8,128)(2,1)} %collective-permute-done.2), kind=kLoop, calls=%fused_computation.8 | loop fusion | flops 18874368 | bytes 37748736 | tf_op jit(solution)/shard_map/concatenate | solution.py:17
  397.2 6.9 %fusion.6 = (bf16[9,512,1024]{2,1,0:T(8,128)(2,1)}, bf16[9,512,1024]{2,1,0:T(8,128)(2,1)}) fusion(bf16[9,1024,1024]{2,1,0:T(8,128)(2,1)S(1)} %bitcast.61), kind=kLoop, calls=%fused_computation.43 | loop fusion | bytes 37748736 | tf_op jit(solution)/shard_map/jit(_take)/gather | solution.py:53
  404.1 6.5 %gather_fusion.4 = bf16[4,512,1024]{2,1,0:T(8,128)(2,1)} fusion(bf16[9,512,1024]{2,1,0:T(8,128)(2,1)} %get-tuple-element.12, s32[1024]{0:T(1024)S(1)} %get-tuple-element.23), kind=kCustom, calls=%fused_computation.4.clone | custom fusion | bytes 8388624 | tf_op jit(solution)/shard_map/jit(_take)/gather | solution.py:53
  410.6 6.4 %gather_fusion.5 = bf16[4,512,1024]{2,1,0:T(8,128)(2,1)} fusion(bf16[9,512,1024]{2,1,0:T(8,128)(2,1)} %get-tuple-element.13, s32[1024]{0:T(1024)S(1)} %get-tuple-element.23), kind=kCustom, calls=%fused_computation.5.clone | custom fusion | bytes 8388624 | tf_op jit(solution)/shard_map/jit(_take)/gather | solution.py:53
  417.0 6.6 %gather_fusion.6 = bf16[4,512,1024]{2,1,0:T(8,128)(2,1)} fusion(bf16[9,512,1024]{2,1,0:T(8,128)(2,1)} %get-tuple-element.12, s32[1024]{0:T(1024)S(1)} %get-tuple-element.22), kind=kCustom, calls=%fused_computation.6.clone | custom fusion | bytes 8388624 | tf_op jit(solution)/shard_map/jit(_take)/gather | solution.py:53
  423.6 6.5 %gather_fusion.7 = bf16[4,512,1024]{2,1,0:T(8,128)(2,1)} fusion(bf16[9,512,1024]{2,1,0:T(8,128)(2,1)} %get-tuple-element.13, s32[1024]{0:T(1024)S(1)} %get-tuple-element.22), kind=kCustom, calls=%fused_computation.7.clone | custom fusion | bytes 8388624 | tf_op jit(solution)/shard_map/jit(_take)/gather | solution.py:53
  430.1 6.5 %gather_fusion.2 = bf16[4,512,1024]{2,1,0:T(8,128)(2,1)} fusion(bf16[9,512,1024]{2,1,0:T(8,128)(2,1)} %get-tuple-element.12, s32[1024]{0:T(1024)S(1)} %get-tuple-element.24), kind=kCustom, calls=%fused_computation.2.clone | custom fusion | bytes 8388624 | tf_op jit(solution)/shard_map/jit(_take)/gather | solution.py:53
  436.7 6.5 %gather_fusion.3 = bf16[4,512,1024]{2,1,0:T(8,128)(2,1)} fusion(bf16[9,512,1024]{2,1,0:T(8,128)(2,1)} %get-tuple-element.13, s32[1024]{0:T(1024)S(1)} %get-tuple-element.24), kind=kCustom, calls=%fused_computation.3.clone | custom fusion | bytes 8388624 | tf_op jit(solution)/shard_map/jit(_take)/gather | solution.py:53
  443.2 6.5 %gather_fusion = bf16[4,512,1024]{2,1,0:T(8,128)(2,1)} fusion(bf16[9,512,1024]{2,1,0:T(8,128)(2,1)} %get-tuple-element.12, s32[1024]{0:T(1024)S(1)} %get-tuple-element.25), kind=kCustom, calls=%fused_computation.clone | custom fusion | bytes 8388624 | tf_op jit(solution)/shard_map/jit(_take)/gather | solution.py:53
  449.7 6.6 %gather_fusion.1 = bf16[4,512,1024]{2,1,0:T(8,128)(2,1)} fusion(bf16[9,512,1024]{2,1,0:T(8,128)(2,1)} %get-tuple-element.13, s32[1024]{0:T(1024)S(1)} %get-tuple-element.25), kind=kCustom, calls=%fused_computation.1.clone | custom fusion | bytes 8388624 | tf_op jit(solution)/shard_map/jit(_take)/gather | solution.py:53
  456.3 13.9 %multiply_add_fusion = f32[4,1024,1024]{2,1,0:T(8,128)S(1)} fusion(bf16[4,512,1024]{2,1,0:T(8,128)(2,1)} %gather_fusion.1, bf16[4,512,1024]{2,1,0:T(8,128)(2,1)} %gather_fusion, bf16[4,512,1024]{2,1,0:T(8,128)(2,1)} %gather_fusion.3, bf16[4,512,1024]{2,1,0:T(8,128)(2,1)} %gather_fusion.2, bf16[4,512,1024]{2,1,0:T(8,128)(2,1)} %gather_fusion.5, ...), kind=kLoop, calls=%fused_computation.10 | loop fusion | flops 121634816 | bytes 50331724 | tf_op jit(solution)/shard_map/add | solution.py:53
  470.3 4.4 fusion
  474.7 4.1 fusion.2
  478.8 3.0 fusion.4
  484.5 60.1 %all_to_all.70 = bf16[4,1024,1,1,256]{4,0,3,2,1:T(4,128)(2,1)S(1)} all-to-all(bf16[4,1024,1,1,256]{4,0,3,2,1:T(4,128)(2,1)} %copy.19), channel_id=1, replica_groups=mesh['mem'=64,'grp'=4] {'mem'}, dimensions={1} | all-to-all | bytes 4194304 | tf_op jit(solution)/shard_map/all_to_all | solution.py:66
  544.9 32.0 %all_to_all.71 = bf16[4,16,1,64,256]{4,1,3,2,0:T(8,128)(2,1)S(1)} all-to-all(bf16[4,16,1,64,256]{4,1,3,2,0:T(8,128)(2,1)S(1)} %bitcast.70), channel_id=1, replica_groups=mesh['mem'=64,'grp'=4] {'grp'}, dimensions={0} | all-to-all | bytes 4194304 | tf_op jit(solution)/shard_map/all_to_all | solution.py:65
  (27 shorter events, 16.0 us)
Async XLA Ops:
  0.0 63.6 %copy-start.1 = (bf16[1,16,4,64,256]{4,3,2,1,0:T(8,128)(2,1)S(1)}, bf16[1,16,4,64,256]{4,3,2,1,0:T(8,128)(2,1)}, u32[]{:S(2)}) copy-start(bf16[1,16,4,64,256]{4,3,2,1,0:T(8,128)(2,1)} %param.6) | copy-start | bytes 6291460
  0.0 45.9 %collective-permute-start = (bf16[1,1,1024,1024]{3,2,1,0:T(8,128)(2,1)}, bf16[1,1,1024,1024]{3,2,1,0:T(8,128)(2,1)S(1)}, u32[]{:S(2)}, u32[]{:S(2)}) collective-permute-start(bf16[1,1,1024,1024]{3,2,1,0:T(8,128)(2,1)} %param.7), channel_id=1, source_target_pairs={{0,1},{1,2},{2,3},{3,0},{4,5},{5,6},{6,7},{7,4},{8,9},{9,10},{10,1... | collective-permute-start | bytes 6291464 | tf_op jit(solution)/shard_map/ppermute | solution.py:13
  2.7 48.2 %collective-permute-start.1 = (bf16[1,1,1024,1024]{3,2,1,0:T(8,128)(2,1)}, bf16[1,1,1024,1024]{3,2,1,0:T(8,128)(2,1)S(1)}, u32[]{:S(2)}, u32[]{:S(2)}) collective-permute-start(bf16[1,1,1024,1024]{3,2,1,0:T(8,128)(2,1)} %param.7), channel_id=1, source_target_pairs={{1,0},{2,1},{3,2},{0,3},{5,4},{6,5},{7,6},{4,7},{9,8},{10,9},{11,1... | collective-permute-start | bytes 6291464 | tf_op jit(solution)/shard_map/ppermute | solution.py:16
  52.4 334.8 %collective-permute-start.2 = (bf16[3,1,1024,1024]{3,2,1,0:T(8,128)(2,1)}, bf16[3,1,1024,1024]{3,2,1,0:T(8,128)(2,1)}, u32[]{:S(2)}, u32[]{:S(2)}) collective-permute-start(bf16[3,1,1024,1024]{3,2,1,0:T(8,128)(2,1)} %constant_dynamic-update-slice_fusion), channel_id=1, source_target_pairs={{0,4},{4,8},{8,12},{12,16},{16,20},{20,24},{24,28},{28,32},{32,36}... | collective-permute-start | bytes 18874376 | tf_op jit(solution)/shard_map/ppermute | solution.py:13
  56.1 331.1 %collective-permute-start.3 = (bf16[3,1,1024,1024]{3,2,1,0:T(8,128)(2,1)}, bf16[3,1,1024,1024]{3,2,1,0:T(8,128)(2,1)}, u32[]{:S(2)}, u32[]{:S(2)}) collective-permute-start(bf16[3,1,1024,1024]{3,2,1,0:T(8,128)(2,1)} %constant_dynamic-update-slice_fusion), channel_id=1, source_target_pairs={{4,0},{8,4},{12,8},{16,12},{20,16},{24,20},{28,24},{32,28},{36,32}... | collective-permute-start | bytes 18874376 | tf_op jit(solution)/shard_map/ppermute | solution.py:16
  64.8 293.4 %copy-start.3 = (s32[1,1,4,2]{2,3,1,0:T(2,128)S(1)}, s32[1,1,4,2]{2,3,1,0:T(2,128)}, u32[]{:S(2)}) copy-start(s32[1,1,4,2]{2,3,1,0:T(2,128)} %param.8) | copy-start | bytes 100
  64.8 293.4 %copy-start.2 = (s32[1,1,4,2]{2,3,1,0:T(2,128)S(1)}, s32[1,1,4,2]{2,3,1,0:T(2,128)}, u32[]{:S(2)}) copy-start(s32[1,1,4,2]{2,3,1,0:T(2,128)} %param.9) | copy-start | bytes 100
  352.5 30.4 %all-to-all-start.1 = ((bf16[1,1024,4,1,256]{4,1,3,0,2:T(8,128)(2,1)}), bf16[1,1024,4,1,256]{4,1,3,0,2:T(8,128)(2,1)S(1)}, u32[]{:S(2)}, u32[]{:S(2)}) async-start(bf16[1,1024,4,1,256]{4,1,3,0,2:T(8,128)(2,1)} %bitcast.67), calls=%async_computation.1 | async-start | bytes 4194304 | tf_op jit(solution)/shard_map/all_to_all | solution.py:22
  387.2 83.1 %copy-start = (bf16[4,1024,4,64]{1,3,0,2:T(8,128)(2,1)}, bf16[4,1024,4,64]{1,3,0,2:T(8,128)(2,1)S(1)}, u32[]{:S(2)}) copy-start(bf16[4,1024,4,64]{1,3,0,2:T(8,128)(2,1)S(1)} %copy.16) | copy-start | bytes 6291460
where the time goes:
time: 580 us; the launch traced here: 579 us
  blocking collectives  378 us (65%)
  local copies, waits for them, and re-layouts  77.1 us (13%)
  waiting for transfers between devices  67.8 us (12%)
  other arithmetic  27 us (5%)
  starting transfers between devices  20.1 us (3%)
  matrix products  8.49 us (1%)
    all_to_all x1, blocking collectives, body(): lax.all_to_all(fields, 'mem', split_axis=3, concat_axis=1, tiled=True)  286 us
    all_to_all x1, blocking collectives, body(): lax.all_to_all(result, 'mem', split_axis=1, concat_axis=3, tiled=True)  60.1 us
    gather x9, local copies, waits for them, and re-layouts, body(): jnp.take(centre_table, index, axis=0).astype(jnp.float32)  59.1 us
    ppermute x2, waiting for transfers between devices, with_halo(): lax.ppermute(lax.slice_in_dim(block, block.shape[dim] - width, None, axis...  42.7 us
    all_to_all x1, blocking collectives, body(): lax.all_to_all(lax.all_to_all(result, 'mem', split_axis=1, concat_axis=3,...  32 us
    all_to_all x1, waiting for transfers between devices, body(): lax.all_to_all(lax.all_to_all(fields, 'mem', split_axis=3, concat_axis=1,...  24.8 us
    add x1, other arithmetic, body(): blend + weight[:, None, None] * jnp.take(centre_table, index, axis=0).ast...  13.9 us
  transfers between devices with their start and end apart: 5, of which 3 were waited for; matrix products, arithmetic and copies ran while one was open for 2% of the time, Pallas kernels for 0%

commit v1 on v0

v1 whole, which is shorter than its diff:
```python
import functools

import jax
import jax.numpy as jnp
from jax import lax
from jax.experimental import pallas as pl
from jax.experimental.pallas import tpu as pltpu
from jax.sharding import PartitionSpec as P

AX = ("mem", "grp")
MEM = 64
GRP = 4
K = 1024
JQ = 256


def flat_perm(move):
    pairs = []
    for mem in range(MEM):
        for grp in range(GRP):
            to_mem, to_grp = move(mem, grp)
            pairs.append((mem * GRP + grp, (to_mem % MEM) * GRP + to_grp))
    return pairs


CORE = flat_perm(lambda m, g: (m, g ^ 1))
PAL = flat_perm(lambda m, g: (m, g ^ 2))
CROSS = flat_perm(lambda m, g: (m ^ 1, g ^ 2))
SIDE = flat_perm(lambda m, g: (m + 2 if m % 2 else m - 2, g))


def split_kernel(where_ref, centre_ref, *outs):
    grp = where_ref[0]
    parity = where_ref[1]
    row = lax.broadcasted_iota(jnp.int32, (JQ, K), 0)
    col = lax.broadcasted_iota(jnp.int32, (JQ, K), 1)
    base = (row // 4) * 16 + row % 4
    for rho in range(GRP):
        quarter = lax.bitwise_xor(lax.bitwise_xor(grp, rho), 2 * parity)
        pick = jnp.where(col == base + 4 * quarter, 1.0, 0.0).astype(jnp.bfloat16)
        outs[rho][...] = lax.dot_general(
            pick,
            centre_ref[...],
            (((1,), (1,)), ((), ())),
            preferred_element_type=jnp.float32,
        ).astype(jnp.bfloat16)


def split_centres(where, centre):
    return pl.pallas_call(
        split_kernel,
        out_shape=[jax.ShapeDtypeStruct((JQ, K), jnp.bfloat16)] * GRP,
        in_specs=[
            pl.BlockSpec(memory_space=pltpu.SMEM),
            pl.BlockSpec(memory_space=pltpu.VMEM),
        ],
        out_specs=[pl.BlockSpec(memory_space=pltpu.VMEM)] * GRP,
        compiler_params=pltpu.CompilerParams(vmem_limit_bytes=40 * 1024 * 1024),
        cost_estimate=pl.CostEstimate(flops=2 * K * K * K, bytes_accessed=4 * K * K, transcendentals=0),
    )(where, centre)


def apply_kernel(where_ref, params_ref, *refs):
    pieces = refs[:12]
    fields = refs[12:16]
    out_ref = refs[16]
    table, blend, sems = refs[17:]
    row = pl.program_id(0)
    grp = where_ref[0]
    parity = where_ref[1]

    @pl.when(row == 0)
    def _():
        copies = [
            pltpu.make_async_copy(pieces[i], table.at[i], sems.at[i]) for i in range(12)
        ]
        for copy in copies:
            copy.start()
        for copy in copies:
            copy.wait()

    lane = lax.broadcasted_iota(jnp.int32, (JQ, 128), 1)
    for pair in range(2):
        for half in range(2):
            sub = 2 * pair + half
            side_row = params_ref[row, sub, 0]
            side_col = params_ref[row, sub, 1]
            a = params_ref[row, sub, 2].astype(jnp.float32) * 0.25
            b = params_ref[row, sub, 3].astype(jnp.float32) * 0.25
            row2 = lax.bitwise_and(row + 2 * side_row - 1, 3)
            base2 = jnp.where(side_col == parity, 0, 4)
            i_own = 8 + lax.bitwise_xor(lax.bitwise_xor(row, grp), 2)
            i_row = 8 + lax.bitwise_xor(lax.bitwise_xor(row2, grp), 2)
            i_col = base2 + lax.bitwise_xor(row, grp)
            i_diag = base2 + lax.bitwise_xor(row2, grp)
            w_own = (1.0 - a) * (1.0 - b)
            w_row = a * (1.0 - b)
            w_col = (1.0 - a) * b
            w_diag = a * b

            @pl.loop(0, JQ // 32)
            def _(step):
                at = pl.ds(pl.multiple_of(step * 32, 32), 32)
                mixed = w_own * table[i_own, at, :].astype(jnp.float32)
                mixed = mixed + w_row * table[i_row, at, :].astype(jnp.float32)
                mixed = mixed + w_col * table[i_col, at, :].astype(jnp.float32)
                mixed = mixed + w_diag * table[i_diag, at, :].astype(jnp.float32)
                to = pl.ds(pl.multiple_of(half * JQ + step * 32, 32), 32)
                blend[to, :] = mixed.astype(jnp.bfloat16)

        for two in range(2):
            right = jnp.concatenate(
                [
                    fields[2 * two + i][:, 0, :, pair * 128 : pair * 128 + 128].reshape(K, 128)
                    for i in range(2)
                ],
                axis=1,
            )
            product = jnp.dot(blend[...], right, preferred_element_type=jnp.float32)
            for i in range(2):
                rho = 2 * two + i
                level = lax.bitwise_xor(grp, rho)
                low = product[:JQ, i * 128 : i * 128 + 128]
                high = product[JQ:, i * 128 : i * 128 + 128]
                out_ref[level, 0, :, pair * 128 : pair * 128 + 128] = jnp.where(
                    lane < 64, low, high
                ).astype(jnp.bfloat16)


def apply_transforms(where, params, pieces, fields):
    return pl.pallas_call(
        apply_kernel,
        grid=(4,),
        out_shape=jax.ShapeDtypeStruct((4, 4, JQ, 256), jnp.bfloat16),
        in_specs=[
            pl.BlockSpec(memory_space=pltpu.SMEM),
            pl.BlockSpec(memory_space=pltpu.SMEM),
        ]
        + [pl.BlockSpec(memory_space=pl.ANY)] * 12
        + [pl.BlockSpec((MEM, 1, 16, 256), lambda r: (0, r, 0, 0))] * 4,
        out_specs=pl.BlockSpec((4, 1, JQ, 256), lambda r: (0, r, 0, 0)),
        scratch_shapes=[
            pltpu.VMEM((12, JQ, K), jnp.bfloat16),
            pltpu.VMEM((2 * JQ, K), jnp.bfloat16),
            pltpu.SemaphoreType.DMA((12,)),
        ],
        compiler_params=pltpu.CompilerParams(vmem_limit_bytes=40 * 1024 * 1024),
        cost_estimate=pl.CostEstimate(
            flops=4 * K * K * K, bytes_accessed=16 * K * K, transcendentals=0
        ),
    )(where, params, *pieces, *fields)


def body(fields, centres, sides, quarters):
    shift = functools.partial(lax.ppermute, axis_name=AX)
    grp = lax.axis_index("grp")
    parity = lax.axis_index("mem") % 2
    where = jnp.stack([grp, parity]).astype(jnp.int32)

    by_col = fields[0].reshape(16, 4, 32, 2, 256)[:, :, :, ::-1, :]
    by_col = by_col.transpose(2, 3, 1, 0, 4).reshape(MEM, 4, 16, 256)
    mine = lax.all_to_all(by_col, "mem", 0, 0, tiled=True)

    small = jnp.concatenate([sides[0, 0], quarters[0, 0]], axis=-1)
    params = shift(lax.all_gather(small, "grp"), perm=flat_perm(lambda m, g: (m ^ 1, g)))

    parts = split_centres(where, centres[0, 0])
    own = [
        parts[0],
        shift(parts[1], perm=CORE),
        shift(parts[2], perm=PAL),
        shift(parts[3], perm=flat_perm(lambda m, g: (m, g ^ 3))),
    ]
    side = [shift(p, perm=SIDE) for p in own]
    cross = [shift(p, perm=CROSS) for p in own]

    near = shift(mine, perm=CORE)
    far = shift(mine, perm=PAL)
    far_near = shift(far, perm=CORE)
    result = apply_transforms(where, params, own + side + cross, [mine, near, far, far_near])

    send = result.reshape(4, 4, MEM, 4, 256).transpose(2, 0, 1, 3, 4).reshape(MEM * GRP, 16, 256)
    got = lax.all_to_all(send, AX, 0, 0, tiled=True)
    got = got.reshape(32, 2, 2, 2, 4, 4, 256)
    got = jnp.stack([got[:, 1, ::-1], got[:, 0]], axis=1)
    return got.transpose(2, 3, 5, 4, 0, 1, 6).reshape(1, 16, 4, MEM, 256)


def solution(mesh):
    return jax.shard_map(
        body,
        mesh=mesh,
        in_specs=(
            P("grp", "mem", None, None, None),
            P("grp", "mem", None, None),
            P("grp", "mem", None, None),
            P("grp", "mem", None, None),
        ),
        out_specs=P("grp", "mem", None, None, None),
        check_vma=False,
    )
```

time: 580 us -> 286 us (0.49)
  blocking collectives: 378 us -> 138 us
  local copies, waits for them, and re-layouts: 77.1 us -> 24.4 us
  other arithmetic: 27 us -> 1.44 us
  starting transfers between devices: 20.1 us -> 40 us
  Pallas kernels: 0 us -> 19.7 us
  matrix products: 8.49 us -> 0 us
    all_to_all x3 -> x2, blocking collectives: 378 us -> 131 us  [the longest x1 67.5 us: body(): got = lax.all_to_all(send, AX, 0, 0, tiled=True)]
    gather x9 -> x0, local copies, waits for them, and re-layouts: 59.1 us -> none  [body(): jnp.take(centre_table, index, axis=0).astype(jnp.float32)]
    ppermute x4 -> x15, starting transfers between devices: 14.5 us -> 40 us  [the longest x4 11.7 us: body(): cross = [shift(p, perm=CROSS) for p in own]]
    all_to_all x1 -> x0, waiting for transfers between devices: 24.8 us -> none  [body(): lax.all_to_all(lax.all_to_all(fields, 'mem', split_axis=3, concat_axis=1,...]
    pallas_call x0 -> x2, Pallas kernels: none -> 19.7 us  [the longest x1 16.2 us: apply_transforms(): pl.pallas_call(apply_kernel, grid=(4,), out_shape=jax.ShapeDtypeStruct((4...]
    ppermute x4 -> x15, waiting for transfers between devices: 43.1 us -> 62 us  [the longest x1 29.4 us: body(): far = shift(mine, perm=PAL)]
    add x1 -> x0, other arithmetic: 13.9 us -> none  [body(): blend + weight[:, None, None] * jnp.take(centre_table, index, axis=0).ast...]
    concatenate x1, other arithmetic: 10 us -> 0.01 us  [body(): small = jnp.concatenate([sides[0, 0], quarters[0, 0]], axis=-1)]
  transfers between devices with their start and end apart: 5 -> 15, of which waited for: 3 -> 7; matrix products, arithmetic and copies ran while one was open for 2% -> 0% of each run, Pallas kernels for 0% -> 1%
where the time goes in v1:
time: 286 us; the launch traced here: 285 us
  blocking collectives  138 us (48%)
  waiting for transfers between devices  62 us (22%)
  starting transfers between devices  40 us (14%)
  local copies, waits for them, and re-layouts  24.4 us (9%)
  Pallas kernels  19.7 us (7%)
    all_to_all x1, blocking collectives, body(): got = lax.all_to_all(send, AX, 0, 0, tiled=True)  67.5 us
    all_to_all x1, blocking collectives, body(): mine = lax.all_to_all(by_col, 'mem', 0, 0, tiled=True)  63.8 us
    ppermute x1, waiting for transfers between devices, body(): far = shift(mine, perm=PAL)  29.4 us
    ppermute x4, waiting for transfers between devices, body(): cross = [shift(p, perm=CROSS) for p in own]  21.3 us
    pallas_call x1, Pallas kernels, apply_transforms(): pl.pallas_call(apply_kernel, grid=(4,), out_shape=jax.ShapeDtypeStruct((4...  16.2 us
    ppermute x4, starting transfers between devices, body(): cross = [shift(p, perm=CROSS) for p in own]  11.7 us
    ppermute x1, starting transfers between devices, body(): far_near = shift(far, perm=CORE)  11.3 us
    ppermute x1, waiting for transfers between devices, body(): shift(parts[3], perm=flat_perm(lambda m, g: (m, g ^ 3)))  9.18 us
  transfers between devices with their start and end apart: 15, of which 7 were waited for; matrix products, arithmetic and copies ran while one was open for 0% of the time, Pallas kernels for 1%

profile of v1, /device:TPU:1, one launch (start us, length us, event | category | flops | bytes accessed | tf_op | source)
XLA Modules:
  0.0 285.3 jit_solution(12561869370227485321)
XLA Ops:
  0.0 2.8 copy.20
  4.2 63.8 %all_to_all.10.refs_12_ = bf16[64,4,16,256]{3,2,1,0:T(8,128)(2,1)S(1)} all-to-all(bf16[64,4,16,256]{3,2,1,0:T(8,128)(2,1)} %bitcast.19), channel_id=1, replica_groups=mesh['mem'=64,'grp'=4] {'mem'}, dimensions={0} | all-to-all | bytes 4194304 | tf_op jit(solution)/shard_map/all_to_all | solution.py:162
  70.1 3.5 %shard_map.46 = (bf16[256,1024]{1,0:T(8,128)(2,1)S(1)}, bf16[256,1024]{1,0:T(8,128)(2,1)}, bf16[256,1024]{1,0:T(8,128)(2,1)}, bf16[256,1024]{1,0:T(8,128)(2,1)S(1)}) custom-call(s32[2]{0:T(128)S(1)} %pad_add_fusion.1.where_ref, bf16[1024,1024]{1,0:T(8,128)(2,1)S(1)} %bitcast.18), custom_call_target="tpu_custom_call" | custom-call | flops 2147483648 | bytes 4194304 | tf_op jit(solution)/shard_map/pallas_call | solution.py:50
  74.4 5.2 %collective-permute-start.1 = (bf16[256,1024]{1,0:T(8,128)(2,1)}, bf16[256,1024]{1,0:T(8,128)(2,1)S(1)}, u32[]{:S(2)}, u32[]{:S(2)}) collective-permute-start(bf16[256,1024]{1,0:T(8,128)(2,1)} %get-tuple-element.10), channel_id=1, source_target_pairs={{0,1},{1,0},{2,3},{3,2},{4,5},{5,4},{6,7},{7,6},{8,9},{9,8},{10,11... | collective-permute-start | bytes 1572872 | tf_op jit(solution)/shard_map/ppermute | solution.py:170
  81.0 29.4 %collective-permute-done.13.refs_14_ = bf16[64,4,16,256]{3,2,1,0:T(8,128)(2,1)} collective-permute-done((bf16[64,4,16,256]{3,2,1,0:T(8,128)(2,1)S(1)}, bf16[64,4,16,256]{3,2,1,0:T(8,128)(2,1)}, u32[]{:S(2)}, u32[]{:S(2)}) %collective-permute-start.13) | collective-permute-done | bytes 2097184 | tf_op jit(solution)/shard_map/ppermute | solution.py:178
  110.4 11.3 %collective-permute-start.14 = (bf16[64,4,16,256]{3,2,1,0:T(8,128)(2,1)}, bf16[64,4,16,256]{3,2,1,0:T(8,128)(2,1)}, u32[]{:S(2)}, u32[]{:S(2)}) collective-permute-start(bf16[64,4,16,256]{3,2,1,0:T(8,128)(2,1)} %collective-permute-done.13.refs_14_), channel_id=1, source_target_pairs={{0,1},{1,0},{2,3},{3,2},{4,5},{5,4},{6,7},{7,6},{8,9},{9,8},{10,11... | collective-permute-start | bytes 6291464 | tf_op jit(solution)/shard_map/ppermute | solution.py:179
  121.8 6.4 %all-gather.1 = s32[4,4,4]{2,1,0:T(4,128)S(1)} all-gather(s32[1,4,4]{2,1,0:T(4,128)S(1)} %bitcast.23), channel_id=2, replica_groups=mesh['mem'=64,'grp'=4] {'grp'}, dimensions={0}, use_global_device_ids=true | all-gather | bytes 320 | tf_op jit(solution)/shard_map/all_gather | solution.py:165
  128.1 2.0 collective-permute-start
  130.2 2.0 collective-permute-done.params_ref
  133.8 1.9 collective-permute-start.8
  137.2 9.2 %collective-permute-done.3.refs_3_ = bf16[256,1024]{1,0:T(8,128)(2,1)S(1)} collective-permute-done((bf16[256,1024]{1,0:T(8,128)(2,1)}, bf16[256,1024]{1,0:T(8,128)(2,1)S(1)}, u32[]{:S(2)}, u32[]{:S(2)}) %collective-permute-start.3) | collective-permute-done | bytes 524320 | tf_op jit(solution)/shard_map/ppermute | solution.py:172
  146.4 1.9 collective-permute-start.9
  150.6 2.8 collective-permute-start.10
  153.4 6.7 %collective-permute-done.9.refs_9_ = bf16[256,1024]{1,0:T(8,128)(2,1)S(1)} collective-permute-done((bf16[256,1024]{1,0:T(8,128)(2,1)S(1)}, bf16[256,1024]{1,0:T(8,128)(2,1)S(1)}, u32[]{:S(2)}, u32[]{:S(2)}) %collective-permute-start.9) | collective-permute-done | bytes 524320 | tf_op jit(solution)/shard_map/ppermute | solution.py:175
  161.6 5.1 %collective-permute-start.11 = (bf16[256,1024]{1,0:T(8,128)(2,1)S(1)}, bf16[256,1024]{1,0:T(8,128)(2,1)S(1)}, u32[]{:S(2)}, u32[]{:S(2)}) collective-permute-start(bf16[256,1024]{1,0:T(8,128)(2,1)S(1)} %collective-permute-done.3.refs_3_), channel_id=1, source_target_pairs={{0,6},{1,7},{2,4},{3,5},{4,2},{5,3},{6,0},{7,1},{8,14},{9,15},{10,... | collective-permute-start | bytes 1572872 | tf_op jit(solution)/shard_map/ppermute | solution.py:175
  166.8 4.5 %collective-permute-done.10.refs_10_ = bf16[256,1024]{1,0:T(8,128)(2,1)S(1)} collective-permute-done((bf16[256,1024]{1,0:T(8,128)(2,1)}, bf16[256,1024]{1,0:T(8,128)(2,1)S(1)}, u32[]{:S(2)}, u32[]{:S(2)}) %collective-permute-start.10) | collective-permute-done | bytes 524320 | tf_op jit(solution)/shard_map/ppermute | solution.py:175
  172.9 9.6 %collective-permute-done.11.refs_11_ = bf16[256,1024]{1,0:T(8,128)(2,1)S(1)} collective-permute-done((bf16[256,1024]{1,0:T(8,128)(2,1)S(1)}, bf16[256,1024]{1,0:T(8,128)(2,1)S(1)}, u32[]{:S(2)}, u32[]{:S(2)}) %collective-permute-start.11) | collective-permute-done | bytes 524320 | tf_op jit(solution)/shard_map/ppermute | solution.py:175
  182.5 16.2 %shard_map.47 = bf16[4,4,256,256]{3,2,1,0:T(8,128)(2,1)S(1)} custom-call(s32[2]{0:T(128)S(1)} %pad_add_fusion.1.where_ref, s32[4,4,4]{2,1,0:T(4,128)S(1)} %collective-permute-done.params_ref, bf16[256,1024]{1,0:T(8,128)(2,1)S(1)} %get-tuple-element.9.refs_0_, bf16[256,1024]{1,0:T(8,128)(2,1)S(1)} %collective-permute-done.1.refs_1_, ...), custom_call_target="tpu_custom_call" | custom-call | flops 4294967296 | bytes 16777216 | tf_op jit(solution)/shard_map/pallas_call | solution.py:131
  200.1 2.5 reshape.16
  202.6 2.5 copy.22
  205.1 2.5 reshape.17
  207.6 67.5 %all_to_all.11 = bf16[256,16,256]{2,1,0:T(8,128)(2,1)} all-to-all(bf16[256,16,256]{2,1,0:T(8,128)(2,1)S(1)} %reshape.17), channel_id=1, replica_groups=mesh['mem'=64,'grp'=4] {'mem','grp'}, dimensions={0} | all-to-all | bytes 4194304 | tf_op jit(solution)/shard_map/all_to_all | solution.py:183
  275.1 2.5 reshape.18
  277.7 2.4 fusion
  (37 shorter events, 20.9 us)
Async XLA Ops:
  68.1 42.3 %collective-permute-start.13 = (bf16[64,4,16,256]{3,2,1,0:T(8,128)(2,1)S(1)}, bf16[64,4,16,256]{3,2,1,0:T(8,128)(2,1)}, u32[]{:S(2)}, u32[]{:S(2)}) collective-permute-start(bf16[64,4,16,256]{3,2,1,0:T(8,128)(2,1)S(1)} %all_to_all.10.refs_12_), channel_id=1, source_target_pairs={{0,2},{1,3},{2,0},{3,1},{4,6},{5,7},{6,4},{7,5},{8,10},{9,11},{10,... | collective-permute-start | bytes 6291464 | tf_op jit(solution)/shard_map/ppermute | solution.py:178
  68.6 1.6 copy-start.1
  70.1 51.5 %copy-start.4 = (s32[1,1,4,2]{2,3,1,0:T(2,128)S(1)}, s32[1,1,4,2]{2,3,1,0:T(2,128)}, u32[]{:S(2)}) copy-start(s32[1,1,4,2]{2,3,1,0:T(2,128)} %param.7) | copy-start | bytes 100
  70.1 51.5 %copy-start.5 = (s32[1,1,4,2]{2,3,1,0:T(2,128)S(1)}, s32[1,1,4,2]{2,3,1,0:T(2,128)}, u32[]{:S(2)}) copy-start(s32[1,1,4,2]{2,3,1,0:T(2,128)} %param.6) | copy-start | bytes 100
  73.6 0.8 copy-start.2
  74.4 59.4 %collective-permute-start.1 = (bf16[256,1024]{1,0:T(8,128)(2,1)}, bf16[256,1024]{1,0:T(8,128)(2,1)S(1)}, u32[]{:S(2)}, u32[]{:S(2)}) collective-permute-start(bf16[256,1024]{1,0:T(8,128)(2,1)} %get-tuple-element.10), channel_id=1, source_target_pairs={{0,1},{1,0},{2,3},{3,2},{4,5},{5,4},{6,7},{7,6},{8,9},{9,8},{10,11... | collective-permute-start | bytes 1572872 | tf_op jit(solution)/shard_map/ppermute | solution.py:170
  79.6 56.0 %collective-permute-start.2 = (bf16[256,1024]{1,0:T(8,128)(2,1)}, bf16[256,1024]{1,0:T(8,128)(2,1)}, u32[]{:S(2)}, u32[]{:S(2)}) collective-permute-start(bf16[256,1024]{1,0:T(8,128)(2,1)} %get-tuple-element.11), channel_id=1, source_target_pairs={{0,2},{1,3},{2,0},{3,1},{4,6},{5,7},{6,4},{7,5},{8,10},{9,11},{10,... | collective-permute-start | bytes 1572872 | tf_op jit(solution)/shard_map/ppermute | solution.py:171
  80.7 101.8 %collective-permute-start.12 = (bf16[64,4,16,256]{3,2,1,0:T(8,128)(2,1)S(1)}, bf16[64,4,16,256]{3,2,1,0:T(8,128)(2,1)}, u32[]{:S(2)}, u32[]{:S(2)}) collective-permute-start(bf16[64,4,16,256]{3,2,1,0:T(8,128)(2,1)S(1)} %all_to_all.10.refs_12_), channel_id=1, source_target_pairs={{0,1},{1,0},{2,3},{3,2},{4,5},{5,4},{6,7},{7,6},{8,9},{9,8},{10,11... | collective-permute-start | bytes 6291464 | tf_op jit(solution)/shard_map/ppermute | solution.py:177
  110.4 72.1 %collective-permute-start.14 = (bf16[64,4,16,256]{3,2,1,0:T(8,128)(2,1)}, bf16[64,4,16,256]{3,2,1,0:T(8,128)(2,1)}, u32[]{:S(2)}, u32[]{:S(2)}) collective-permute-start(bf16[64,4,16,256]{3,2,1,0:T(8,128)(2,1)} %collective-permute-done.13.refs_14_), channel_id=1, source_target_pairs={{0,1},{1,0},{2,3},{3,2},{4,5},{5,4},{6,7},{7,6},{8,9},{9,8},{10,11... | collective-permute-start | bytes 6291464 | tf_op jit(solution)/shard_map/ppermute | solution.py:179
  128.1 4.1 %collective-permute-start = (s32[4,4,4]{2,1,0:T(4,128)S(1)}, s32[4,4,4]{2,1,0:T(4,128)S(1)}, u32[]{:S(2)}, u32[]{:S(2)}) collective-permute-start(s32[4,4,4]{2,1,0:T(4,128)S(1)} %all-gather.1), channel_id=1, source_target_pairs={{0,4},{1,5},{2,6},{3,7},{4,0},{5,1},{6,2},{7,3},{8,12},{9,13},{10,... | collective-permute-start | bytes 776 | tf_op jit(solution)/shard_map/ppermute | solution.py:165
  132.2 14.2 %collective-permute-start.3 = (bf16[256,1024]{1,0:T(8,128)(2,1)}, bf16[256,1024]{1,0:T(8,128)(2,1)S(1)}, u32[]{:S(2)}, u32[]{:S(2)}) collective-permute-start(bf16[256,1024]{1,0:T(8,128)(2,1)} %copy-done.2), channel_id=1, source_target_pairs={{0,3},{1,2},{2,1},{3,0},{4,7},{5,6},{6,5},{7,4},{8,11},{9,10},{10,... | collective-permute-start | bytes 1572872 | tf_op jit(solution)/shard_map/ppermute | solution.py:172
  133.8 15.0 %collective-permute-start.8 = (bf16[256,1024]{1,0:T(8,128)(2,1)S(1)}, bf16[256,1024]{1,0:T(8,128)(2,1)S(1)}, u32[]{:S(2)}, u32[]{:S(2)}) collective-permute-start(bf16[256,1024]{1,0:T(8,128)(2,1)S(1)} %get-tuple-element.9.refs_0_), channel_id=1, source_target_pairs={{0,6},{1,7},{2,4},{3,5},{4,2},{5,3},{6,0},{7,1},{8,14},{9,15},{10,... | collective-permute-start | bytes 1572872 | tf_op jit(solution)/shard_map/ppermute | solution.py:175
  135.7 14.9 %collective-permute-start.4 = (bf16[256,1024]{1,0:T(8,128)(2,1)S(1)}, bf16[256,1024]{1,0:T(8,128)(2,1)S(1)}, u32[]{:S(2)}, u32[]{:S(2)}) collective-permute-start(bf16[256,1024]{1,0:T(8,128)(2,1)S(1)} %get-tuple-element.9.refs_0_), channel_id=1, source_target_pairs={{0,248},{1,249},{2,250},{3,251},{4,12},{5,13},{6,14},{7,15},{8,0},... | collective-permute-start | bytes 1572872 | tf_op jit(solution)/shard_map/ppermute | solution.py:174
  146.4 13.7 %collective-permute-start.9 = (bf16[256,1024]{1,0:T(8,128)(2,1)S(1)}, bf16[256,1024]{1,0:T(8,128)(2,1)S(1)}, u32[]{:S(2)}, u32[]{:S(2)}) collective-permute-start(bf16[256,1024]{1,0:T(8,128)(2,1)S(1)} %collective-permute-done.1.refs_1_), channel_id=1, source_target_pairs={{0,6},{1,7},{2,4},{3,5},{4,2},{5,3},{6,0},{7,1},{8,14},{9,15},{10,... | collective-permute-start | bytes 1572872 | tf_op jit(solution)/shard_map/ppermute | solution.py:175
  148.8 12.9 %collective-permute-start.5 = (bf16[256,1024]{1,0:T(8,128)(2,1)S(1)}, bf16[256,1024]{1,0:T(8,128)(2,1)S(1)}, u32[]{:S(2)}, u32[]{:S(2)}) collective-permute-start(bf16[256,1024]{1,0:T(8,128)(2,1)S(1)} %collective-permute-done.1.refs_1_), channel_id=1, source_target_pairs={{0,248},{1,249},{2,250},{3,251},{4,12},{5,13},{6,14},{7,15},{8,0},... | collective-permute-start | bytes 1572872 | tf_op jit(solution)/shard_map/ppermute | solution.py:174
  150.6 20.7 %collective-permute-start.10 = (bf16[256,1024]{1,0:T(8,128)(2,1)}, bf16[256,1024]{1,0:T(8,128)(2,1)S(1)}, u32[]{:S(2)}, u32[]{:S(2)}) collective-permute-start(bf16[256,1024]{1,0:T(8,128)(2,1)} %collective-permute-done.2.refs_2_), channel_id=1, source_target_pairs={{0,6},{1,7},{2,4},{3,5},{4,2},{5,3},{6,0},{7,1},{8,14},{9,15},{10,... | collective-permute-start | bytes 1572872 | tf_op jit(solution)/shard_map/ppermute | solution.py:175
  160.0 12.8 %collective-permute-start.6 = (bf16[256,1024]{1,0:T(8,128)(2,1)}, bf16[256,1024]{1,0:T(8,128)(2,1)S(1)}, u32[]{:S(2)}, u32[]{:S(2)}) collective-permute-start(bf16[256,1024]{1,0:T(8,128)(2,1)} %collective-permute-done.2.refs_2_), channel_id=1, source_target_pairs={{0,248},{1,249},{2,250},{3,251},{4,12},{5,13},{6,14},{7,15},{8,0},... | collective-permute-start | bytes 1572872 | tf_op jit(solution)/shard_map/ppermute | solution.py:174
  161.6 20.9 %collective-permute-start.11 = (bf16[256,1024]{1,0:T(8,128)(2,1)S(1)}, bf16[256,1024]{1,0:T(8,128)(2,1)S(1)}, u32[]{:S(2)}, u32[]{:S(2)}) collective-permute-start(bf16[256,1024]{1,0:T(8,128)(2,1)S(1)} %collective-permute-done.3.refs_3_), channel_id=1, source_target_pairs={{0,6},{1,7},{2,4},{3,5},{4,2},{5,3},{6,0},{7,1},{8,14},{9,15},{10,... | collective-permute-start | bytes 1572872 | tf_op jit(solution)/shard_map/ppermute | solution.py:175
  171.3 11.2 %collective-permute-start.7 = (bf16[256,1024]{1,0:T(8,128)(2,1)S(1)}, bf16[256,1024]{1,0:T(8,128)(2,1)S(1)}, u32[]{:S(2)}, u32[]{:S(2)}) collective-permute-start(bf16[256,1024]{1,0:T(8,128)(2,1)S(1)} %collective-permute-done.3.refs_3_), channel_id=1, source_target_pairs={{0,248},{1,249},{2,250},{3,251},{4,12},{5,13},{6,14},{7,15},{8,0},... | collective-permute-start | bytes 1572872 | tf_op jit(solution)/shard_map/ppermute | solution.py:174
  198.7 1.3 copy-start
  280.0 1.2 copy-start.3

commit v2 on v0

v2 whole, which is shorter than its diff:
```python
import functools

import jax
import jax.numpy as jnp
from jax import lax
from jax.experimental import pallas as pl
from jax.experimental.layout import Layout, with_layout_constraint
from jax.experimental.pallas import tpu as pltpu
from jax.sharding import PartitionSpec as P

AX = ("mem", "grp")
MEM = 64
GRP = 4
K = 1024
JQ = 256
JP = JQ + 16
HALF = K // 2
CUT = 192


def flat_perm(move):
    pairs = []
    for mem in range(MEM):
        for grp in range(GRP):
            to_mem, to_grp = move(mem, grp)
            pairs.append((mem * GRP + grp, (to_mem % MEM) * GRP + to_grp))
    return pairs


CORE = flat_perm(lambda m, g: (m, g ^ 1))
PAL = flat_perm(lambda m, g: (m, g ^ 2))
CROSS = flat_perm(lambda m, g: (m ^ 1, g ^ 2))
SIDE = flat_perm(lambda m, g: (m + 2 if m % 2 else m - 2, g))


FIELD_GROUPS = [
    [(c ^ 1) * GRP + 2 * (((c ^ 1) & 1) ^ flank) + core for c in range(MEM)]
    for flank in range(2)
    for core in range(2)
]
RESULT_GROUP = [
    [(c ^ 1) * GRP + (quarter ^ (2 * ((c ^ 1) & 1))) for c in range(MEM) for quarter in range(GRP)]
]
VMEM_LIMIT = 24 * 1024 * 1024
LIGHT = pl.CostEstimate(flops=1, bytes_accessed=1, transcendentals=0)


def split_kernel(where_ref, sides_ref, quarters_ref, centre_ref, keep_ref, mate_ref, far_ref):
    grp = where_ref[0]
    parity = where_ref[1]
    row = lax.broadcasted_iota(jnp.int32, (JQ, K), 0)
    col = lax.broadcasted_iota(jnp.int32, (JQ, K), 1)
    base = lax.bitwise_xor(row // 4, 1) * 16 + row % 4
    lane = lax.broadcasted_iota(jnp.int32, (16, K), 1)
    small = jnp.zeros((16, K), jnp.int32)
    for sub in range(4):
        for n in range(2):
            small = jnp.where(lane == 4 * sub + n, sides_ref[sub, n], small)
            small = jnp.where(lane == 4 * sub + 2 + n, quarters_ref[sub, n], small)
    small = small.astype(jnp.float32).astype(jnp.bfloat16)
    ordered = jnp.concatenate(
        [centre_ref[:, 1].reshape(HALF, K), centre_ref[:, 0].reshape(HALF, K)], axis=0
    )
    for rho, out in enumerate((keep_ref, mate_ref.at[0], far_ref, mate_ref.at[1])):
        quarter = lax.bitwise_xor(lax.bitwise_xor(grp, rho), 2 * parity)
        pick = jnp.where(col == base + 4 * quarter, 1.0, 0.0).astype(jnp.bfloat16)
        out[:JQ, :] = lax.dot_general(
            pick, ordered, (((1,), (1,)), ((), ())), preferred_element_type=jnp.float32
        ).astype(jnp.bfloat16)
        out[JQ:, :] = small


def split_centres(where, sides, quarters, centre):
    smem = pl.BlockSpec(memory_space=pltpu.SMEM)
    vmem = pl.BlockSpec(memory_space=pltpu.VMEM)
    one = jax.ShapeDtypeStruct((JP, K), jnp.bfloat16)
    two = jax.ShapeDtypeStruct((2, JP, K), jnp.bfloat16)
    return pl.pallas_call(
        split_kernel,
        out_shape=[one, two, one],
        in_specs=[smem, smem, smem, vmem],
        out_specs=[vmem] * 3,
        compiler_params=pltpu.CompilerParams(vmem_limit_bytes=VMEM_LIMIT),
        cost_estimate=LIGHT,
    )(where, sides, quarters, centre.reshape(32, 2, 16, K))


def blend_kernel(first, count, where_ref, params_ref, own01, own23, cross01, cross23, side, out_ref, table, sems):
    grp = where_ref[0]
    parity = where_ref[1]
    at = pl.ds(first, count)
    copies = [
        pltpu.make_async_copy(own01.at[:, at], table.at[0:2], sems.at[0]),
        pltpu.make_async_copy(own23.at[:, at], table.at[2:4], sems.at[1]),
        pltpu.make_async_copy(side, table.at[4:8], sems.at[2]),
        pltpu.make_async_copy(cross01.at[:, at], table.at[8:10], sems.at[3]),
        pltpu.make_async_copy(cross23.at[:, at], table.at[10:12], sems.at[4]),
    ]
    for copy in copies:
        copy.start()
    for copy in copies:
        copy.wait()

    @pl.loop(0, 4)
    def _(row):
        i_own = lax.bitwise_xor(lax.bitwise_xor(row, grp), 2)
        for sub in range(4):
            side_row = params_ref[i_own, 4 * sub]
            side_col = params_ref[i_own, 4 * sub + 1]
            a = params_ref[i_own, 4 * sub + 2].astype(jnp.float32) * 0.25
            b = params_ref[i_own, 4 * sub + 3].astype(jnp.float32) * 0.25
            row2 = lax.bitwise_and(row + 2 * side_row - 1, 3)
            base2 = jnp.where(side_col == parity, 0, 4)
            i_row = lax.bitwise_xor(lax.bitwise_xor(row2, grp), 2)
            i_col = base2 + lax.bitwise_xor(row, grp)
            i_diag = base2 + lax.bitwise_xor(row2, grp)
            w_own = (1.0 - a) * (1.0 - b)
            w_row = a * (1.0 - b)
            w_col = (1.0 - a) * b
            w_diag = a * b

            @pl.loop(0, count // 32)
            def _(step):
                at = pl.ds(pl.multiple_of(step * 32, 32), 32)
                mixed = w_own * table[8 + i_own, at, :].astype(jnp.float32)
                mixed = mixed + w_row * table[8 + i_row, at, :].astype(jnp.float32)
                mixed = mixed + w_col * table[i_col, at, :].astype(jnp.float32)
                mixed = mixed + w_diag * table[i_diag, at, :].astype(jnp.float32)
                out_ref[4 * row + sub, at, :] = mixed.astype(jnp.bfloat16)


def blend_centres(where, params, own01, own23, cross01, cross23, side, first, count):
    smem = pl.BlockSpec(memory_space=pltpu.SMEM)
    return pl.pallas_call(
        functools.partial(blend_kernel, first, count),
        out_shape=jax.ShapeDtypeStruct((16, count, K), jnp.bfloat16),
        in_specs=[smem, smem] + [pl.BlockSpec(memory_space=pltpu.HBM)] * 5,
        out_specs=pl.BlockSpec(memory_space=pltpu.VMEM),
        scratch_shapes=[
            pltpu.VMEM((12, count, K), jnp.bfloat16),
            pltpu.SemaphoreType.DMA((5,)),
        ],
        compiler_params=pltpu.CompilerParams(vmem_limit_bytes=VMEM_LIMIT),
        cost_estimate=LIGHT,
    )(where, params, own01, own23, cross01, cross23, side)


def sub_block(product, cols, rows):
    lane = lax.broadcasted_iota(jnp.int32, (rows, 128), 1)
    return jnp.where(lane < 64, product[:rows, cols], product[rows:, cols])


def side_by_side(refs, half, row, at):
    return jnp.concatenate(
        [ref[:, half, pl.ds(row, 1), :, at].reshape(HALF, 128) for ref in refs], axis=1
    )


def here_kernel(blend_ref, mine, near, out_ref):
    @pl.loop(0, 4)
    def _(row):
        for pair in range(2):
            at = slice(pair * 128, pair * 128 + 128)
            for two in range(2):
                half = 1 - two
                left = blend_ref[pl.ds(4 * row + 2 * pair, 2), :, half * HALF : half * HALF + HALF]
                product = jnp.dot(
                    left.reshape(2 * CUT, HALF),
                    side_by_side((mine, near), half, row, at),
                    preferred_element_type=jnp.float32,
                )
                for n in range(2):
                    out_ref[2 * pair + two, n, row] = sub_block(
                        product, slice(n * 128, n * 128 + 128), CUT
                    )


def apply_here(blend, mine, near):
    vmem = pl.BlockSpec(memory_space=pltpu.VMEM)
    return pl.pallas_call(
        here_kernel,
        out_shape=jax.ShapeDtypeStruct((4, 2, 4, CUT, 128), jnp.float32),
        in_specs=[vmem] * 3,
        out_specs=vmem,
        compiler_params=pltpu.CompilerParams(vmem_limit_bytes=VMEM_LIMIT),
        cost_estimate=LIGHT,
    )(blend, mine.reshape(32, 2, 4, 16, 256), near.reshape(32, 2, 4, 16, 256))


def apply_kernel(where_ref, blend_a, blend_b, part, mine, near, far, far_near, out_ref, total):
    quarter = where_ref[2]

    @pl.loop(0, 4)
    def _(row):
        for pair in range(2):
            at = slice(pair * 128, pair * 128 + 128)
            subs = pl.ds(4 * row + 2 * pair, 2)
            for two in range(2):
                there = side_by_side((far, far_near), two, row, at)
                here = side_by_side((mine, near), 1 - two, row, at)
                both = (there, here) if two == 0 else (here, there)
                top = jnp.dot(
                    blend_a[subs, :, two * HALF : two * HALF + HALF].reshape(2 * CUT, HALF),
                    there,
                    preferred_element_type=jnp.float32,
                )
                rest = jnp.dot(
                    blend_b[subs].reshape(2 * (JQ - CUT), K),
                    jnp.concatenate(both, axis=0),
                    preferred_element_type=jnp.float32,
                )
                for n in range(2):
                    cols = slice(n * 128, n * 128 + 128)
                    to = (pair, 2 * two + n)
                    total[(*to, pl.ds(row, CUT, stride=4), slice(None))] = (
                        sub_block(top, cols, CUT) + part[2 * pair + two, n, row]
                    )
                    total[(*to, pl.ds(row + 4 * CUT, JQ - CUT, stride=4), slice(None))] = (
                        sub_block(rest, cols, JQ - CUT)
                    )

    for rho in range(4):
        level = lax.bitwise_xor(quarter, rho)
        for pair in range(2):
            at = slice(pair * 128, pair * 128 + 128)
            done = total[pair, rho].reshape(32, 2, 16, 128).astype(jnp.bfloat16)
            out_ref[:, 0, lax.bitwise_xor(level, 2), :, at] = done[:, 0]
            out_ref[:, 1, level, :, at] = done[:, 1]


def apply_transforms(where, blend_a, blend_b, part, fields):
    vmem = pl.BlockSpec(memory_space=pltpu.VMEM)
    return pl.pallas_call(
        apply_kernel,
        out_shape=jax.ShapeDtypeStruct((32, 2, 4, 16, 256), jnp.bfloat16),
        in_specs=[pl.BlockSpec(memory_space=pltpu.SMEM)] + [vmem] * 7,
        out_specs=vmem,
        scratch_shapes=[pltpu.VMEM((2, 4, 4 * JQ, 128), jnp.float32)],
        compiler_params=pltpu.CompilerParams(vmem_limit_bytes=VMEM_LIMIT),
        cost_estimate=LIGHT,
    )(where, blend_a, blend_b, part, *(f.reshape(32, 2, 4, 16, 256) for f in fields))


def body(fields, centres, sides, quarters):
    shift = functools.partial(lax.ppermute, axis_name=AX)
    grp = lax.axis_index("grp")
    parity = lax.bitwise_and(lax.axis_index("mem"), 1)
    where = jnp.stack([grp, parity, lax.bitwise_xor(grp, 2 * parity)]).astype(jnp.int32)

    by_col = with_layout_constraint(
        fields[0].transpose(2, 1, 0, 3), Layout(major_to_minor=(0, 1, 2, 3))
    )
    mine = lax.all_to_all(by_col, AX, 0, 0, axis_index_groups=FIELD_GROUPS, tiled=True)

    keep, to_mate, to_far = split_centres(where, sides[0, 0], quarters[0, 0], centres[0, 0])
    mate = shift(to_mate, perm=CORE)
    own23 = shift(jnp.stack([to_far, mate[1]]), perm=PAL)
    own01 = jnp.stack([keep, mate[0]])
    cross01 = shift(own01, perm=CROSS)
    own_a = jnp.concatenate([own01[:, :CUT], own23[:, :CUT]])
    own_b = jnp.concatenate([own01[:, CUT:JQ], own23[:, CUT:JQ]])
    mine, own01, own23, own_a, own_b, cross01 = lax.optimization_barrier(
        (mine, own01, own23, own_a, own_b, cross01)
    )

    far = shift(mine, perm=PAL)
    side_a = shift(own_a, perm=SIDE)
    cross23 = shift(own23, perm=CROSS)
    side_b = shift(own_b, perm=SIDE)
    near = shift(mine, perm=CORE)
    params = jnp.concatenate([cross01[:, JQ, :16], cross23[:, JQ, :16]]).astype(jnp.int32)
    four = (own01, own23, cross01, cross23)
    blend_a = blend_centres(where, params, *four, side_a, 0, CUT)
    part = apply_here(blend_a, mine, near)
    far, part, side_b = lax.optimization_barrier((far, part, side_b))
    far_near = shift(far, perm=CORE)
    blend_b = blend_centres(where, params, *four, side_b, CUT, JQ - CUT)
    result = apply_transforms(where, blend_a, blend_b, part, (mine, near, far, far_near))

    got = lax.all_to_all(
        result.reshape(MEM * GRP, 16, 256), AX, 0, 0, axis_index_groups=RESULT_GROUP, tiled=True
    )
    return got.reshape(MEM, 64, 256).transpose(1, 0, 2).reshape(1, 16, 4, MEM, 256)


def solution(mesh):
    return jax.shard_map(
        body,
        mesh=mesh,
        in_specs=(
            P("grp", "mem", None, None, None),
            P("grp", "mem", None, None),
            P("grp", "mem", None, None),
            P("grp", "mem", None, None),
        ),
        out_specs=P("grp", "mem", None, None, None),
        check_vma=False,
    )
```

time: 580 us -> 199 us (0.34)
  blocking collectives: 378 us -> 64.9 us
  local copies, waits for them, and re-layouts: 77.1 us -> 11.4 us
  other arithmetic: 27 us -> 2.53 us
  Pallas kernels: 0 us -> 20.8 us
  matrix products: 8.49 us -> 0 us
  starting transfers between devices: 20.1 us -> 26.2 us
    all_to_all x3 -> x1, blocking collectives: 378 us -> 64.9 us  [body(): lax.all_to_all(result.reshape(MEM * GRP, 16, 256), AX, 0, 0, axis_index_g...]
    gather x9 -> x0, local copies, waits for them, and re-layouts: 59.1 us -> none  [body(): jnp.take(centre_table, index, axis=0).astype(jnp.float32)]
    ppermute x4 -> x9, waiting for transfers between devices: 43.1 us -> 72.5 us  [the longest x1 24.9 us: body(): own23 = shift(jnp.stack([to_far, mate[1]]), perm=PAL)]
    all_to_all x1, waiting for transfers between devices: 24.8 us -> 0.01 us  [body(): lax.all_to_all(by_col, AX, 0, 0, axis_index_groups=FIELD_GROUPS, tiled=True)]
    pallas_call x0 -> x5, Pallas kernels: none -> 20.8 us  [the longest x2 10.8 us: blend_centres(): pl.pallas_call(functools.partial(blend_kernel, first, count), out_shape=j...]
    add x1 -> x0, other arithmetic: 13.9 us -> none  [body(): blend + weight[:, None, None] * jnp.take(centre_table, index, axis=0).ast...]
    all_to_all x1, starting transfers between devices: 5.62 us -> 14.9 us  [body(): lax.all_to_all(by_col, AX, 0, 0, axis_index_groups=FIELD_GROUPS, tiled=True)]
    unnamed x2 -> x0, matrix products: 8.49 us -> none
  transfers between devices with their start and end apart: 5 -> 10, of which waited for: 3 -> 7; matrix products, arithmetic and copies ran while one was open for 2% -> 2% of each run, Pallas kernels for 0% -> 8%
where the time goes in v2:
time: 199 us
  waiting for transfers between devices  72.5 us (36%)
  blocking collectives  64.9 us (33%)
  starting transfers between devices  26.2 us (13%)
  Pallas kernels  20.8 us (10%)
  local copies, waits for them, and re-layouts  11.4 us (6%)
  other arithmetic  2.53 us (1%)
    all_to_all x1, blocking collectives, body(): lax.all_to_all(result.reshape(MEM * GRP, 16, 256), AX, 0, 0, axis_index_g...  64.9 us
    ppermute x1, waiting for transfers between devices, body(): own23 = shift(jnp.stack([to_far, mate[1]]), perm=PAL)  24.9 us
    ppermute x1, waiting for transfers between devices, body(): cross23 = shift(own23, perm=CROSS)  23.9 us
    all_to_all x1, starting transfers between devices, body(): lax.all_to_all(by_col, AX, 0, 0, axis_index_groups=FIELD_GROUPS, tiled=True)  14.9 us
    ppermute x1, waiting for transfers between devices, body(): cross01 = shift(own01, perm=CROSS)  13.9 us
    pallas_call x2, Pallas kernels, blend_centres(): pl.pallas_call(functools.partial(blend_kernel, first, count), out_shape=j...  10.8 us
    unnamed x15, local copies, waits for them, and re-layouts  7.92 us
    ppermute x1, waiting for transfers between devices, body(): side_a = shift(own_a, perm=SIDE)  6.81 us
  transfers between devices with their start and end apart: 10, of which 7 were waited for; matrix products, arithmetic and copies ran while one was open for 2% of the time, Pallas kernels for 8%

profile of v2, /device:TPU:1, one launch (start us, length us, event | category | flops | bytes accessed | tf_op | source)
XLA Modules:
  0.0 198.5 jit_solution(16746607292638434304)
XLA Ops:
  0.0 4.1 %copy.18 = bf16[1,16,4,64,256]{4,1,2,3,0:T(8,128)(2,1)} copy(bf16[1,16,4,64,256]{4,3,2,1,0:T(8,128)(2,1)} %param.4) | data formatting | bytes 4194304 | tf_op args[0]
  4.1 14.9 %all-to-all-start = ((bf16[64,4,16,256]{3,2,1,0:T(8,128)(2,1)}), bf16[64,4,16,256]{3,2,1,0:T(8,128)(2,1)S(1)}, u32[]{:S(2)}, u32[]{:S(2)}) async-start(bf16[64,4,16,256]{3,2,1,0:T(8,128)(2,1)} %bitcast.40), calls=%async_computation | async-start | bytes 4194304 | tf_op jit(solution)/shard_map/all_to_all | solution.py:253
  19.3 1.6 copy-done.3
  20.9 3.0 %shard_map.46 = (bf16[272,1024]{1,0:T(8,128)(2,1)S(1)}, bf16[2,272,1024]{2,1,0:T(8,128)(2,1)S(1)}, bf16[272,1024]{1,0:T(8,128)(2,1)S(1)}) custom-call(s32[3]{0:T(128)S(1)} %pad_add_fusion.where_ref, s32[4,2]{1,0:T(4,128)S(1)} %copy.10.sides_ref, s32[4,2]{1,0:T(4,128)S(1)} %copy.11.quarters_ref, bf16[32,2,16,1024]{3,2,1,0:T(8,128)(2,1)S(1)} %bitcast.38), custom_call_target="tpu_custom_call" | custom-call | flops 1 | bytes 1 | tf_op jit(solution)/shard_map/pallas_call | solution.py:78
  23.8 1.3 collective-permute-start
  25.2 2.4 %collective-permute-done = bf16[2,272,1024]{2,1,0:T(8,128)(2,1)S(1)} collective-permute-done((bf16[2,272,1024]{2,1,0:T(8,128)(2,1)S(1)}, bf16[2,272,1024]{2,1,0:T(8,128)(2,1)S(1)}, u32[]{:S(2)}, u32[]{:S(2)}) %collective-permute-start) | collective-permute-done | bytes 1114144 | tf_op jit(solution)/shard_map/ppermute | solution.py:256
  28.8 24.9 %collective-permute-done.1.own23 = bf16[2,272,1024]{2,1,0:T(8,128)(2,1)S(1)} collective-permute-done((bf16[2,272,1024]{2,1,0:T(8,128)(2,1)S(1)}, bf16[2,272,1024]{2,1,0:T(8,128)(2,1)S(1)}, u32[]{:S(2)}, u32[]{:S(2)}) %collective-permute-start.1) | collective-permute-done | bytes 1114144 | tf_op jit(solution)/shard_map/ppermute | solution.py:257
  53.7 1.0 copy-done
  54.8 0.8 pad_maximum_fusion.3
  55.6 1.3 pad_maximum_fusion
  56.9 13.9 %collective-permute-done.2.cross01 = bf16[2,272,1024]{2,1,0:T(8,128)(2,1)} collective-permute-done((bf16[2,272,1024]{2,1,0:T(8,128)(2,1)S(1)}, bf16[2,272,1024]{2,1,0:T(8,128)(2,1)}, u32[]{:S(2)}, u32[]{:S(2)}) %collective-permute-start.2) | collective-permute-done | bytes 1114144 | tf_op jit(solution)/shard_map/ppermute | solution.py:259
  70.8 1.2 collective-permute-start.6
  72.1 3.7 %collective-permute-start.4 = (bf16[4,192,1024]{2,1,0:T(8,128)(2,1)}, bf16[4,192,1024]{2,1,0:T(8,128)(2,1)S(1)}, u32[]{:S(2)}, u32[]{:S(2)}) collective-permute-start(bf16[4,192,1024]{2,1,0:T(8,128)(2,1)} %pad_maximum_fusion), channel_id=1, source_target_pairs={{0,248},{1,249},{2,250},{3,251},{4,12},{5,13},{6,14},{7,15},{8,0},... | collective-permute-start | bytes 4718600 | tf_op jit(solution)/shard_map/ppermute | solution.py:267
  75.7 2.4 %collective-permute-start.7 = (bf16[4,64,1024]{2,1,0:T(8,128)(2,1)}, bf16[4,64,1024]{2,1,0:T(8,128)(2,1)S(1)}, u32[]{:S(2)}, u32[]{:S(2)}) collective-permute-start(bf16[4,64,1024]{2,1,0:T(8,128)(2,1)} %pad_maximum_fusion.3), channel_id=1, source_target_pairs={{0,248},{1,249},{2,250},{3,251},{4,12},{5,13},{6,14},{7,15},{8,0},... | collective-permute-start | bytes 1572872 | tf_op jit(solution)/shard_map/ppermute | solution.py:269
  78.8 23.9 %collective-permute-done.3.cross23 = bf16[2,272,1024]{2,1,0:T(8,128)(2,1)S(1)} collective-permute-done((bf16[2,272,1024]{2,1,0:T(8,128)(2,1)}, bf16[2,272,1024]{2,1,0:T(8,128)(2,1)S(1)}, u32[]{:S(2)}, u32[]{:S(2)}) %collective-permute-start.3) | collective-permute-done | bytes 1114144 | tf_op jit(solution)/shard_map/ppermute | solution.py:268
  102.8 6.8 %collective-permute-done.4.side = bf16[4,192,1024]{2,1,0:T(8,128)(2,1)S(1)} collective-permute-done((bf16[4,192,1024]{2,1,0:T(8,128)(2,1)}, bf16[4,192,1024]{2,1,0:T(8,128)(2,1)S(1)}, u32[]{:S(2)}, u32[]{:S(2)}) %collective-permute-start.4) | collective-permute-done | bytes 1572896 | tf_op jit(solution)/shard_map/ppermute | solution.py:267
  109.6 1.2 copy-done.1
  110.8 7.3 %shard_map.47.blend_ref.blend_a = bf16[16,192,1024]{2,1,0:T(8,128)(2,1)S(1)} custom-call(s32[3]{0:T(128)S(1)} %pad_add_fusion.where_ref, s32[4,16]{1,0:T(4,128)S(1)} %maximum_convert_fusion.params_ref, bf16[2,272,1024]{2,1,0:T(8,128)(2,1)S(1)} %pad_maximum_fusion.1.own01, bf16[2,272,1024]{2,1,0:T(8,128)(2,1)S(1)} %copy-done.1, ...), custom_call_target="tpu_custom_call" | custom-call | flops 1 | bytes 1 | tf_op jit(solution)/shard_map/pallas_call | solution.py:134
  118.2 2.4 %shard_map.48.part = f32[4,2,4,192,128]{4,3,2,1,0:T(8,128)S(1)} custom-call(bf16[16,192,1024]{2,1,0:T(8,128)(2,1)S(1)} %shard_map.47.blend_ref.blend_a, bf16[32,2,4,16,256]{4,3,2,1,0:T(8,128)(2,1)S(1)} %bitcast.28, bf16[32,2,4,16,256]{4,3,2,1,0:T(8,128)(2,1)S(1)} %bitcast.31), custom_call_target="tpu_custom_call" | custom-call | flops 1 | bytes 1 | tf_op jit(solution)/shard_map/pallas_call | solution.py:180
  120.8 1.8 collective-permute-start.8
  122.6 3.5 %shard_map.49.blend_b = bf16[16,64,1024]{2,1,0:T(8,128)(2,1)S(1)} custom-call(s32[3]{0:T(128)S(1)} %pad_add_fusion.where_ref, s32[4,16]{1,0:T(4,128)S(1)} %maximum_convert_fusion.params_ref, bf16[2,272,1024]{2,1,0:T(8,128)(2,1)S(1)} %pad_maximum_fusion.1.own01, bf16[2,272,1024]{2,1,0:T(8,128)(2,1)S(1)} %copy-done.2, ...), custom_call_target="tpu_custom_call" | custom-call | flops 1 | bytes 1 | tf_op jit(solution)/shard_map/pallas_call | solution.py:134
  126.4 4.6 %shard_map.50 = bf16[32,2,4,16,256]{4,3,2,1,0:T(8,128)(2,1)S(1)} custom-call(s32[3]{0:T(128)S(1)} %pad_add_fusion.where_ref, bf16[16,192,1024]{2,1,0:T(8,128)(2,1)S(1)} %shard_map.47.blend_ref.blend_a, bf16[16,64,1024]{2,1,0:T(8,128)(2,1)S(1)} %shard_map.49.blend_b, f32[4,2,4,192,128]{4,3,2,1,0:T(8,128)S(1)} %shard_map.48.part, ...), custom_call_target="tpu_custom_call" | custom-call | flops 1 | bytes 1 | tf_op jit(solution)/shard_map/pallas_call | solution.py:233
  131.1 64.9 %all_to_all.10 = bf16[256,16,256]{2,1,0:T(8,128)(2,1)S(1)} all-to-all(bf16[256,16,256]{2,1,0:T(8,128)(2,1)S(1)} %bitcast.30), channel_id=1, replica_groups={{6,7,4,5,0,1,2,3,14,15,12,13,8,9,10,11,22,23,20,21,16,17,18,19,30,31,28..., dimensions={0} | all-to-all | bytes 4194304 | tf_op jit(solution)/shard_map/all_to_all | solution.py:280
  196.0 2.5 %copy.12 = bf16[64,64,256]{2,0,1:T(8,128)(2,1)} copy(bf16[64,64,256]{2,1,0:T(8,128)(2,1)S(1)} %bitcast.41) | data formatting | bytes 4194304 | tf_op jit(solution)/shard_map/reshape | solution.py:283
  (33 shorter events, 2.9 us)
Async XLA Ops:
  4.1 14.9 %copy-start.4 = (s32[1,1,4,2]{2,3,1,0:T(2,128)S(1)}, s32[1,1,4,2]{2,3,1,0:T(2,128)}, u32[]{:S(2)}) copy-start(s32[1,1,4,2]{2,3,1,0:T(2,128)} %param.6) | copy-start | bytes 100
  4.1 15.0 %copy-start.5 = (s32[1,1,4,2]{2,3,1,0:T(2,128)S(1)}, s32[1,1,4,2]{2,3,1,0:T(2,128)}, u32[]{:S(2)}) copy-start(s32[1,1,4,2]{2,3,1,0:T(2,128)} %param.7) | copy-start | bytes 100
  4.1 66.7 %all-to-all-start = ((bf16[64,4,16,256]{3,2,1,0:T(8,128)(2,1)}), bf16[64,4,16,256]{3,2,1,0:T(8,128)(2,1)S(1)}, u32[]{:S(2)}, u32[]{:S(2)}) async-start(bf16[64,4,16,256]{3,2,1,0:T(8,128)(2,1)} %bitcast.40), calls=%async_computation | async-start | bytes 4194304 | tf_op jit(solution)/shard_map/all_to_all | solution.py:253
  19.3 1.6 copy-start.3
  23.8 3.7 %collective-permute-start = (bf16[2,272,1024]{2,1,0:T(8,128)(2,1)S(1)}, bf16[2,272,1024]{2,1,0:T(8,128)(2,1)S(1)}, u32[]{:S(2)}, u32[]{:S(2)}) collective-permute-start(bf16[2,272,1024]{2,1,0:T(8,128)(2,1)S(1)} %get-tuple-element.18), channel_id=1, source_target_pairs={{0,1},{1,0},{2,3},{3,2},{4,5},{5,4},{6,7},{7,6},{8,9},{9,8},{10,11... | collective-permute-start | bytes 3342344 | tf_op jit(solution)/shard_map/ppermute | solution.py:256
  27.7 26.0 %collective-permute-start.1 = (bf16[2,272,1024]{2,1,0:T(8,128)(2,1)S(1)}, bf16[2,272,1024]{2,1,0:T(8,128)(2,1)S(1)}, u32[]{:S(2)}, u32[]{:S(2)}) collective-permute-start(bf16[2,272,1024]{2,1,0:T(8,128)(2,1)S(1)} %pad_maximum_fusion.2), channel_id=1, source_target_pairs={{0,2},{1,3},{2,0},{3,1},{4,6},{5,7},{6,4},{7,5},{8,10},{9,11},{10,... | collective-permute-start | bytes 3342344 | tf_op jit(solution)/shard_map/ppermute | solution.py:257
  28.0 42.8 %collective-permute-start.2 = (bf16[2,272,1024]{2,1,0:T(8,128)(2,1)S(1)}, bf16[2,272,1024]{2,1,0:T(8,128)(2,1)}, u32[]{:S(2)}, u32[]{:S(2)}) collective-permute-start(bf16[2,272,1024]{2,1,0:T(8,128)(2,1)S(1)} %pad_maximum_fusion.1.own01), channel_id=1, source_target_pairs={{0,6},{1,7},{2,4},{3,5},{4,2},{5,3},{6,0},{7,1},{8,14},{9,15},{10,... | collective-permute-start | bytes 3342344 | tf_op jit(solution)/shard_map/ppermute | solution.py:259
  53.7 1.0 copy-start
  70.8 47.4 %collective-permute-start.6 = (bf16[64,4,16,256]{3,2,1,0:T(8,128)(2,1)S(1)}, bf16[64,4,16,256]{3,2,1,0:T(8,128)(2,1)S(1)}, u32[]{:S(2)}, u32[]{:S(2)}) collective-permute-start(bf16[64,4,16,256]{3,2,1,0:T(8,128)(2,1)S(1)} %all-to-all-done), channel_id=1, source_target_pairs={{0,1},{1,0},{2,3},{3,2},{4,5},{5,4},{6,7},{7,6},{8,9},{9,8},{10,11... | collective-permute-start | bytes 6291464 | tf_op jit(solution)/shard_map/ppermute | solution.py:270
  72.0 48.9 %collective-permute-start.5 = (bf16[64,4,16,256]{3,2,1,0:T(8,128)(2,1)S(1)}, bf16[64,4,16,256]{3,2,1,0:T(8,128)(2,1)S(1)}, u32[]{:S(2)}, u32[]{:S(2)}) collective-permute-start(bf16[64,4,16,256]{3,2,1,0:T(8,128)(2,1)S(1)} %all-to-all-done), channel_id=1, source_target_pairs={{0,2},{1,3},{2,0},{3,1},{4,6},{5,7},{6,4},{7,5},{8,10},{9,11},{10,... | collective-permute-start | bytes 6291464 | tf_op jit(solution)/shard_map/ppermute | solution.py:266
  72.1 37.5 %collective-permute-start.4 = (bf16[4,192,1024]{2,1,0:T(8,128)(2,1)}, bf16[4,192,1024]{2,1,0:T(8,128)(2,1)S(1)}, u32[]{:S(2)}, u32[]{:S(2)}) collective-permute-start(bf16[4,192,1024]{2,1,0:T(8,128)(2,1)} %pad_maximum_fusion), channel_id=1, source_target_pairs={{0,248},{1,249},{2,250},{3,251},{4,12},{5,13},{6,14},{7,15},{8,0},... | collective-permute-start | bytes 4718600 | tf_op jit(solution)/shard_map/ppermute | solution.py:267
  75.7 27.0 %collective-permute-start.3 = (bf16[2,272,1024]{2,1,0:T(8,128)(2,1)}, bf16[2,272,1024]{2,1,0:T(8,128)(2,1)S(1)}, u32[]{:S(2)}, u32[]{:S(2)}) collective-permute-start(bf16[2,272,1024]{2,1,0:T(8,128)(2,1)} %copy-done), channel_id=1, source_target_pairs={{0,6},{1,7},{2,4},{3,5},{4,2},{5,3},{6,0},{7,1},{8,14},{9,15},{10,... | collective-permute-start | bytes 3342344 | tf_op jit(solution)/shard_map/ppermute | solution.py:268
  75.7 45.1 %collective-permute-start.7 = (bf16[4,64,1024]{2,1,0:T(8,128)(2,1)}, bf16[4,64,1024]{2,1,0:T(8,128)(2,1)S(1)}, u32[]{:S(2)}, u32[]{:S(2)}) collective-permute-start(bf16[4,64,1024]{2,1,0:T(8,128)(2,1)} %pad_maximum_fusion.3), channel_id=1, source_target_pairs={{0,248},{1,249},{2,250},{3,251},{4,12},{5,13},{6,14},{7,15},{8,0},... | collective-permute-start | bytes 1572872 | tf_op jit(solution)/shard_map/ppermute | solution.py:269
  109.6 1.2 copy-start.1
  118.2 4.5 %copy-start.2 = (bf16[2,272,1024]{2,1,0:T(8,128)(2,1)S(1)}, bf16[2,272,1024]{2,1,0:T(8,128)(2,1)}, u32[]{:S(2)}) copy-start(bf16[2,272,1024]{2,1,0:T(8,128)(2,1)} %copy-done) | copy-start | bytes 3342340
  120.8 5.6 %collective-permute-start.8 = (bf16[64,4,16,256]{3,2,1,0:T(8,128)(2,1)S(1)}, bf16[64,4,16,256]{3,2,1,0:T(8,128)(2,1)S(1)}, u32[]{:S(2)}, u32[]{:S(2)}) collective-permute-start(bf16[64,4,16,256]{3,2,1,0:T(8,128)(2,1)S(1)} %collective-permute-done.5), channel_id=1, source_target_pairs={{0,1},{1,0},{2,3},{3,2},{4,5},{5,4},{6,7},{7,6},{8,9},{9,8},{10,11... | collective-permute-start | bytes 6291464 | tf_op jit(solution)/shard_map/ppermute | solution.py:276

commit v3 on v2

--- a/solution.py
+++ b/solution.py
@@ -15,7 +15,7 @@
 JQ = 256
 JP = JQ + 16
 HALF = K // 2
-CUT = 192
+CUT = 176
 
 
 def flat_perm(move):
@@ -85,17 +85,17 @@
     )(where, sides, quarters, centre.reshape(32, 2, 16, K))
 
 
-def blend_kernel(first, count, where_ref, params_ref, own01, own23, cross01, cross23, side, out_ref, table, sems):
+def blend_kernel(first, count, where_ref, params_ref, own, side, cross0, cross123, out_ref, table, sems):
     grp = where_ref[0]
     parity = where_ref[1]
     at = pl.ds(first, count)
-    copies = [
-        pltpu.make_async_copy(own01.at[:, at], table.at[0:2], sems.at[0]),
-        pltpu.make_async_copy(own23.at[:, at], table.at[2:4], sems.at[1]),
-        pltpu.make_async_copy(side, table.at[4:8], sems.at[2]),
-        pltpu.make_async_copy(cross01.at[:, at], table.at[8:10], sems.at[3]),
-        pltpu.make_async_copy(cross23.at[:, at], table.at[10:12], sems.at[4]),
-    ]
+    ends = (
+        (own, table.at[0:4]),
+        (side, table.at[4:8]),
+        (cross0.at[at], table.at[8]),
+        (cross123.at[:, at], table.at[9:12]),
+    )
+    copies = [pltpu.make_async_copy(a, b, sems.at[n]) for n, (a, b) in enumerate(ends)]
     for copy in copies:
         copy.start()
     for copy in copies:
@@ -104,6 +104,7 @@
     @pl.loop(0, 4)
     def _(row):
         i_own = lax.bitwise_xor(lax.bitwise_xor(row, grp), 2)
+        plans = []
         for sub in range(4):
             side_row = params_ref[i_own, 4 * sub]
             side_col = params_ref[i_own, 4 * sub + 1]
@@ -111,38 +112,37 @@
             b = params_ref[i_own, 4 * sub + 3].astype(jnp.float32) * 0.25
             row2 = lax.bitwise_and(row + 2 * side_row - 1, 3)
             base2 = jnp.where(side_col == parity, 0, 4)
-            i_row = lax.bitwise_xor(lax.bitwise_xor(row2, grp), 2)
+            i_row = 8 + lax.bitwise_xor(lax.bitwise_xor(row2, grp), 2)
             i_col = base2 + lax.bitwise_xor(row, grp)
             i_diag = base2 + lax.bitwise_xor(row2, grp)
-            w_own = (1.0 - a) * (1.0 - b)
-            w_row = a * (1.0 - b)
-            w_col = (1.0 - a) * b
-            w_diag = a * b
-
-            @pl.loop(0, count // 32)
-            def _(step):
-                at = pl.ds(pl.multiple_of(step * 32, 32), 32)
-                mixed = w_own * table[8 + i_own, at, :].astype(jnp.float32)
-                mixed = mixed + w_row * table[8 + i_row, at, :].astype(jnp.float32)
-                mixed = mixed + w_col * table[i_col, at, :].astype(jnp.float32)
-                mixed = mixed + w_diag * table[i_diag, at, :].astype(jnp.float32)
+            terms = ((a * (1.0 - b), i_row), ((1.0 - a) * b, i_col), (a * b, i_diag))
+            plans.append(((1.0 - a) * (1.0 - b), terms))
+
+        @pl.loop(0, count // 16)
+        def _(step):
+            at = pl.ds(pl.multiple_of(step * 16, 16), 16)
+            own_part = table[8 + i_own, at, :].astype(jnp.float32)
+            for sub, (weight, terms) in enumerate(plans):
+                mixed = weight * own_part
+                for share, index in terms:
+                    mixed = mixed + share * table[index, at, :].astype(jnp.float32)
                 out_ref[4 * row + sub, at, :] = mixed.astype(jnp.bfloat16)
 
 
-def blend_centres(where, params, own01, own23, cross01, cross23, side, first, count):
+def blend_centres(where, params, own, side, cross0, cross123, first, count):
     smem = pl.BlockSpec(memory_space=pltpu.SMEM)
     return pl.pallas_call(
         functools.partial(blend_kernel, first, count),
         out_shape=jax.ShapeDtypeStruct((16, count, K), jnp.bfloat16),
-        in_specs=[smem, smem] + [pl.BlockSpec(memory_space=pltpu.HBM)] * 5,
+        in_specs=[smem, smem] + [pl.BlockSpec(memory_space=pltpu.HBM)] * 4,
         out_specs=pl.BlockSpec(memory_space=pltpu.VMEM),
         scratch_shapes=[
             pltpu.VMEM((12, count, K), jnp.bfloat16),
-            pltpu.SemaphoreType.DMA((5,)),
+            pltpu.SemaphoreType.DMA((4,)),
         ],
         compiler_params=pltpu.CompilerParams(vmem_limit_bytes=VMEM_LIMIT),
         cost_estimate=LIGHT,
-    )(where, params, own01, own23, cross01, cross23, side)
+    )(where, params, own, side, cross0, cross123)
 
 
 def sub_block(product, cols, rows):
@@ -255,26 +255,25 @@
     keep, to_mate, to_far = split_centres(where, sides[0, 0], quarters[0, 0], centres[0, 0])
     mate = shift(to_mate, perm=CORE)
     own23 = shift(jnp.stack([to_far, mate[1]]), perm=PAL)
-    own01 = jnp.stack([keep, mate[0]])
-    cross01 = shift(own01, perm=CROSS)
-    own_a = jnp.concatenate([own01[:, :CUT], own23[:, :CUT]])
-    own_b = jnp.concatenate([own01[:, CUT:JQ], own23[:, CUT:JQ]])
-    mine, own01, own23, own_a, own_b, cross01 = lax.optimization_barrier(
-        (mine, own01, own23, own_a, own_b, cross01)
+    cross0 = shift(keep, perm=CROSS)
+    own_a = jnp.concatenate([keep[None, :CUT], mate[:1, :CUT], own23[:, :CUT]])
+    own_b = jnp.concatenate([keep[None, CUT:JQ], mate[:1, CUT:JQ], own23[:, CUT:JQ]])
+    own123 = jnp.concatenate([mate[:1], own23])
+    mine, own123, own_a, own_b, cross0 = lax.optimization_barrier(
+        (mine, own123, own_a, own_b, cross0)
     )
 
     far = shift(mine, perm=PAL)
     side_a = shift(own_a, perm=SIDE)
-    cross23 = shift(own23, perm=CROSS)
+    cross123 = shift(own123, perm=CROSS)
     side_b = shift(own_b, perm=SIDE)
     near = shift(mine, perm=CORE)
-    params = jnp.concatenate([cross01[:, JQ, :16], cross23[:, JQ, :16]]).astype(jnp.int32)
-    four = (own01, own23, cross01, cross23)
-    blend_a = blend_centres(where, params, *four, side_a, 0, CUT)
+    params = jnp.concatenate([cross0[JQ : JQ + 1, :16], cross123[:, JQ, :16]]).astype(jnp.int32)
+    blend_a = blend_centres(where, params, own_a, side_a, cross0, cross123, 0, CUT)
     part = apply_here(blend_a, mine, near)
     far, part, side_b = lax.optimization_barrier((far, part, side_b))
     far_near = shift(far, perm=CORE)
-    blend_b = blend_centres(where, params, *four, side_b, CUT, JQ - CUT)
+    blend_b = blend_centres(where, params, own_b, side_b, cross0, cross123, CUT, JQ - CUT)
     result = apply_transforms(where, blend_a, blend_b, part, (mine, near, far, far_near))
 
     got = lax.all_to_all(

time: 199 us -> 195 us (0.980)
  local copies, waits for them, and re-layouts: 11.4 us -> 9.27 us
  blocking collectives: 64.9 us -> 62.8 us
  waiting for transfers between devices: 72.5 us -> 74.5 us
    all_to_all x1, waiting for transfers between devices: 0.01 us -> 10.8 us  [body(): lax.all_to_all(by_col, AX, 0, 0, axis_index_groups=FIELD_GROUPS, tiled=True)]
    ppermute x1, waiting for transfers between devices: 6.81 us -> 0.01 us  [body(): side_a = shift(own_a, perm=SIDE)]
    ppermute x1, starting transfers between devices: 3.67 us -> 0.87 us  [body(): side_a = shift(own_a, perm=SIDE)]
    ppermute x1, starting transfers between devices: 1.18 us -> 3.78 us  [body(): near = shift(mine, perm=CORE)]
    ppermute x1, starting transfers between devices: 2.38 us -> 0.03 us  [body(): side_b = shift(own_b, perm=SIDE)]
    unnamed x15 -> x10, local copies, waits for them, and re-layouts: 7.92 us -> 5.69 us
    ppermute x2, waiting for transfers between devices: 37.8 us -> 35.6 us  [the longest x1 35.6 us: body(): cross123 = shift(own123, perm=CROSS)]
    all_to_all x1, blocking collectives: 64.9 us -> 62.8 us  [body(): lax.all_to_all(result.reshape(MEM * GRP, 16, 256), AX, 0, 0, axis_index_g...]
  transfers between devices with their start and end apart: 10 -> 10, of which waited for: 7 -> 5; matrix products, arithmetic and copies ran while one was open for 2% -> 2% of each run, Pallas kernels for 8% -> 8%
where the time goes in v3:
time: 195 us
  waiting for transfers between devices  74.5 us (38%)
  blocking collectives  62.8 us (32%)
  starting transfers between devices  24.9 us (13%)
  Pallas kernels  20.7 us (11%)
  local copies, waits for them, and re-layouts  9.27 us (5%)
  other arithmetic  2.57 us (1%)
    all_to_all x1, blocking collectives, body(): lax.all_to_all(result.reshape(MEM * GRP, 16, 256), AX, 0, 0, axis_index_g...  62.8 us
    ppermute x1, waiting for transfers between devices, body(): cross123 = shift(own123, perm=CROSS)  35.6 us
    ppermute x1, waiting for transfers between devices, body(): own23 = shift(jnp.stack([to_far, mate[1]]), perm=PAL)  25 us
    all_to_all x1, starting transfers between devices, body(): lax.all_to_all(by_col, AX, 0, 0, axis_index_groups=FIELD_GROUPS, tiled=True)  14.9 us
    pallas_call x2, Pallas kernels, blend_centres(): pl.pallas_call(functools.partial(blend_kernel, first, count), out_shape=j...  10.8 us
    all_to_all x1, waiting for transfers between devices, body(): lax.all_to_all(by_col, AX, 0, 0, axis_index_groups=FIELD_GROUPS, tiled=True)  10.8 us
    unnamed x10, local copies, waits for them, and re-layouts  5.69 us
    pallas_call x1, Pallas kernels, apply_transforms(): pl.pallas_call(apply_kernel, out_shape=jax.ShapeDtypeStruct((32, 2, 4, 16...  4.77 us
  transfers between devices with their start and end apart: 10, of which 5 were waited for; matrix products, arithmetic and copies ran while one was open for 2% of the time, Pallas kernels for 8%

profile of v3, /device:TPU:1, one launch (start us, length us, event | category | flops | bytes accessed | tf_op | source)
XLA Modules:
  0.0 195.0 jit_solution(318475152726020437)
XLA Ops:
  0.0 4.1 %copy.16 = bf16[1,16,4,64,256]{4,1,2,3,0:T(8,128)(2,1)} copy(bf16[1,16,4,64,256]{4,3,2,1,0:T(8,128)(2,1)} %param.4) | data formatting | bytes 4194304 | tf_op args[0]
  4.1 14.9 %all-to-all-start = ((bf16[64,4,16,256]{3,2,1,0:T(8,128)(2,1)}), bf16[64,4,16,256]{3,2,1,0:T(8,128)(2,1)S(1)}, u32[]{:S(2)}, u32[]{:S(2)}) async-start(bf16[64,4,16,256]{3,2,1,0:T(8,128)(2,1)} %bitcast.37), calls=%async_computation | async-start | bytes 4194304 | tf_op jit(solution)/shard_map/all_to_all | solution.py:253
  19.3 1.6 copy-done.1
  20.9 3.0 %shard_map.46 = (bf16[272,1024]{1,0:T(8,128)(2,1)S(1)}, bf16[2,272,1024]{2,1,0:T(8,128)(2,1)S(1)}, bf16[272,1024]{1,0:T(8,128)(2,1)S(1)}) custom-call(s32[3]{0:T(128)S(1)} %pad_add_fusion.where_ref, s32[4,2]{1,0:T(4,128)S(1)} %copy.10.sides_ref, s32[4,2]{1,0:T(4,128)S(1)} %copy.11.quarters_ref, bf16[32,2,16,1024]{3,2,1,0:T(8,128)(2,1)S(1)} %bitcast.35), custom_call_target="tpu_custom_call" | custom-call | flops 1 | bytes 1 | tf_op jit(solution)/shard_map/pallas_call | solution.py:78
  23.8 1.3 collective-permute-start
  25.2 2.4 %collective-permute-done = bf16[2,272,1024]{2,1,0:T(8,128)(2,1)S(1)} collective-permute-done((bf16[2,272,1024]{2,1,0:T(8,128)(2,1)S(1)}, bf16[2,272,1024]{2,1,0:T(8,128)(2,1)S(1)}, u32[]{:S(2)}, u32[]{:S(2)}) %collective-permute-start) | collective-permute-done | bytes 1114144 | tf_op jit(solution)/shard_map/ppermute | solution.py:256
  27.8 0.6 collective-permute-start.2
  28.6 25.0 %collective-permute-done.1 = bf16[2,272,1024]{2,1,0:T(8,128)(2,1)S(1)} collective-permute-done((bf16[2,272,1024]{2,1,0:T(8,128)(2,1)S(1)}, bf16[2,272,1024]{2,1,0:T(8,128)(2,1)S(1)}, u32[]{:S(2)}, u32[]{:S(2)}) %collective-permute-start.1) | collective-permute-done | bytes 1114144 | tf_op jit(solution)/shard_map/ppermute | solution.py:257
  53.7 0.9 pad_maximum_fusion.3.own
  54.7 1.3 pad_maximum_fusion
  56.1 10.8 %all-to-all-done = bf16[64,4,16,256]{3,2,1,0:T(8,128)(2,1)S(1)} async-done(((bf16[64,4,16,256]{3,2,1,0:T(8,128)(2,1)}), bf16[64,4,16,256]{3,2,1,0:T(8,128)(2,1)S(1)}, u32[]{:S(2)}, u32[]{:S(2)}) %all-to-all-start) | async-done | bytes 2097184 | tf_op jit(solution)/shard_map/all_to_all | solution.py:253
  66.8 3.8 %collective-permute-start.6 = (bf16[64,4,16,256]{3,2,1,0:T(8,128)(2,1)S(1)}, bf16[64,4,16,256]{3,2,1,0:T(8,128)(2,1)S(1)}, u32[]{:S(2)}, u32[]{:S(2)}) collective-permute-start(bf16[64,4,16,256]{3,2,1,0:T(8,128)(2,1)S(1)} %all-to-all-done), channel_id=1, source_target_pairs={{0,1},{1,0},{2,3},{3,2},{4,5},{5,4},{6,7},{7,6},{8,9},{9,8},{10,11... | collective-permute-start | bytes 6291464 | tf_op jit(solution)/shard_map/ppermute | solution.py:270
  70.6 2.2 %collective-permute-start.3 = (bf16[3,272,1024]{2,1,0:T(8,128)(2,1)}, bf16[3,272,1024]{2,1,0:T(8,128)(2,1)S(1)}, u32[]{:S(2)}, u32[]{:S(2)}) collective-permute-start(bf16[3,272,1024]{2,1,0:T(8,128)(2,1)} %pad_maximum_fusion), channel_id=1, source_target_pairs={{0,6},{1,7},{2,4},{3,5},{4,2},{5,3},{6,0},{7,1},{8,14},{9,15},{10,... | collective-permute-start | bytes 5013512 | tf_op jit(solution)/shard_map/ppermute | solution.py:268
  72.8 0.9 collective-permute-start.4
  73.7 0.7 slice.38
  74.4 35.6 %collective-permute-done.3.cross123 = bf16[3,272,1024]{2,1,0:T(8,128)(2,1)S(1)} collective-permute-done((bf16[3,272,1024]{2,1,0:T(8,128)(2,1)}, bf16[3,272,1024]{2,1,0:T(8,128)(2,1)S(1)}, u32[]{:S(2)}, u32[]{:S(2)}) %collective-permute-start.3) | collective-permute-done | bytes 1671200 | tf_op jit(solution)/shard_map/ppermute | solution.py:268
  110.0 6.7 %shard_map.47.blend_ref.blend_a = bf16[16,176,1024]{2,1,0:T(8,128)(2,1)S(1)} custom-call(s32[3]{0:T(128)S(1)} %pad_add_fusion.where_ref, s32[4,16]{1,0:T(4,128)S(1)} %maximum_convert_fusion.params_ref, bf16[4,176,1024]{2,1,0:T(8,128)(2,1)S(1)} %pad_maximum_fusion.1.own, bf16[4,176,1024]{2,1,0:T(8,128)(2,1)S(1)} %collective-permute-done.4.side, ...), custom_call_target="tpu_custom_call" | custom-call | flops 1 | bytes 1 | tf_op jit(solution)/shard_map/pallas_call | solution.py:134
  116.8 2.2 %shard_map.48.part = f32[4,2,4,176,128]{4,3,2,1,0:T(8,128)S(1)} custom-call(bf16[16,176,1024]{2,1,0:T(8,128)(2,1)S(1)} %shard_map.47.blend_ref.blend_a, bf16[32,2,4,16,256]{4,3,2,1,0:T(8,128)(2,1)S(1)} %bitcast.28, bf16[32,2,4,16,256]{4,3,2,1,0:T(8,128)(2,1)S(1)} %bitcast.30), custom_call_target="tpu_custom_call" | custom-call | flops 1 | bytes 1 | tf_op jit(solution)/shard_map/pallas_call | solution.py:180
  119.0 0.7 collective-permute-done.7.side
  119.7 1.1 collective-permute-start.8
  120.8 4.1 %shard_map.49.blend_b = bf16[16,80,1024]{2,1,0:T(8,128)(2,1)S(1)} custom-call(s32[3]{0:T(128)S(1)} %pad_add_fusion.where_ref, s32[4,16]{1,0:T(4,128)S(1)} %maximum_convert_fusion.params_ref, bf16[4,80,1024]{2,1,0:T(8,128)(2,1)S(1)} %copy-done, bf16[4,80,1024]{2,1,0:T(8,128)(2,1)S(1)} %collective-permute-done.7.side, ...), custom_call_target="tpu_custom_call" | custom-call | flops 1 | bytes 1 | tf_op jit(solution)/shard_map/pallas_call | solution.py:134
  124.9 4.8 %shard_map.50 = bf16[32,2,4,16,256]{4,3,2,1,0:T(8,128)(2,1)S(1)} custom-call(s32[3]{0:T(128)S(1)} %pad_add_fusion.where_ref, bf16[16,176,1024]{2,1,0:T(8,128)(2,1)S(1)} %shard_map.47.blend_ref.blend_a, bf16[16,80,1024]{2,1,0:T(8,128)(2,1)S(1)} %shard_map.49.blend_b, f32[4,2,4,176,128]{4,3,2,1,0:T(8,128)S(1)} %shard_map.48.part, ...), custom_call_target="tpu_custom_call" | custom-call | flops 1 | bytes 1 | tf_op jit(solution)/shard_map/pallas_call | solution.py:233
  129.7 62.8 %all_to_all.10 = bf16[256,16,256]{2,1,0:T(8,128)(2,1)S(1)} all-to-all(bf16[256,16,256]{2,1,0:T(8,128)(2,1)S(1)} %bitcast.32), channel_id=1, replica_groups={{6,7,4,5,0,1,2,3,14,15,12,13,8,9,10,11,22,23,20,21,16,17,18,19,30,31,28..., dimensions={0} | all-to-all | bytes 4194304 | tf_op jit(solution)/shard_map/all_to_all | solution.py:279
  192.5 2.5 %copy.12 = bf16[64,64,256]{2,0,1:T(8,128)(2,1)} copy(bf16[64,64,256]{2,1,0:T(8,128)(2,1)S(1)} %bitcast.38) | data formatting | bytes 4194304 | tf_op jit(solution)/shard_map/reshape | solution.py:282
  (30 shorter events, 0.9 us)
Async XLA Ops:
  4.1 14.9 %copy-start.2 = (s32[1,1,4,2]{2,3,1,0:T(2,128)S(1)}, s32[1,1,4,2]{2,3,1,0:T(2,128)}, u32[]{:S(2)}) copy-start(s32[1,1,4,2]{2,3,1,0:T(2,128)} %param.6) | copy-start | bytes 100
  4.1 15.0 %copy-start.3 = (s32[1,1,4,2]{2,3,1,0:T(2,128)S(1)}, s32[1,1,4,2]{2,3,1,0:T(2,128)}, u32[]{:S(2)}) copy-start(s32[1,1,4,2]{2,3,1,0:T(2,128)} %param.7) | copy-start | bytes 100
  4.1 62.7 %all-to-all-start = ((bf16[64,4,16,256]{3,2,1,0:T(8,128)(2,1)}), bf16[64,4,16,256]{3,2,1,0:T(8,128)(2,1)S(1)}, u32[]{:S(2)}, u32[]{:S(2)}) async-start(bf16[64,4,16,256]{3,2,1,0:T(8,128)(2,1)} %bitcast.37), calls=%async_computation | async-start | bytes 4194304 | tf_op jit(solution)/shard_map/all_to_all | solution.py:253
  19.3 1.6 copy-start.1
  23.8 3.7 %collective-permute-start = (bf16[2,272,1024]{2,1,0:T(8,128)(2,1)S(1)}, bf16[2,272,1024]{2,1,0:T(8,128)(2,1)S(1)}, u32[]{:S(2)}, u32[]{:S(2)}) collective-permute-start(bf16[2,272,1024]{2,1,0:T(8,128)(2,1)S(1)} %get-tuple-element.16), channel_id=1, source_target_pairs={{0,1},{1,0},{2,3},{3,2},{4,5},{5,4},{6,7},{7,6},{8,9},{9,8},{10,11... | collective-permute-start | bytes 3342344 | tf_op jit(solution)/shard_map/ppermute | solution.py:256
  27.7 25.9 %collective-permute-start.1 = (bf16[2,272,1024]{2,1,0:T(8,128)(2,1)S(1)}, bf16[2,272,1024]{2,1,0:T(8,128)(2,1)S(1)}, u32[]{:S(2)}, u32[]{:S(2)}) collective-permute-start(bf16[2,272,1024]{2,1,0:T(8,128)(2,1)S(1)} %pad_maximum_fusion.2), channel_id=1, source_target_pairs={{0,2},{1,3},{2,0},{3,1},{4,6},{5,7},{6,4},{7,5},{8,10},{9,11},{10,... | collective-permute-start | bytes 3342344 | tf_op jit(solution)/shard_map/ppermute | solution.py:257
  27.8 28.2 %collective-permute-start.2 = (bf16[272,1024]{1,0:T(8,128)(2,1)S(1)}, bf16[272,1024]{1,0:T(8,128)(2,1)}, u32[]{:S(2)}, u32[]{:S(2)}) collective-permute-start(bf16[272,1024]{1,0:T(8,128)(2,1)S(1)} %get-tuple-element.18), channel_id=1, source_target_pairs={{0,6},{1,7},{2,4},{3,5},{4,2},{5,3},{6,0},{7,1},{8,14},{9,15},{10,... | collective-permute-start | bytes 1671176 | tf_op jit(solution)/shard_map/ppermute | solution.py:258
  66.8 49.9 %collective-permute-start.6 = (bf16[64,4,16,256]{3,2,1,0:T(8,128)(2,1)S(1)}, bf16[64,4,16,256]{3,2,1,0:T(8,128)(2,1)S(1)}, u32[]{:S(2)}, u32[]{:S(2)}) collective-permute-start(bf16[64,4,16,256]{3,2,1,0:T(8,128)(2,1)S(1)} %all-to-all-done), channel_id=1, source_target_pairs={{0,1},{1,0},{2,3},{3,2},{4,5},{5,4},{6,7},{7,6},{8,9},{9,8},{10,11... | collective-permute-start | bytes 6291464 | tf_op jit(solution)/shard_map/ppermute | solution.py:270
  70.6 49.1 %collective-permute-start.5 = (bf16[64,4,16,256]{3,2,1,0:T(8,128)(2,1)S(1)}, bf16[64,4,16,256]{3,2,1,0:T(8,128)(2,1)S(1)}, u32[]{:S(2)}, u32[]{:S(2)}) collective-permute-start(bf16[64,4,16,256]{3,2,1,0:T(8,128)(2,1)S(1)} %all-to-all-done), channel_id=1, source_target_pairs={{0,2},{1,3},{2,0},{3,1},{4,6},{5,7},{6,4},{7,5},{8,10},{9,11},{10,... | collective-permute-start | bytes 6291464 | tf_op jit(solution)/shard_map/ppermute | solution.py:266
  70.6 39.4 %collective-permute-start.3 = (bf16[3,272,1024]{2,1,0:T(8,128)(2,1)}, bf16[3,272,1024]{2,1,0:T(8,128)(2,1)S(1)}, u32[]{:S(2)}, u32[]{:S(2)}) collective-permute-start(bf16[3,272,1024]{2,1,0:T(8,128)(2,1)} %pad_maximum_fusion), channel_id=1, source_target_pairs={{0,6},{1,7},{2,4},{3,5},{4,2},{5,3},{6,0},{7,1},{8,14},{9,15},{10,... | collective-permute-start | bytes 5013512 | tf_op jit(solution)/shard_map/ppermute | solution.py:268
  72.8 37.2 %collective-permute-start.4 = (bf16[4,176,1024]{2,1,0:T(8,128)(2,1)S(1)}, bf16[4,176,1024]{2,1,0:T(8,128)(2,1)S(1)}, u32[]{:S(2)}, u32[]{:S(2)}) collective-permute-start(bf16[4,176,1024]{2,1,0:T(8,128)(2,1)S(1)} %pad_maximum_fusion.1.own), channel_id=1, source_target_pairs={{0,248},{1,249},{2,250},{3,251},{4,12},{5,13},{6,14},{7,15},{8,0},... | collective-permute-start | bytes 4325384 | tf_op jit(solution)/shard_map/ppermute | solution.py:267
  73.7 46.1 %collective-permute-start.7 = (bf16[4,80,1024]{2,1,0:T(8,128)(2,1)}, bf16[4,80,1024]{2,1,0:T(8,128)(2,1)S(1)}, u32[]{:S(2)}, u32[]{:S(2)}) collective-permute-start(bf16[4,80,1024]{2,1,0:T(8,128)(2,1)} %pad_maximum_fusion.3.own), channel_id=1, source_target_pairs={{0,248},{1,249},{2,250},{3,251},{4,12},{5,13},{6,14},{7,15},{8,0},... | collective-permute-start | bytes 1966088 | tf_op jit(solution)/shard_map/ppermute | solution.py:269
  116.8 4.1 %copy-start = (bf16[4,80,1024]{2,1,0:T(8,128)(2,1)S(1)}, bf16[4,80,1024]{2,1,0:T(8,128)(2,1)}, u32[]{:S(2)}) copy-start(bf16[4,80,1024]{2,1,0:T(8,128)(2,1)} %pad_maximum_fusion.3.own) | copy-start | bytes 1966084
  119.7 5.2 %collective-permute-start.8 = (bf16[64,4,16,256]{3,2,1,0:T(8,128)(2,1)S(1)}, bf16[64,4,16,256]{3,2,1,0:T(8,128)(2,1)S(1)}, u32[]{:S(2)}, u32[]{:S(2)}) collective-permute-start(bf16[64,4,16,256]{3,2,1,0:T(8,128)(2,1)S(1)} %collective-permute-done.5), channel_id=1, source_target_pairs={{0,1},{1,0},{2,3},{3,2},{4,5},{5,4},{6,7},{7,6},{8,9},{9,8},{10,11... | collective-permute-start | bytes 6291464 | tf_op jit(solution)/shard_map/ppermute | solution.py:275

commit v4 on v3

--- a/solution.py
+++ b/solution.py
@@ -15,7 +15,7 @@
 JQ = 256
 JP = JQ + 16
 HALF = K // 2
-CUT = 176
+CUT = 192
 
 
 def flat_perm(move):
@@ -39,7 +39,7 @@
     for core in range(2)
 ]
 RESULT_GROUP = [
-    [(c ^ 1) * GRP + (quarter ^ (2 * ((c ^ 1) & 1))) for c in range(MEM) for quarter in range(GRP)]
+    [(c ^ 1) * GRP + (quarter ^ (2 * ((c ^ 1) & 1))) for quarter in range(GRP) for c in range(MEM)]
 ]
 VMEM_LIMIT = 24 * 1024 * 1024
 LIGHT = pl.CostEstimate(flops=1, bytes_accessed=1, transcendentals=0)
@@ -157,6 +157,8 @@
 
 
 def here_kernel(blend_ref, mine, near, out_ref):
+    count = blend_ref.shape[1]
+
     @pl.loop(0, 4)
     def _(row):
         for pair in range(2):
@@ -165,13 +167,13 @@
                 half = 1 - two
                 left = blend_ref[pl.ds(4 * row + 2 * pair, 2), :, half * HALF : half * HALF + HALF]
                 product = jnp.dot(
-                    left.reshape(2 * CUT, HALF),
+                    left.reshape(2 * count, HALF),
                     side_by_side((mine, near), half, row, at),
                     preferred_element_type=jnp.float32,
                 )
                 for n in range(2):
                     out_ref[2 * pair + two, n, row] = sub_block(
-                        product, slice(n * 128, n * 128 + 128), CUT
+                        product, slice(n * 128, n * 128 + 128), count
                     )
 
 
@@ -179,7 +181,7 @@
     vmem = pl.BlockSpec(memory_space=pltpu.VMEM)
     return pl.pallas_call(
         here_kernel,
-        out_shape=jax.ShapeDtypeStruct((4, 2, 4, CUT, 128), jnp.float32),
+        out_shape=jax.ShapeDtypeStruct((4, 2, 4, blend.shape[1], 128), jnp.float32),
         in_specs=[vmem] * 3,
         out_specs=vmem,
         compiler_params=pltpu.CompilerParams(vmem_limit_bytes=VMEM_LIMIT),
@@ -187,8 +189,9 @@
     )(blend, mine.reshape(32, 2, 4, 16, 256), near.reshape(32, 2, 4, 16, 256))
 
 
-def apply_kernel(where_ref, blend_a, blend_b, part, mine, near, far, far_near, out_ref, total):
+def apply_kernel(where_ref, blend_a, blend_b, part_a, part_b, far, far_near, out_ref, total):
     quarter = where_ref[2]
+    rest = JQ - CUT
 
     @pl.loop(0, 4)
     def _(row):
@@ -196,27 +199,27 @@
             at = slice(pair * 128, pair * 128 + 128)
             subs = pl.ds(4 * row + 2 * pair, 2)
             for two in range(2):
-                there = side_by_side((far, far_near), two, row, at)
-                here = side_by_side((mine, near), 1 - two, row, at)
-                both = (there, here) if two == 0 else (here, there)
-                top = jnp.dot(
-                    blend_a[subs, :, two * HALF : two * HALF + HALF].reshape(2 * CUT, HALF),
-                    there,
-                    preferred_element_type=jnp.float32,
+                lanes = slice(two * HALF, two * HALF + HALF)
+                left = jnp.concatenate(
+                    [
+                        blend_a[subs, :, lanes].reshape(2 * CUT, HALF),
+                        blend_b[subs, :, lanes].reshape(2 * rest, HALF),
+                    ],
+                    axis=0,
                 )
-                rest = jnp.dot(
-                    blend_b[subs].reshape(2 * (JQ - CUT), K),
-                    jnp.concatenate(both, axis=0),
+                product = jnp.dot(
+                    left,
+                    side_by_side((far, far_near), two, row, at),
                     preferred_element_type=jnp.float32,
                 )
                 for n in range(2):
                     cols = slice(n * 128, n * 128 + 128)
                     to = (pair, 2 * two + n)
                     total[(*to, pl.ds(row, CUT, stride=4), slice(None))] = (
-                        sub_block(top, cols, CUT) + part[2 * pair + two, n, row]
+                        sub_block(product[: 2 * CUT], cols, CUT) + part_a[2 * pair + two, n, row]
                     )
-                    total[(*to, pl.ds(row + 4 * CUT, JQ - CUT, stride=4), slice(None))] = (
-                        sub_block(rest, cols, JQ - CUT)
+                    total[(*to, pl.ds(row + 4 * CUT, rest, stride=4), slice(None))] = (
+                        sub_block(product[2 * CUT :], cols, rest) + part_b[2 * pair + two, n, row]
                     )
 
     for rho in range(4):
@@ -224,21 +227,21 @@
         for pair in range(2):
             at = slice(pair * 128, pair * 128 + 128)
             done = total[pair, rho].reshape(32, 2, 16, 128).astype(jnp.bfloat16)
-            out_ref[:, 0, lax.bitwise_xor(level, 2), :, at] = done[:, 0]
-            out_ref[:, 1, level, :, at] = done[:, 1]
-
-
-def apply_transforms(where, blend_a, blend_b, part, fields):
+            out_ref[lax.bitwise_xor(level, 2), :, 0, :, at] = done[:, 0]
+            out_ref[level, :, 1, :, at] = done[:, 1]
+
+
+def apply_transforms(where, blend_a, blend_b, part_a, part_b, fields):
     vmem = pl.BlockSpec(memory_space=pltpu.VMEM)
     return pl.pallas_call(
         apply_kernel,
-        out_shape=jax.ShapeDtypeStruct((32, 2, 4, 16, 256), jnp.bfloat16),
-        in_specs=[pl.BlockSpec(memory_space=pltpu.SMEM)] + [vmem] * 7,
+        out_shape=jax.ShapeDtypeStruct((4, 32, 2, 16, 256), jnp.bfloat16),
+        in_specs=[pl.BlockSpec(memory_space=pltpu.SMEM)] + [vmem] * 6,
         out_specs=vmem,
         scratch_shapes=[pltpu.VMEM((2, 4, 4 * JQ, 128), jnp.float32)],
         compiler_params=pltpu.CompilerParams(vmem_limit_bytes=VMEM_LIMIT),
         cost_estimate=LIGHT,
-    )(where, blend_a, blend_b, part, *(f.reshape(32, 2, 4, 16, 256) for f in fields))
+    )(where, blend_a, blend_b, part_a, part_b, *(f.reshape(32, 2, 4, 16, 256) for f in fields))
 
 
 def body(fields, centres, sides, quarters):
@@ -270,16 +273,17 @@
     near = shift(mine, perm=CORE)
     params = jnp.concatenate([cross0[JQ : JQ + 1, :16], cross123[:, JQ, :16]]).astype(jnp.int32)
     blend_a = blend_centres(where, params, own_a, side_a, cross0, cross123, 0, CUT)
-    part = apply_here(blend_a, mine, near)
-    far, part, side_b = lax.optimization_barrier((far, part, side_b))
+    part_a = apply_here(blend_a, mine, near)
+    far, part_a, side_b = lax.optimization_barrier((far, part_a, side_b))
     far_near = shift(far, perm=CORE)
     blend_b = blend_centres(where, params, own_b, side_b, cross0, cross123, CUT, JQ - CUT)
-    result = apply_transforms(where, blend_a, blend_b, part, (mine, near, far, far_near))
+    part_b = apply_here(blend_b, mine, near)
+    result = apply_transforms(where, blend_a, blend_b, part_a, part_b, (far, far_near))
 
     got = lax.all_to_all(
         result.reshape(MEM * GRP, 16, 256), AX, 0, 0, axis_index_groups=RESULT_GROUP, tiled=True
     )
-    return got.reshape(MEM, 64, 256).transpose(1, 0, 2).reshape(1, 16, 4, MEM, 256)
+    return got.reshape(GRP, MEM, 16, 256).transpose(0, 2, 1, 3).reshape(1, 16, 4, MEM, 256)
 
 
 def solution(mesh):

time: 195 us -> 194 us (level)
    pallas_call x2 -> x3, Pallas kernels: 7 us -> 7.68 us  [the longest x1 3.97 us: apply_transforms(): pl.pallas_call(apply_kernel, out_shape=jax.ShapeDtypeStruct((4, 32, 2, 16...]
  transfers between devices with their start and end apart: 10 -> 10, of which waited for: 5 -> 4; matrix products, arithmetic and copies ran while one was open for 2% -> 2% of each run, Pallas kernels for 8% -> 8%
where the time goes in v4:
time: 194 us; the launch traced here: 193 us
  waiting for transfers between devices  74.2 us (38%)
  blocking collectives  62 us (32%)
  starting transfers between devices  25 us (13%)
  Pallas kernels  19.5 us (10%)
  local copies, waits for them, and re-layouts  9.63 us (5%)
  other arithmetic  2.88 us (1%)
    all_to_all x1, blocking collectives, body(): lax.all_to_all(result.reshape(MEM * GRP, 16, 256), AX, 0, 0, axis_index_g...  62 us
    ppermute x1, waiting for transfers between devices, body(): cross123 = shift(own123, perm=CROSS)  36.3 us
    ppermute x1, waiting for transfers between devices, body(): own23 = shift(jnp.stack([to_far, mate[1]]), perm=PAL)  25 us
    all_to_all x1, starting transfers between devices, body(): lax.all_to_all(by_col, AX, 0, 0, axis_index_groups=FIELD_GROUPS, tiled=True)  14.9 us
    all_to_all x1, waiting for transfers between devices, body(): lax.all_to_all(by_col, AX, 0, 0, axis_index_groups=FIELD_GROUPS, tiled=True)  10.4 us
    pallas_call x2, Pallas kernels, blend_centres(): pl.pallas_call(functools.partial(blend_kernel, first, count), out_shape=j...  8.82 us
    unnamed x10, local copies, waits for them, and re-layouts  7.09 us
    pallas_call x1, Pallas kernels, apply_transforms(): pl.pallas_call(apply_kernel, out_shape=jax.ShapeDtypeStruct((4, 32, 2, 16...  3.97 us
  transfers between devices with their start and end apart: 10, of which 4 were waited for; matrix products, arithmetic and copies ran while one was open for 2% of the time, Pallas kernels for 8%

profile of v4, /device:TPU:1, one launch (start us, length us, event | category | flops | bytes accessed | tf_op | source)
XLA Modules:
  0.0 193.3 jit_solution(816873632522034880)
XLA Ops:
  0.0 4.1 %copy.16 = bf16[1,16,4,64,256]{4,1,2,3,0:T(8,128)(2,1)} copy(bf16[1,16,4,64,256]{4,3,2,1,0:T(8,128)(2,1)} %param.4) | data formatting | bytes 4194304 | tf_op args[0]
  4.1 14.9 %all-to-all-start = ((bf16[64,4,16,256]{3,2,1,0:T(8,128)(2,1)}), bf16[64,4,16,256]{3,2,1,0:T(8,128)(2,1)S(1)}, u32[]{:S(2)}, u32[]{:S(2)}) async-start(bf16[64,4,16,256]{3,2,1,0:T(8,128)(2,1)} %bitcast.37), calls=%async_computation | async-start | bytes 4194304 | tf_op jit(solution)/shard_map/all_to_all | solution.py:256
  19.3 1.6 copy-done.1
  20.9 3.0 %shard_map.46 = (bf16[272,1024]{1,0:T(8,128)(2,1)S(1)}, bf16[2,272,1024]{2,1,0:T(8,128)(2,1)S(1)}, bf16[272,1024]{1,0:T(8,128)(2,1)S(1)}) custom-call(s32[3]{0:T(128)S(1)} %pad_add_fusion.where_ref, s32[4,2]{1,0:T(4,128)S(1)} %copy.10.sides_ref, s32[4,2]{1,0:T(4,128)S(1)} %copy.11.quarters_ref, bf16[32,2,16,1024]{3,2,1,0:T(8,128)(2,1)S(1)} %bitcast.33), custom_call_target="tpu_custom_call" | custom-call | flops 1 | bytes 1 | tf_op jit(solution)/shard_map/pallas_call | solution.py:78
  23.8 1.3 collective-permute-start
  25.2 2.4 %collective-permute-done = bf16[2,272,1024]{2,1,0:T(8,128)(2,1)S(1)} collective-permute-done((bf16[2,272,1024]{2,1,0:T(8,128)(2,1)S(1)}, bf16[2,272,1024]{2,1,0:T(8,128)(2,1)S(1)}, u32[]{:S(2)}, u32[]{:S(2)}) %collective-permute-start) | collective-permute-done | bytes 1114144 | tf_op jit(solution)/shard_map/ppermute | solution.py:259
  27.8 0.6 collective-permute-start.2
  28.6 25.0 %collective-permute-done.1 = bf16[2,272,1024]{2,1,0:T(8,128)(2,1)S(1)} collective-permute-done((bf16[2,272,1024]{2,1,0:T(8,128)(2,1)S(1)}, bf16[2,272,1024]{2,1,0:T(8,128)(2,1)S(1)}, u32[]{:S(2)}, u32[]{:S(2)}) %collective-permute-start.1) | collective-permute-done | bytes 1114144 | tf_op jit(solution)/shard_map/ppermute | solution.py:260
  53.8 1.3 pad_maximum_fusion.1.own
  55.0 1.3 pad_maximum_fusion
  56.4 10.4 %all-to-all-done = bf16[64,4,16,256]{3,2,1,0:T(8,128)(2,1)S(1)} async-done(((bf16[64,4,16,256]{3,2,1,0:T(8,128)(2,1)}), bf16[64,4,16,256]{3,2,1,0:T(8,128)(2,1)S(1)}, u32[]{:S(2)}, u32[]{:S(2)}) %all-to-all-start) | async-done | bytes 2097184 | tf_op jit(solution)/shard_map/all_to_all | solution.py:256
  66.8 3.8 %collective-permute-start.6 = (bf16[64,4,16,256]{3,2,1,0:T(8,128)(2,1)S(1)}, bf16[64,4,16,256]{3,2,1,0:T(8,128)(2,1)S(1)}, u32[]{:S(2)}, u32[]{:S(2)}) collective-permute-start(bf16[64,4,16,256]{3,2,1,0:T(8,128)(2,1)S(1)} %all-to-all-done), channel_id=1, source_target_pairs={{0,1},{1,0},{2,3},{3,2},{4,5},{5,4},{6,7},{7,6},{8,9},{9,8},{10,11... | collective-permute-start | bytes 6291464 | tf_op jit(solution)/shard_map/ppermute | solution.py:273
  70.6 2.2 %collective-permute-start.3 = (bf16[3,272,1024]{2,1,0:T(8,128)(2,1)}, bf16[3,272,1024]{2,1,0:T(8,128)(2,1)S(1)}, u32[]{:S(2)}, u32[]{:S(2)}) collective-permute-start(bf16[3,272,1024]{2,1,0:T(8,128)(2,1)} %pad_maximum_fusion), channel_id=1, source_target_pairs={{0,6},{1,7},{2,4},{3,5},{4,2},{5,3},{6,0},{7,1},{8,14},{9,15},{10,... | collective-permute-start | bytes 5013512 | tf_op jit(solution)/shard_map/ppermute | solution.py:271
  72.8 0.9 collective-permute-start.4
  73.7 36.3 %collective-permute-done.3.cross123 = bf16[3,272,1024]{2,1,0:T(8,128)(2,1)S(1)} collective-permute-done((bf16[3,272,1024]{2,1,0:T(8,128)(2,1)}, bf16[3,272,1024]{2,1,0:T(8,128)(2,1)S(1)}, u32[]{:S(2)}, u32[]{:S(2)}) %collective-permute-start.3) | collective-permute-done | bytes 1671200 | tf_op jit(solution)/shard_map/ppermute | solution.py:271
  110.0 1.4 copy-done
  111.4 6.1 %shard_map.47.blend_ref.blend_a = bf16[16,192,1024]{2,1,0:T(8,128)(2,1)S(1)} custom-call(s32[3]{0:T(128)S(1)} %pad_add_fusion.where_ref, s32[4,16]{1,0:T(4,128)S(1)} %maximum_convert_fusion.params_ref, bf16[4,192,1024]{2,1,0:T(8,128)(2,1)S(1)} %copy-done, bf16[4,192,1024]{2,1,0:T(8,128)(2,1)S(1)} %collective-permute-done.4.side, ...), custom_call_target="tpu_custom_call" | custom-call | flops 1 | bytes 1 | tf_op jit(solution)/shard_map/pallas_call | solution.py:134
  117.6 2.4 %shard_map.48.part_a = f32[4,2,4,192,128]{4,3,2,1,0:T(8,128)S(1)} custom-call(bf16[16,192,1024]{2,1,0:T(8,128)(2,1)S(1)} %shard_map.47.blend_ref.blend_a, bf16[32,2,4,16,256]{4,3,2,1,0:T(8,128)(2,1)S(1)} %bitcast.28, bf16[32,2,4,16,256]{4,3,2,1,0:T(8,128)(2,1)S(1)} %bitcast.30), custom_call_target="tpu_custom_call" | custom-call | flops 1 | bytes 1 | tf_op jit(solution)/shard_map/pallas_call | solution.py:182
  120.0 1.2 collective-permute-start.8
  121.2 2.7 %shard_map.49.blend_ref.blend_b = bf16[16,64,1024]{2,1,0:T(8,128)(2,1)S(1)} custom-call(s32[3]{0:T(128)S(1)} %pad_add_fusion.where_ref, s32[4,16]{1,0:T(4,128)S(1)} %maximum_convert_fusion.params_ref, bf16[4,64,1024]{2,1,0:T(8,128)(2,1)S(1)} %pad_maximum_fusion.3.own, bf16[4,64,1024]{2,1,0:T(8,128)(2,1)S(1)} %collective-permute-done.7.side, ...), custom_call_target="tpu_custom_call" | custom-call | flops 1 | bytes 1 | tf_op jit(solution)/shard_map/pallas_call | solution.py:134
  123.9 1.3 shard_map.50.part_b
  125.3 4.0 %shard_map.51 = bf16[4,32,2,16,256]{4,3,2,1,0:T(8,128)(2,1)S(1)} custom-call(s32[3]{0:T(128)S(1)} %pad_add_fusion.where_ref, bf16[16,192,1024]{2,1,0:T(8,128)(2,1)S(1)} %shard_map.47.blend_ref.blend_a, bf16[16,64,1024]{2,1,0:T(8,128)(2,1)S(1)} %shard_map.49.blend_ref.blend_b, f32[4,2,4,192,128]{4,3,2,1,0:T(8,128)S(1)} %shard_map.48.part_a, ...), custom_call_target="tpu_custom_call" | custom-call | flops 1 | bytes 1 | tf_op jit(solution)/shard_map/pallas_call | solution.py:236
  129.3 62.0 %all_to_all.10 = bf16[256,16,256]{2,1,0:T(8,128)(2,1)S(1)} all-to-all(bf16[256,16,256]{2,1,0:T(8,128)(2,1)S(1)} %bitcast.32), channel_id=1, replica_groups={{6,0,14,8,22,16,30,24,38,32,46,40,54,48,62,56,70,64,78,72,86,80,94,88,1..., dimensions={0} | all-to-all | bytes 4194304 | tf_op jit(solution)/shard_map/all_to_all | solution.py:283
  191.2 2.1 %copy.12 = bf16[4,64,16,256]{3,1,2,0:T(8,128)(2,1)} copy(bf16[4,64,16,256]{3,2,1,0:T(8,128)(2,1)S(1)} %bitcast.38) | data formatting | bytes 4194304 | tf_op jit(solution)/shard_map/reshape | solution.py:286
  (31 shorter events, 0.8 us)
Async XLA Ops:
  4.1 14.9 %copy-start.2 = (s32[1,1,4,2]{2,3,1,0:T(2,128)S(1)}, s32[1,1,4,2]{2,3,1,0:T(2,128)}, u32[]{:S(2)}) copy-start(s32[1,1,4,2]{2,3,1,0:T(2,128)} %param.6) | copy-start | bytes 100
  4.1 15.0 %copy-start.3 = (s32[1,1,4,2]{2,3,1,0:T(2,128)S(1)}, s32[1,1,4,2]{2,3,1,0:T(2,128)}, u32[]{:S(2)}) copy-start(s32[1,1,4,2]{2,3,1,0:T(2,128)} %param.7) | copy-start | bytes 100
  4.1 62.7 %all-to-all-start = ((bf16[64,4,16,256]{3,2,1,0:T(8,128)(2,1)}), bf16[64,4,16,256]{3,2,1,0:T(8,128)(2,1)S(1)}, u32[]{:S(2)}, u32[]{:S(2)}) async-start(bf16[64,4,16,256]{3,2,1,0:T(8,128)(2,1)} %bitcast.37), calls=%async_computation | async-start | bytes 4194304 | tf_op jit(solution)/shard_map/all_to_all | solution.py:256
  19.3 1.6 copy-start.1
  23.8 3.7 %collective-permute-start = (bf16[2,272,1024]{2,1,0:T(8,128)(2,1)S(1)}, bf16[2,272,1024]{2,1,0:T(8,128)(2,1)S(1)}, u32[]{:S(2)}, u32[]{:S(2)}) collective-permute-start(bf16[2,272,1024]{2,1,0:T(8,128)(2,1)S(1)} %get-tuple-element.16), channel_id=1, source_target_pairs={{0,1},{1,0},{2,3},{3,2},{4,5},{5,4},{6,7},{7,6},{8,9},{9,8},{10,11... | collective-permute-start | bytes 3342344 | tf_op jit(solution)/shard_map/ppermute | solution.py:259
  27.7 25.9 %collective-permute-start.1 = (bf16[2,272,1024]{2,1,0:T(8,128)(2,1)S(1)}, bf16[2,272,1024]{2,1,0:T(8,128)(2,1)S(1)}, u32[]{:S(2)}, u32[]{:S(2)}) collective-permute-start(bf16[2,272,1024]{2,1,0:T(8,128)(2,1)S(1)} %pad_maximum_fusion.2), channel_id=1, source_target_pairs={{0,2},{1,3},{2,0},{3,1},{4,6},{5,7},{6,4},{7,5},{8,10},{9,11},{10,... | collective-permute-start | bytes 3342344 | tf_op jit(solution)/shard_map/ppermute | solution.py:260
  27.8 28.5 %collective-permute-start.2 = (bf16[272,1024]{1,0:T(8,128)(2,1)S(1)}, bf16[272,1024]{1,0:T(8,128)(2,1)S(1)}, u32[]{:S(2)}, u32[]{:S(2)}) collective-permute-start(bf16[272,1024]{1,0:T(8,128)(2,1)S(1)} %get-tuple-element.18), channel_id=1, source_target_pairs={{0,6},{1,7},{2,4},{3,5},{4,2},{5,3},{6,0},{7,1},{8,14},{9,15},{10,... | collective-permute-start | bytes 1671176 | tf_op jit(solution)/shard_map/ppermute | solution.py:261
  66.8 50.7 %collective-permute-start.6 = (bf16[64,4,16,256]{3,2,1,0:T(8,128)(2,1)S(1)}, bf16[64,4,16,256]{3,2,1,0:T(8,128)(2,1)S(1)}, u32[]{:S(2)}, u32[]{:S(2)}) collective-permute-start(bf16[64,4,16,256]{3,2,1,0:T(8,128)(2,1)S(1)} %all-to-all-done), channel_id=1, source_target_pairs={{0,1},{1,0},{2,3},{3,2},{4,5},{5,4},{6,7},{7,6},{8,9},{9,8},{10,11... | collective-permute-start | bytes 6291464 | tf_op jit(solution)/shard_map/ppermute | solution.py:273
  70.6 49.4 %collective-permute-start.5 = (bf16[64,4,16,256]{3,2,1,0:T(8,128)(2,1)S(1)}, bf16[64,4,16,256]{3,2,1,0:T(8,128)(2,1)S(1)}, u32[]{:S(2)}, u32[]{:S(2)}) collective-permute-start(bf16[64,4,16,256]{3,2,1,0:T(8,128)(2,1)S(1)} %all-to-all-done), channel_id=1, source_target_pairs={{0,2},{1,3},{2,0},{3,1},{4,6},{5,7},{6,4},{7,5},{8,10},{9,11},{10,... | collective-permute-start | bytes 6291464 | tf_op jit(solution)/shard_map/ppermute | solution.py:269
  70.6 39.4 %collective-permute-start.3 = (bf16[3,272,1024]{2,1,0:T(8,128)(2,1)}, bf16[3,272,1024]{2,1,0:T(8,128)(2,1)S(1)}, u32[]{:S(2)}, u32[]{:S(2)}) collective-permute-start(bf16[3,272,1024]{2,1,0:T(8,128)(2,1)} %pad_maximum_fusion), channel_id=1, source_target_pairs={{0,6},{1,7},{2,4},{3,5},{4,2},{5,3},{6,0},{7,1},{8,14},{9,15},{10,... | collective-permute-start | bytes 5013512 | tf_op jit(solution)/shard_map/ppermute | solution.py:271
  72.8 37.2 %collective-permute-start.4 = (bf16[4,192,1024]{2,1,0:T(8,128)(2,1)}, bf16[4,192,1024]{2,1,0:T(8,128)(2,1)S(1)}, u32[]{:S(2)}, u32[]{:S(2)}) collective-permute-start(bf16[4,192,1024]{2,1,0:T(8,128)(2,1)} %pad_maximum_fusion.1.own), channel_id=1, source_target_pairs={{0,248},{1,249},{2,250},{3,251},{4,12},{5,13},{6,14},{7,15},{8,0},... | collective-permute-start | bytes 4718600 | tf_op jit(solution)/shard_map/ppermute | solution.py:270
  73.7 46.3 %collective-permute-start.7 = (bf16[4,64,1024]{2,1,0:T(8,128)(2,1)S(1)}, bf16[4,64,1024]{2,1,0:T(8,128)(2,1)S(1)}, u32[]{:S(2)}, u32[]{:S(2)}) collective-permute-start(bf16[4,64,1024]{2,1,0:T(8,128)(2,1)S(1)} %pad_maximum_fusion.3.own), channel_id=1, source_target_pairs={{0,248},{1,249},{2,250},{3,251},{4,12},{5,13},{6,14},{7,15},{8,0},... | collective-permute-start | bytes 1572872 | tf_op jit(solution)/shard_map/ppermute | solution.py:272
  110.0 1.4 copy-start
  120.0 5.3 %collective-permute-start.8 = (bf16[64,4,16,256]{3,2,1,0:T(8,128)(2,1)S(1)}, bf16[64,4,16,256]{3,2,1,0:T(8,128)(2,1)S(1)}, u32[]{:S(2)}, u32[]{:S(2)}) collective-permute-start(bf16[64,4,16,256]{3,2,1,0:T(8,128)(2,1)S(1)} %collective-permute-done.5), channel_id=1, source_target_pairs={{0,1},{1,0},{2,3},{3,2},{4,5},{5,4},{6,7},{7,6},{8,9},{9,8},{10,11... | collective-permute-start | bytes 6291464 | tf_op jit(solution)/shard_map/ppermute | solution.py:278

commit v5 on v4

--- a/solution.py
+++ b/solution.py
@@ -118,7 +118,7 @@
             terms = ((a * (1.0 - b), i_row), ((1.0 - a) * b, i_col), (a * b, i_diag))
             plans.append(((1.0 - a) * (1.0 - b), terms))
 
-        @pl.loop(0, count // 16)
+        @pl.loop(0, count // 16, unroll=2)
         def _(step):
             at = pl.ds(pl.multiple_of(step * 16, 16), 16)
             own_part = table[8 + i_own, at, :].astype(jnp.float32)
@@ -159,7 +159,7 @@
 def here_kernel(blend_ref, mine, near, out_ref):
     count = blend_ref.shape[1]
 
-    @pl.loop(0, 4)
+    @pl.loop(0, 4, unroll=2)
     def _(row):
         for pair in range(2):
             at = slice(pair * 128, pair * 128 + 128)
@@ -193,7 +193,7 @@
     quarter = where_ref[2]
     rest = JQ - CUT
 
-    @pl.loop(0, 4)
+    @pl.loop(0, 4, unroll=2)
     def _(row):
         for pair in range(2):
             at = slice(pair * 128, pair * 128 + 128)
@@ -261,9 +261,11 @@
     cross0 = shift(keep, perm=CROSS)
     own_a = jnp.concatenate([keep[None, :CUT], mate[:1, :CUT], own23[:, :CUT]])
     own_b = jnp.concatenate([keep[None, CUT:JQ], mate[:1, CUT:JQ], own23[:, CUT:JQ]])
-    own123 = jnp.concatenate([mate[:1], own23])
-    mine, own123, own_a, own_b, cross0 = lax.optimization_barrier(
-        (mine, own123, own_a, own_b, cross0)
+    own123 = jnp.concatenate([mate[:1, :JQ], own23[:, :JQ]])
+    params = jnp.concatenate([keep[None, JQ, :128], mate[:1, JQ, :128], own23[:, JQ, :128]])
+    params = shift(params, perm=CROSS)
+    mine, own123, own_a, own_b, cross0, params = lax.optimization_barrier(
+        (mine, own123, own_a, own_b, cross0, params)
     )
 
     far = shift(mine, perm=PAL)
@@ -271,7 +273,7 @@
     cross123 = shift(own123, perm=CROSS)
     side_b = shift(own_b, perm=SIDE)
     near = shift(mine, perm=CORE)
-    params = jnp.concatenate([cross0[JQ : JQ + 1, :16], cross123[:, JQ, :16]]).astype(jnp.int32)
+    params = params[:, :16].astype(jnp.int32)
     blend_a = blend_centres(where, params, own_a, side_a, cross0, cross123, 0, CUT)
     part_a = apply_here(blend_a, mine, near)
     far, part_a, side_b = lax.optimization_barrier((far, part_a, side_b))

time: 194 us -> 193 us (level)
    ppermute x1, waiting for transfers between devices: 36.3 us -> 34.2 us  [body(): cross123 = shift(own123, perm=CROSS)]
    unnamed x10 -> x12, local copies, waits for them, and re-layouts: 7.09 us -> 7.67 us
  transfers between devices with their start and end apart: 10 -> 11, of which waited for: 4 -> 8; matrix products, arithmetic and copies ran while one was open for 2% -> 2% of each run, Pallas kernels for 8% -> 8%
where the time goes in v5:
time: 193 us
  waiting for transfers between devices  73.8 us (38%)
  blocking collectives  62.4 us (32%)
  starting transfers between devices  25.2 us (13%)
  Pallas kernels  18.4 us (10%)
  local copies, waits for them, and re-layouts  10.3 us (5%)
  other arithmetic  2.85 us (1%)
    all_to_all x1, blocking collectives, body(): lax.all_to_all(result.reshape(MEM * GRP, 16, 256), AX, 0, 0, axis_index_g...  62.4 us
    ppermute x1, waiting for transfers between devices, body(): cross123 = shift(own123, perm=CROSS)  34.2 us
    ppermute x1, waiting for transfers between devices, body(): own23 = shift(jnp.stack([to_far, mate[1]]), perm=PAL)  25 us
    all_to_all x1, starting transfers between devices, body(): lax.all_to_all(by_col, AX, 0, 0, axis_index_groups=FIELD_GROUPS, tiled=True)  14.9 us
    all_to_all x1, waiting for transfers between devices, body(): lax.all_to_all(by_col, AX, 0, 0, axis_index_groups=FIELD_GROUPS, tiled=True)  9.21 us
    pallas_call x2, Pallas kernels, blend_centres(): pl.pallas_call(functools.partial(blend_kernel, first, count), out_shape=j...  8.69 us
    unnamed x12, local copies, waits for them, and re-layouts  7.67 us
  transfers between devices with their start and end apart: 11, of which 8 were waited for; matrix products, arithmetic and copies ran while one was open for 2% of the time, Pallas kernels for 8%

profile of v5, /device:TPU:1, one launch (start us, length us, event | category | flops | bytes accessed | tf_op | source)
XLA Modules:
  0.0 193.0 jit_solution(13549377057087705620)
XLA Ops:
  0.0 4.1 %copy.16 = bf16[1,16,4,64,256]{4,1,2,3,0:T(8,128)(2,1)} copy(bf16[1,16,4,64,256]{4,3,2,1,0:T(8,128)(2,1)} %param.4) | data formatting | bytes 4194304 | tf_op args[0]
  4.1 14.9 %all-to-all-start = ((bf16[64,4,16,256]{3,2,1,0:T(8,128)(2,1)}), bf16[64,4,16,256]{3,2,1,0:T(8,128)(2,1)S(1)}, u32[]{:S(2)}, u32[]{:S(2)}) async-start(bf16[64,4,16,256]{3,2,1,0:T(8,128)(2,1)} %bitcast.39), calls=%async_computation | async-start | bytes 4194304 | tf_op jit(solution)/shard_map/all_to_all | solution.py:256
  19.3 1.6 copy-done.1
  20.9 3.0 %shard_map.46 = (bf16[272,1024]{1,0:T(8,128)(2,1)S(1)}, bf16[2,272,1024]{2,1,0:T(8,128)(2,1)S(1)}, bf16[272,1024]{1,0:T(8,128)(2,1)S(1)}) custom-call(s32[3]{0:T(128)S(1)} %pad_add_fusion.where_ref, s32[4,2]{1,0:T(4,128)S(1)} %copy.10.sides_ref, s32[4,2]{1,0:T(4,128)S(1)} %copy.11.quarters_ref, bf16[32,2,16,1024]{3,2,1,0:T(8,128)(2,1)S(1)} %bitcast.35), custom_call_target="tpu_custom_call" | custom-call | flops 1 | bytes 1 | tf_op jit(solution)/shard_map/pallas_call | solution.py:78
  23.8 1.3 collective-permute-start
  25.2 2.4 %collective-permute-done = bf16[2,272,1024]{2,1,0:T(8,128)(2,1)S(1)} collective-permute-done((bf16[2,272,1024]{2,1,0:T(8,128)(2,1)S(1)}, bf16[2,272,1024]{2,1,0:T(8,128)(2,1)S(1)}, u32[]{:S(2)}, u32[]{:S(2)}) %collective-permute-start) | collective-permute-done | bytes 1114144 | tf_op jit(solution)/shard_map/ppermute | solution.py:259
  28.6 25.0 %collective-permute-done.1 = bf16[2,272,1024]{2,1,0:T(8,128)(2,1)S(1)} collective-permute-done((bf16[2,272,1024]{2,1,0:T(8,128)(2,1)S(1)}, bf16[2,272,1024]{2,1,0:T(8,128)(2,1)S(1)}, u32[]{:S(2)}, u32[]{:S(2)}) %collective-permute-start.1) | collective-permute-done | bytes 1114144 | tf_op jit(solution)/shard_map/ppermute | solution.py:260
  54.6 1.3 pad_maximum_fusion
  55.8 1.3 pad_maximum_fusion.1.own
  57.6 9.2 %all-to-all-done = bf16[64,4,16,256]{3,2,1,0:T(8,128)(2,1)S(1)} async-done(((bf16[64,4,16,256]{3,2,1,0:T(8,128)(2,1)}), bf16[64,4,16,256]{3,2,1,0:T(8,128)(2,1)S(1)}, u32[]{:S(2)}, u32[]{:S(2)}) %all-to-all-start) | async-done | bytes 2097184 | tf_op jit(solution)/shard_map/all_to_all | solution.py:256
  66.8 3.8 %collective-permute-start.7 = (bf16[64,4,16,256]{3,2,1,0:T(8,128)(2,1)S(1)}, bf16[64,4,16,256]{3,2,1,0:T(8,128)(2,1)S(1)}, u32[]{:S(2)}, u32[]{:S(2)}) collective-permute-start(bf16[64,4,16,256]{3,2,1,0:T(8,128)(2,1)S(1)} %all-to-all-done), channel_id=1, source_target_pairs={{0,1},{1,0},{2,3},{3,2},{4,5},{5,4},{6,7},{7,6},{8,9},{9,8},{10,11... | collective-permute-start | bytes 6291464 | tf_op jit(solution)/shard_map/ppermute | solution.py:275
  70.6 2.2 %collective-permute-start.5 = (bf16[3,256,1024]{2,1,0:T(8,128)(2,1)}, bf16[3,256,1024]{2,1,0:T(8,128)(2,1)S(1)}, u32[]{:S(2)}, u32[]{:S(2)}) collective-permute-start(bf16[3,256,1024]{2,1,0:T(8,128)(2,1)} %pad_maximum_fusion), channel_id=1, source_target_pairs={{0,6},{1,7},{2,4},{3,5},{4,2},{5,3},{6,0},{7,1},{8,14},{9,15},{10,... | collective-permute-start | bytes 4718600 | tf_op jit(solution)/shard_map/ppermute | solution.py:273
  72.8 0.9 collective-permute-start.4
  73.7 34.2 %collective-permute-done.5.cross123 = bf16[3,256,1024]{2,1,0:T(8,128)(2,1)S(1)} collective-permute-done((bf16[3,256,1024]{2,1,0:T(8,128)(2,1)}, bf16[3,256,1024]{2,1,0:T(8,128)(2,1)S(1)}, u32[]{:S(2)}, u32[]{:S(2)}) %collective-permute-start.5) | collective-permute-done | bytes 1572896 | tf_op jit(solution)/shard_map/ppermute | solution.py:273
  108.7 1.4 copy-done
  110.1 6.0 %shard_map.47.blend_ref.blend_a = bf16[16,192,1024]{2,1,0:T(8,128)(2,1)S(1)} custom-call(s32[3]{0:T(128)S(1)} %pad_add_fusion.where_ref, s32[4,16]{1,0:T(4,128)S(1)} %slice_convert_fusion.params_ref, bf16[4,192,1024]{2,1,0:T(8,128)(2,1)S(1)} %copy-done, bf16[4,192,1024]{2,1,0:T(8,128)(2,1)S(1)} %collective-permute-done.4.side, ...), custom_call_target="tpu_custom_call" | custom-call | flops 1 | bytes 1 | tf_op jit(solution)/shard_map/pallas_call | solution.py:134
  116.2 2.0 %shard_map.48.part_a = f32[4,2,4,192,128]{4,3,2,1,0:T(8,128)S(1)} custom-call(bf16[16,192,1024]{2,1,0:T(8,128)(2,1)S(1)} %shard_map.47.blend_ref.blend_a, bf16[32,2,4,16,256]{4,3,2,1,0:T(8,128)(2,1)S(1)} %bitcast.30, bf16[32,2,4,16,256]{4,3,2,1,0:T(8,128)(2,1)S(1)} %bitcast.32), custom_call_target="tpu_custom_call" | custom-call | flops 1 | bytes 1 | tf_op jit(solution)/shard_map/pallas_call | solution.py:182
  118.2 1.7 collective-permute-done.8.side
  119.9 1.1 collective-permute-start.9
  121.0 2.7 %shard_map.49.blend_ref.blend_b = bf16[16,64,1024]{2,1,0:T(8,128)(2,1)S(1)} custom-call(s32[3]{0:T(128)S(1)} %pad_add_fusion.where_ref, s32[4,16]{1,0:T(4,128)S(1)} %slice_convert_fusion.params_ref, bf16[4,64,1024]{2,1,0:T(8,128)(2,1)S(1)} %pad_maximum_fusion.3.own, bf16[4,64,1024]{2,1,0:T(8,128)(2,1)S(1)} %collective-permute-done.8.side, ...), custom_call_target="tpu_custom_call" | custom-call | flops 1 | bytes 1 | tf_op jit(solution)/shard_map/pallas_call | solution.py:134
  123.7 1.0 shard_map.50.part_b
  124.8 3.7 %shard_map.51 = bf16[4,32,2,16,256]{4,3,2,1,0:T(8,128)(2,1)S(1)} custom-call(s32[3]{0:T(128)S(1)} %pad_add_fusion.where_ref, bf16[16,192,1024]{2,1,0:T(8,128)(2,1)S(1)} %shard_map.47.blend_ref.blend_a, bf16[16,64,1024]{2,1,0:T(8,128)(2,1)S(1)} %shard_map.49.blend_ref.blend_b, f32[4,2,4,192,128]{4,3,2,1,0:T(8,128)S(1)} %shard_map.48.part_a, ...), custom_call_target="tpu_custom_call" | custom-call | flops 1 | bytes 1 | tf_op jit(solution)/shard_map/pallas_call | solution.py:236
  128.5 62.4 %all_to_all.10 = bf16[256,16,256]{2,1,0:T(8,128)(2,1)S(1)} all-to-all(bf16[256,16,256]{2,1,0:T(8,128)(2,1)S(1)} %bitcast.34), channel_id=1, replica_groups={{6,0,14,8,22,16,30,24,38,32,46,40,54,48,62,56,70,64,78,72,86,80,94,88,1..., dimensions={0} | all-to-all | bytes 4194304 | tf_op jit(solution)/shard_map/all_to_all | solution.py:285
  190.9 2.1 %copy.12 = bf16[4,64,16,256]{3,1,2,0:T(8,128)(2,1)} copy(bf16[4,64,16,256]{3,2,1,0:T(8,128)(2,1)S(1)} %bitcast.40) | data formatting | bytes 4194304 | tf_op jit(solution)/shard_map/reshape | solution.py:288
  (40 shorter events, 3.6 us)
Async XLA Ops:
  4.1 14.9 %copy-start.3 = (s32[1,1,4,2]{2,3,1,0:T(2,128)S(1)}, s32[1,1,4,2]{2,3,1,0:T(2,128)}, u32[]{:S(2)}) copy-start(s32[1,1,4,2]{2,3,1,0:T(2,128)} %param.6) | copy-start | bytes 100
  4.1 15.0 %copy-start.4 = (s32[1,1,4,2]{2,3,1,0:T(2,128)S(1)}, s32[1,1,4,2]{2,3,1,0:T(2,128)}, u32[]{:S(2)}) copy-start(s32[1,1,4,2]{2,3,1,0:T(2,128)} %param.7) | copy-start | bytes 100
  4.1 62.7 %all-to-all-start = ((bf16[64,4,16,256]{3,2,1,0:T(8,128)(2,1)}), bf16[64,4,16,256]{3,2,1,0:T(8,128)(2,1)S(1)}, u32[]{:S(2)}, u32[]{:S(2)}) async-start(bf16[64,4,16,256]{3,2,1,0:T(8,128)(2,1)} %bitcast.39), calls=%async_computation | async-start | bytes 4194304 | tf_op jit(solution)/shard_map/all_to_all | solution.py:256
  19.3 1.6 copy-start.1
  23.8 3.7 %collective-permute-start = (bf16[2,272,1024]{2,1,0:T(8,128)(2,1)S(1)}, bf16[2,272,1024]{2,1,0:T(8,128)(2,1)S(1)}, u32[]{:S(2)}, u32[]{:S(2)}) collective-permute-start(bf16[2,272,1024]{2,1,0:T(8,128)(2,1)S(1)} %get-tuple-element.17), channel_id=1, source_target_pairs={{0,1},{1,0},{2,3},{3,2},{4,5},{5,4},{6,7},{7,6},{8,9},{9,8},{10,11... | collective-permute-start | bytes 3342344 | tf_op jit(solution)/shard_map/ppermute | solution.py:259
  27.7 25.9 %collective-permute-start.1 = (bf16[2,272,1024]{2,1,0:T(8,128)(2,1)S(1)}, bf16[2,272,1024]{2,1,0:T(8,128)(2,1)S(1)}, u32[]{:S(2)}, u32[]{:S(2)}) collective-permute-start(bf16[2,272,1024]{2,1,0:T(8,128)(2,1)S(1)} %pad_maximum_fusion.2), channel_id=1, source_target_pairs={{0,2},{1,3},{2,0},{3,1},{4,6},{5,7},{6,4},{7,5},{8,10},{9,11},{10,... | collective-permute-start | bytes 3342344 | tf_op jit(solution)/shard_map/ppermute | solution.py:260
  27.8 29.4 %collective-permute-start.2 = (bf16[272,1024]{1,0:T(8,128)(2,1)S(1)}, bf16[272,1024]{1,0:T(8,128)(2,1)S(1)}, u32[]{:S(2)}, u32[]{:S(2)}) collective-permute-start(bf16[272,1024]{1,0:T(8,128)(2,1)S(1)} %get-tuple-element.19), channel_id=1, source_target_pairs={{0,6},{1,7},{2,4},{3,5},{4,2},{5,3},{6,0},{7,1},{8,14},{9,15},{10,... | collective-permute-start | bytes 1671176 | tf_op jit(solution)/shard_map/ppermute | solution.py:261
  53.6 1.0 copy-start.2
  53.6 4.0 %collective-permute-start.3 = (bf16[4,128]{1,0:T(4,128)(2,1)S(1)}, bf16[4,128]{1,0:T(4,128)(2,1)S(1)}, u32[]{:S(2)}, u32[]{:S(2)}) collective-permute-start(bf16[4,128]{1,0:T(4,128)(2,1)S(1)} %pad_maximum_fusion.4), channel_id=1, source_target_pairs={{0,6},{1,7},{2,4},{3,5},{4,2},{5,3},{6,0},{7,1},{8,14},{9,15},{10,... | collective-permute-start | bytes 3080 | tf_op jit(solution)/shard_map/ppermute | solution.py:266
  55.8 1.3 slice-start
  66.8 49.3 %collective-permute-start.7 = (bf16[64,4,16,256]{3,2,1,0:T(8,128)(2,1)S(1)}, bf16[64,4,16,256]{3,2,1,0:T(8,128)(2,1)S(1)}, u32[]{:S(2)}, u32[]{:S(2)}) collective-permute-start(bf16[64,4,16,256]{3,2,1,0:T(8,128)(2,1)S(1)} %all-to-all-done), channel_id=1, source_target_pairs={{0,1},{1,0},{2,3},{3,2},{4,5},{5,4},{6,7},{7,6},{8,9},{9,8},{10,11... | collective-permute-start | bytes 6291464 | tf_op jit(solution)/shard_map/ppermute | solution.py:275
  70.6 49.3 %collective-permute-start.6 = (bf16[64,4,16,256]{3,2,1,0:T(8,128)(2,1)S(1)}, bf16[64,4,16,256]{3,2,1,0:T(8,128)(2,1)S(1)}, u32[]{:S(2)}, u32[]{:S(2)}) collective-permute-start(bf16[64,4,16,256]{3,2,1,0:T(8,128)(2,1)S(1)} %all-to-all-done), channel_id=1, source_target_pairs={{0,2},{1,3},{2,0},{3,1},{4,6},{5,7},{6,4},{7,5},{8,10},{9,11},{10,... | collective-permute-start | bytes 6291464 | tf_op jit(solution)/shard_map/ppermute | solution.py:271
  70.6 37.3 %collective-permute-start.5 = (bf16[3,256,1024]{2,1,0:T(8,128)(2,1)}, bf16[3,256,1024]{2,1,0:T(8,128)(2,1)S(1)}, u32[]{:S(2)}, u32[]{:S(2)}) collective-permute-start(bf16[3,256,1024]{2,1,0:T(8,128)(2,1)} %pad_maximum_fusion), channel_id=1, source_target_pairs={{0,6},{1,7},{2,4},{3,5},{4,2},{5,3},{6,0},{7,1},{8,14},{9,15},{10,... | collective-permute-start | bytes 4718600 | tf_op jit(solution)/shard_map/ppermute | solution.py:273
  72.8 35.9 %collective-permute-start.4 = (bf16[4,192,1024]{2,1,0:T(8,128)(2,1)}, bf16[4,192,1024]{2,1,0:T(8,128)(2,1)S(1)}, u32[]{:S(2)}, u32[]{:S(2)}) collective-permute-start(bf16[4,192,1024]{2,1,0:T(8,128)(2,1)} %pad_maximum_fusion.1.own), channel_id=1, source_target_pairs={{0,248},{1,249},{2,250},{3,251},{4,12},{5,13},{6,14},{7,15},{8,0},... | collective-permute-start | bytes 4718600 | tf_op jit(solution)/shard_map/ppermute | solution.py:272
  73.7 46.3 %collective-permute-start.8 = (bf16[4,64,1024]{2,1,0:T(8,128)(2,1)S(1)}, bf16[4,64,1024]{2,1,0:T(8,128)(2,1)S(1)}, u32[]{:S(2)}, u32[]{:S(2)}) collective-permute-start(bf16[4,64,1024]{2,1,0:T(8,128)(2,1)S(1)} %pad_maximum_fusion.3.own), channel_id=1, source_target_pairs={{0,248},{1,249},{2,250},{3,251},{4,12},{5,13},{6,14},{7,15},{8,0},... | collective-permute-start | bytes 1572872 | tf_op jit(solution)/shard_map/ppermute | solution.py:274
  108.7 1.4 copy-start
  119.9 4.9 %collective-permute-start.9 = (bf16[64,4,16,256]{3,2,1,0:T(8,128)(2,1)S(1)}, bf16[64,4,16,256]{3,2,1,0:T(8,128)(2,1)S(1)}, u32[]{:S(2)}, u32[]{:S(2)}) collective-permute-start(bf16[64,4,16,256]{3,2,1,0:T(8,128)(2,1)S(1)} %collective-permute-done.6), channel_id=1, source_target_pairs={{0,1},{1,0},{2,3},{3,2},{4,5},{5,4},{6,7},{7,6},{8,9},{9,8},{10,11... | collective-permute-start | bytes 6291464 | tf_op jit(solution)/shard_map/ppermute | solution.py:280

commit v6 on v5

--- a/solution.py
+++ b/solution.py
@@ -85,7 +85,7 @@
     )(where, sides, quarters, centre.reshape(32, 2, 16, K))
 
 
-def blend_kernel(first, count, where_ref, params_ref, own, side, cross0, cross123, out_ref, table, sems):
+def blend_kernel(first, count, where_ref, params_ref, cross0, cross123, own, side, out_ref, table, sems):
     grp = where_ref[0]
     parity = where_ref[1]
     at = pl.ds(first, count)
@@ -142,7 +142,7 @@
         ],
         compiler_params=pltpu.CompilerParams(vmem_limit_bytes=VMEM_LIMIT),
         cost_estimate=LIGHT,
-    )(where, params, own, side, cross0, cross123)
+    )(where, params, cross0, cross123, own, side)
 
 
 def sub_block(product, cols, rows):
@@ -226,7 +226,7 @@
         level = lax.bitwise_xor(quarter, rho)
         for pair in range(2):
             at = slice(pair * 128, pair * 128 + 128)
-            done = total[pair, rho].reshape(32, 2, 16, 128).astype(jnp.bfloat16)
+            done = total[pair, rho, : 4 * JQ].reshape(32, 2, 16, 128).astype(jnp.bfloat16)
             out_ref[lax.bitwise_xor(level, 2), :, 0, :, at] = done[:, 0]
             out_ref[level, :, 1, :, at] = done[:, 1]
 
@@ -238,7 +238,7 @@
         out_shape=jax.ShapeDtypeStruct((4, 32, 2, 16, 256), jnp.bfloat16),
         in_specs=[pl.BlockSpec(memory_space=pltpu.SMEM)] + [vmem] * 6,
         out_specs=vmem,
-        scratch_shapes=[pltpu.VMEM((2, 4, 4 * JQ, 128), jnp.float32)],
+        scratch_shapes=[pltpu.VMEM((2, 4, 4 * JQ + 8, 128), jnp.float32)],
         compiler_params=pltpu.CompilerParams(vmem_limit_bytes=VMEM_LIMIT),
         cost_estimate=LIGHT,
     )(where, blend_a, blend_b, part_a, part_b, *(f.reshape(32, 2, 4, 16, 256) for f in fields))
@@ -269,8 +269,8 @@
     )
 
     far = shift(mine, perm=PAL)
+    cross123 = shift(own123, perm=CROSS)
     side_a = shift(own_a, perm=SIDE)
-    cross123 = shift(own123, perm=CROSS)
     side_b = shift(own_b, perm=SIDE)
     near = shift(mine, perm=CORE)
     params = params[:, :16].astype(jnp.int32)

time: 193 us -> 193 us (level)
  no operation moved by 1% of the time
where the time goes in v6:
time: 193 us
  waiting for transfers between devices  73.8 us (38%)
  blocking collectives  62.4 us (32%)
  starting transfers between devices  25.2 us (13%)
  Pallas kernels  18.4 us (10%)
  local copies, waits for them, and re-layouts  10.3 us (5%)
  other arithmetic  2.85 us (1%)
    all_to_all x1, blocking collectives, body(): lax.all_to_all(result.reshape(MEM * GRP, 16, 256), AX, 0, 0, axis_index_g...  62.4 us
    ppermute x1, waiting for transfers between devices, body(): cross123 = shift(own123, perm=CROSS)  34.2 us
    ppermute x1, waiting for transfers between devices, body(): own23 = shift(jnp.stack([to_far, mate[1]]), perm=PAL)  25 us
    all_to_all x1, starting transfers between devices, body(): lax.all_to_all(by_col, AX, 0, 0, axis_index_groups=FIELD_GROUPS, tiled=True)  14.9 us
    all_to_all x1, waiting for transfers between devices, body(): lax.all_to_all(by_col, AX, 0, 0, axis_index_groups=FIELD_GROUPS, tiled=True)  9.21 us
    pallas_call x2, Pallas kernels, blend_centres(): pl.pallas_call(functools.partial(blend_kernel, first, count), out_shape=j...  8.69 us
    unnamed x12, local copies, waits for them, and re-layouts  7.67 us
  transfers between devices with their start and end apart: 11, of which 8 were waited for; matrix products, arithmetic and copies ran while one was open for 2% of the time, Pallas kernels for 8%

profile of v6, /device:TPU:1, one launch (start us, length us, event | category | flops | bytes accessed | tf_op | source)
XLA Modules:
  0.0 193.0 jit_solution(12461995669408671844)
XLA Ops:
  0.0 4.1 %copy.16 = bf16[1,16,4,64,256]{4,1,2,3,0:T(8,128)(2,1)} copy(bf16[1,16,4,64,256]{4,3,2,1,0:T(8,128)(2,1)} %param.4) | data formatting | bytes 4194304 | tf_op args[0]
  4.1 14.9 %all-to-all-start = ((bf16[64,4,16,256]{3,2,1,0:T(8,128)(2,1)}), bf16[64,4,16,256]{3,2,1,0:T(8,128)(2,1)S(1)}, u32[]{:S(2)}, u32[]{:S(2)}) async-start(bf16[64,4,16,256]{3,2,1,0:T(8,128)(2,1)} %bitcast.39), calls=%async_computation | async-start | bytes 4194304 | tf_op jit(solution)/shard_map/all_to_all | solution.py:256
  19.3 1.6 copy-done.1
  20.9 3.0 %shard_map.46 = (bf16[272,1024]{1,0:T(8,128)(2,1)S(1)}, bf16[2,272,1024]{2,1,0:T(8,128)(2,1)S(1)}, bf16[272,1024]{1,0:T(8,128)(2,1)S(1)}) custom-call(s32[3]{0:T(128)S(1)} %pad_add_fusion.where_ref, s32[4,2]{1,0:T(4,128)S(1)} %copy.10.sides_ref, s32[4,2]{1,0:T(4,128)S(1)} %copy.11.quarters_ref, bf16[32,2,16,1024]{3,2,1,0:T(8,128)(2,1)S(1)} %bitcast.35), custom_call_target="tpu_custom_call" | custom-call | flops 1 | bytes 1 | tf_op jit(solution)/shard_map/pallas_call | solution.py:78
  23.8 1.3 collective-permute-start
  25.2 2.4 %collective-permute-done = bf16[2,272,1024]{2,1,0:T(8,128)(2,1)S(1)} collective-permute-done((bf16[2,272,1024]{2,1,0:T(8,128)(2,1)S(1)}, bf16[2,272,1024]{2,1,0:T(8,128)(2,1)S(1)}, u32[]{:S(2)}, u32[]{:S(2)}) %collective-permute-start) | collective-permute-done | bytes 1114144 | tf_op jit(solution)/shard_map/ppermute | solution.py:259
  28.6 25.0 %collective-permute-done.1 = bf16[2,272,1024]{2,1,0:T(8,128)(2,1)S(1)} collective-permute-done((bf16[2,272,1024]{2,1,0:T(8,128)(2,1)S(1)}, bf16[2,272,1024]{2,1,0:T(8,128)(2,1)S(1)}, u32[]{:S(2)}, u32[]{:S(2)}) %collective-permute-start.1) | collective-permute-done | bytes 1114144 | tf_op jit(solution)/shard_map/ppermute | solution.py:260
  54.6 1.3 pad_maximum_fusion
  55.9 1.3 pad_maximum_fusion.1.own
  57.6 9.2 %all-to-all-done = bf16[64,4,16,256]{3,2,1,0:T(8,128)(2,1)S(1)} async-done(((bf16[64,4,16,256]{3,2,1,0:T(8,128)(2,1)}), bf16[64,4,16,256]{3,2,1,0:T(8,128)(2,1)S(1)}, u32[]{:S(2)}, u32[]{:S(2)}) %all-to-all-start) | async-done | bytes 2097184 | tf_op jit(solution)/shard_map/all_to_all | solution.py:256
  66.8 3.8 %collective-permute-start.7 = (bf16[64,4,16,256]{3,2,1,0:T(8,128)(2,1)S(1)}, bf16[64,4,16,256]{3,2,1,0:T(8,128)(2,1)S(1)}, u32[]{:S(2)}, u32[]{:S(2)}) collective-permute-start(bf16[64,4,16,256]{3,2,1,0:T(8,128)(2,1)S(1)} %all-to-all-done), channel_id=1, source_target_pairs={{0,1},{1,0},{2,3},{3,2},{4,5},{5,4},{6,7},{7,6},{8,9},{9,8},{10,11... | collective-permute-start | bytes 6291464 | tf_op jit(solution)/shard_map/ppermute | solution.py:275
  70.6 2.2 %collective-permute-start.4 = (bf16[3,256,1024]{2,1,0:T(8,128)(2,1)}, bf16[3,256,1024]{2,1,0:T(8,128)(2,1)S(1)}, u32[]{:S(2)}, u32[]{:S(2)}) collective-permute-start(bf16[3,256,1024]{2,1,0:T(8,128)(2,1)} %pad_maximum_fusion), channel_id=1, source_target_pairs={{0,6},{1,7},{2,4},{3,5},{4,2},{5,3},{6,0},{7,1},{8,14},{9,15},{10,... | collective-permute-start | bytes 4718600 | tf_op jit(solution)/shard_map/ppermute | solution.py:272
  72.8 0.9 collective-permute-start.5
  73.7 34.2 %collective-permute-done.4.cross123 = bf16[3,256,1024]{2,1,0:T(8,128)(2,1)S(1)} collective-permute-done((bf16[3,256,1024]{2,1,0:T(8,128)(2,1)}, bf16[3,256,1024]{2,1,0:T(8,128)(2,1)S(1)}, u32[]{:S(2)}, u32[]{:S(2)}) %collective-permute-start.4) | collective-permute-done | bytes 1572896 | tf_op jit(solution)/shard_map/ppermute | solution.py:272
  108.7 1.4 copy-done
  110.1 6.0 %shard_map.47.blend_ref.blend_a = bf16[16,192,1024]{2,1,0:T(8,128)(2,1)S(1)} custom-call(s32[3]{0:T(128)S(1)} %pad_add_fusion.where_ref, s32[4,16]{1,0:T(4,128)S(1)} %slice_convert_fusion.params_ref, bf16[272,1024]{1,0:T(8,128)(2,1)S(1)} %collective-permute-done.2.cross0, bf16[3,256,1024]{2,1,0:T(8,128)(2,1)S(1)} %collective-permute-done.4.cross123, ...), custom_call_target="tpu_custom_call" | custom-call | flops 1 | bytes 1 | tf_op jit(solution)/shard_map/pallas_call | solution.py:134
  116.2 2.0 %shard_map.48.part_a = f32[4,2,4,192,128]{4,3,2,1,0:T(8,128)S(1)} custom-call(bf16[16,192,1024]{2,1,0:T(8,128)(2,1)S(1)} %shard_map.47.blend_ref.blend_a, bf16[32,2,4,16,256]{4,3,2,1,0:T(8,128)(2,1)S(1)} %bitcast.30, bf16[32,2,4,16,256]{4,3,2,1,0:T(8,128)(2,1)S(1)} %bitcast.32), custom_call_target="tpu_custom_call" | custom-call | flops 1 | bytes 1 | tf_op jit(solution)/shard_map/pallas_call | solution.py:182
  118.2 1.7 collective-permute-done.8.side
  119.9 1.1 collective-permute-start.9
  121.0 2.7 %shard_map.49.blend_ref.blend_b = bf16[16,64,1024]{2,1,0:T(8,128)(2,1)S(1)} custom-call(s32[3]{0:T(128)S(1)} %pad_add_fusion.where_ref, s32[4,16]{1,0:T(4,128)S(1)} %slice_convert_fusion.params_ref, bf16[272,1024]{1,0:T(8,128)(2,1)S(1)} %collective-permute-done.2.cross0, bf16[3,256,1024]{2,1,0:T(8,128)(2,1)S(1)} %collective-permute-done.4.cross123, ...), custom_call_target="tpu_custom_call" | custom-call | flops 1 | bytes 1 | tf_op jit(solution)/shard_map/pallas_call | solution.py:134
  123.7 1.0 shard_map.50.part_b
  124.8 3.7 %shard_map.51 = bf16[4,32,2,16,256]{4,3,2,1,0:T(8,128)(2,1)S(1)} custom-call(s32[3]{0:T(128)S(1)} %pad_add_fusion.where_ref, bf16[16,192,1024]{2,1,0:T(8,128)(2,1)S(1)} %shard_map.47.blend_ref.blend_a, bf16[16,64,1024]{2,1,0:T(8,128)(2,1)S(1)} %shard_map.49.blend_ref.blend_b, f32[4,2,4,192,128]{4,3,2,1,0:T(8,128)S(1)} %shard_map.48.part_a, ...), custom_call_target="tpu_custom_call" | custom-call | flops 1 | bytes 1 | tf_op jit(solution)/shard_map/pallas_call | solution.py:236
  128.5 62.4 %all_to_all.10 = bf16[256,16,256]{2,1,0:T(8,128)(2,1)S(1)} all-to-all(bf16[256,16,256]{2,1,0:T(8,128)(2,1)S(1)} %bitcast.34), channel_id=1, replica_groups={{6,0,14,8,22,16,30,24,38,32,46,40,54,48,62,56,70,64,78,72,86,80,94,88,1..., dimensions={0} | all-to-all | bytes 4194304 | tf_op jit(solution)/shard_map/all_to_all | solution.py:285
  190.9 2.1 %copy.12 = bf16[4,64,16,256]{3,1,2,0:T(8,128)(2,1)} copy(bf16[4,64,16,256]{3,2,1,0:T(8,128)(2,1)S(1)} %bitcast.40) | data formatting | bytes 4194304 | tf_op jit(solution)/shard_map/reshape | solution.py:288
  (40 shorter events, 3.6 us)
Async XLA Ops:
  4.1 14.9 %copy-start.3 = (s32[1,1,4,2]{2,3,1,0:T(2,128)S(1)}, s32[1,1,4,2]{2,3,1,0:T(2,128)}, u32[]{:S(2)}) copy-start(s32[1,1,4,2]{2,3,1,0:T(2,128)} %param.6) | copy-start | bytes 100
  4.1 15.0 %copy-start.4 = (s32[1,1,4,2]{2,3,1,0:T(2,128)S(1)}, s32[1,1,4,2]{2,3,1,0:T(2,128)}, u32[]{:S(2)}) copy-start(s32[1,1,4,2]{2,3,1,0:T(2,128)} %param.7) | copy-start | bytes 100
  4.1 62.7 %all-to-all-start = ((bf16[64,4,16,256]{3,2,1,0:T(8,128)(2,1)}), bf16[64,4,16,256]{3,2,1,0:T(8,128)(2,1)S(1)}, u32[]{:S(2)}, u32[]{:S(2)}) async-start(bf16[64,4,16,256]{3,2,1,0:T(8,128)(2,1)} %bitcast.39), calls=%async_computation | async-start | bytes 4194304 | tf_op jit(solution)/shard_map/all_to_all | solution.py:256
  19.3 1.6 copy-start.1
  23.8 3.7 %collective-permute-start = (bf16[2,272,1024]{2,1,0:T(8,128)(2,1)S(1)}, bf16[2,272,1024]{2,1,0:T(8,128)(2,1)S(1)}, u32[]{:S(2)}, u32[]{:S(2)}) collective-permute-start(bf16[2,272,1024]{2,1,0:T(8,128)(2,1)S(1)} %get-tuple-element.17), channel_id=1, source_target_pairs={{0,1},{1,0},{2,3},{3,2},{4,5},{5,4},{6,7},{7,6},{8,9},{9,8},{10,11... | collective-permute-start | bytes 3342344 | tf_op jit(solution)/shard_map/ppermute | solution.py:259
  27.7 25.9 %collective-permute-start.1 = (bf16[2,272,1024]{2,1,0:T(8,128)(2,1)S(1)}, bf16[2,272,1024]{2,1,0:T(8,128)(2,1)S(1)}, u32[]{:S(2)}, u32[]{:S(2)}) collective-permute-start(bf16[2,272,1024]{2,1,0:T(8,128)(2,1)S(1)} %pad_maximum_fusion.2), channel_id=1, source_target_pairs={{0,2},{1,3},{2,0},{3,1},{4,6},{5,7},{6,4},{7,5},{8,10},{9,11},{10,... | collective-permute-start | bytes 3342344 | tf_op jit(solution)/shard_map/ppermute | solution.py:260
  27.8 29.4 %collective-permute-start.2 = (bf16[272,1024]{1,0:T(8,128)(2,1)S(1)}, bf16[272,1024]{1,0:T(8,128)(2,1)S(1)}, u32[]{:S(2)}, u32[]{:S(2)}) collective-permute-start(bf16[272,1024]{1,0:T(8,128)(2,1)S(1)} %get-tuple-element.19), channel_id=1, source_target_pairs={{0,6},{1,7},{2,4},{3,5},{4,2},{5,3},{6,0},{7,1},{8,14},{9,15},{10,... | collective-permute-start | bytes 1671176 | tf_op jit(solution)/shard_map/ppermute | solution.py:261
  53.6 1.0 copy-start.2
  53.6 4.0 %collective-permute-start.3 = (bf16[4,128]{1,0:T(4,128)(2,1)S(1)}, bf16[4,128]{1,0:T(4,128)(2,1)S(1)}, u32[]{:S(2)}, u32[]{:S(2)}) collective-permute-start(bf16[4,128]{1,0:T(4,128)(2,1)S(1)} %pad_maximum_fusion.4), channel_id=1, source_target_pairs={{0,6},{1,7},{2,4},{3,5},{4,2},{5,3},{6,0},{7,1},{8,14},{9,15},{10,... | collective-permute-start | bytes 3080 | tf_op jit(solution)/shard_map/ppermute | solution.py:266
  55.9 1.3 slice-start
  66.8 49.3 %collective-permute-start.7 = (bf16[64,4,16,256]{3,2,1,0:T(8,128)(2,1)S(1)}, bf16[64,4,16,256]{3,2,1,0:T(8,128)(2,1)S(1)}, u32[]{:S(2)}, u32[]{:S(2)}) collective-permute-start(bf16[64,4,16,256]{3,2,1,0:T(8,128)(2,1)S(1)} %all-to-all-done), channel_id=1, source_target_pairs={{0,1},{1,0},{2,3},{3,2},{4,5},{5,4},{6,7},{7,6},{8,9},{9,8},{10,11... | collective-permute-start | bytes 6291464 | tf_op jit(solution)/shard_map/ppermute | solution.py:275
  70.6 49.3 %collective-permute-start.6 = (bf16[64,4,16,256]{3,2,1,0:T(8,128)(2,1)S(1)}, bf16[64,4,16,256]{3,2,1,0:T(8,128)(2,1)S(1)}, u32[]{:S(2)}, u32[]{:S(2)}) collective-permute-start(bf16[64,4,16,256]{3,2,1,0:T(8,128)(2,1)S(1)} %all-to-all-done), channel_id=1, source_target_pairs={{0,2},{1,3},{2,0},{3,1},{4,6},{5,7},{6,4},{7,5},{8,10},{9,11},{10,... | collective-permute-start | bytes 6291464 | tf_op jit(solution)/shard_map/ppermute | solution.py:271
  70.6 37.3 %collective-permute-start.4 = (bf16[3,256,1024]{2,1,0:T(8,128)(2,1)}, bf16[3,256,1024]{2,1,0:T(8,128)(2,1)S(1)}, u32[]{:S(2)}, u32[]{:S(2)}) collective-permute-start(bf16[3,256,1024]{2,1,0:T(8,128)(2,1)} %pad_maximum_fusion), channel_id=1, source_target_pairs={{0,6},{1,7},{2,4},{3,5},{4,2},{5,3},{6,0},{7,1},{8,14},{9,15},{10,... | collective-permute-start | bytes 4718600 | tf_op jit(solution)/shard_map/ppermute | solution.py:272
  72.8 35.9 %collective-permute-start.5 = (bf16[4,192,1024]{2,1,0:T(8,128)(2,1)}, bf16[4,192,1024]{2,1,0:T(8,128)(2,1)S(1)}, u32[]{:S(2)}, u32[]{:S(2)}) collective-permute-start(bf16[4,192,1024]{2,1,0:T(8,128)(2,1)} %pad_maximum_fusion.1.own), channel_id=1, source_target_pairs={{0,248},{1,249},{2,250},{3,251},{4,12},{5,13},{6,14},{7,15},{8,0},... | collective-permute-start | bytes 4718600 | tf_op jit(solution)/shard_map/ppermute | solution.py:273
  73.7 46.3 %collective-permute-start.8 = (bf16[4,64,1024]{2,1,0:T(8,128)(2,1)S(1)}, bf16[4,64,1024]{2,1,0:T(8,128)(2,1)S(1)}, u32[]{:S(2)}, u32[]{:S(2)}) collective-permute-start(bf16[4,64,1024]{2,1,0:T(8,128)(2,1)S(1)} %pad_maximum_fusion.3.own), channel_id=1, source_target_pairs={{0,248},{1,249},{2,250},{3,251},{4,12},{5,13},{6,14},{7,15},{8,0},... | collective-permute-start | bytes 1572872 | tf_op jit(solution)/shard_map/ppermute | solution.py:274
  108.7 1.4 copy-start
  119.9 4.9 %collective-permute-start.9 = (bf16[64,4,16,256]{3,2,1,0:T(8,128)(2,1)S(1)}, bf16[64,4,16,256]{3,2,1,0:T(8,128)(2,1)S(1)}, u32[]{:S(2)}, u32[]{:S(2)}) collective-permute-start(bf16[64,4,16,256]{3,2,1,0:T(8,128)(2,1)S(1)} %collective-permute-done.6), channel_id=1, source_target_pairs={{0,1},{1,0},{2,3},{3,2},{4,5},{5,4},{6,7},{7,6},{8,9},{9,8},{10,11... | collective-permute-start | bytes 6291464 | tf_op jit(solution)/shard_map/ppermute | solution.py:280

commit v7 on v6

--- a/solution.py
+++ b/solution.py
@@ -33,6 +33,20 @@
 SIDE = flat_perm(lambda m, g: (m + 2 if m % 2 else m - 2, g))
 
 
+def way_round(last):
+    def move(m, g):
+        z, x, parity = m // 8, m // 2 % 4, m % 2
+        if parity:
+            to_z, to_x = z + (last and x == 1), (x - 1) % 4
+        else:
+            to_z, to_x = z - (last and x == 2), (x + 1) % 4
+        return to_z % 8 * 8 + to_x * 2 + parity, g
+
+    return flat_perm(move)
+
+
+BACK = way_round(False)
+BACK_END = way_round(True)
 FIELD_GROUPS = [
     [(c ^ 1) * GRP + 2 * (((c ^ 1) & 1) ^ flank) + core for c in range(MEM)]
     for flank in range(2)
@@ -271,10 +285,11 @@
     far = shift(mine, perm=PAL)
     cross123 = shift(own123, perm=CROSS)
     side_a = shift(own_a, perm=SIDE)
-    side_b = shift(own_b, perm=SIDE)
+    side_b = shift(shift(shift(own_b, perm=BACK), perm=BACK), perm=BACK_END)
     near = shift(mine, perm=CORE)
     params = params[:, :16].astype(jnp.int32)
-    blend_a = blend_centres(where, params, own_a, side_a, cross0, cross123, 0, CUT)
+    own_far = pltpu.with_memory_space_constraint(own_a, pltpu.HBM)
+    blend_a = blend_centres(where, params, own_far, side_a, cross0, cross123, 0, CUT)
     part_a = apply_here(blend_a, mine, near)
     far, part_a, side_b = lax.optimization_barrier((far, part_a, side_b))
     far_near = shift(far, perm=CORE)

time: 193 us -> 191 us (0.990)
  waiting for transfers between devices: 73.8 us -> 71.7 us
    ppermute x1, waiting for transfers between devices: 34.2 us -> 6.88 us  [body(): cross123 = shift(own123, perm=CROSS)]
    ppermute x1 -> x3, waiting for transfers between devices: 1.74 us -> 26.7 us  [body(): side_b = shift(shift(shift(own_b, perm=BACK), perm=BACK), perm=BACK_END)]
    unnamed x12 -> x10, local copies, waits for them, and re-layouts: 7.67 us -> 6.27 us
  transfers between devices with their start and end apart: 11 -> 13, of which waited for: 8 -> 10; matrix products, arithmetic and copies ran while one was open for 2% -> 2% of each run, Pallas kernels for 8% -> 8%
where the time goes in v7:
time: 191 us
  waiting for transfers between devices  71.7 us (38%)
  blocking collectives  62.4 us (33%)
  starting transfers between devices  25.6 us (13%)
  Pallas kernels  19.3 us (10%)
  local copies, waits for them, and re-layouts  8.86 us (5%)
  other arithmetic  2.85 us (1%)
    all_to_all x1, blocking collectives, body(): lax.all_to_all(result.reshape(MEM * GRP, 16, 256), AX, 0, 0, axis_index_g...  62.4 us
    ppermute x3, waiting for transfers between devices, body(): side_b = shift(shift(shift(own_b, perm=BACK), perm=BACK), perm=BACK_END)  26.7 us
    ppermute x1, waiting for transfers between devices, body(): own23 = shift(jnp.stack([to_far, mate[1]]), perm=PAL)  25 us
    all_to_all x1, starting transfers between devices, body(): lax.all_to_all(by_col, AX, 0, 0, axis_index_groups=FIELD_GROUPS, tiled=True)  14.9 us
    pallas_call x2, Pallas kernels, blend_centres(): pl.pallas_call(functools.partial(blend_kernel, first, count), out_shape=j...  9.58 us
    all_to_all x1, waiting for transfers between devices, body(): lax.all_to_all(by_col, AX, 0, 0, axis_index_groups=FIELD_GROUPS, tiled=True)  9.21 us
    ppermute x1, waiting for transfers between devices, body(): cross123 = shift(own123, perm=CROSS)  6.88 us
    unnamed x10, local copies, waits for them, and re-layouts  6.27 us
  transfers between devices with their start and end apart: 13, of which 10 were waited for; matrix products, arithmetic and copies ran while one was open for 2% of the time, Pallas kernels for 8%

profile of v7, /device:TPU:1, one launch (start us, length us, event | category | flops | bytes accessed | tf_op | source)
XLA Modules:
  0.0 190.8 jit_solution(9763387993582146490)
XLA Ops:
  0.0 4.1 %copy.16 = bf16[1,16,4,64,256]{4,1,2,3,0:T(8,128)(2,1)} copy(bf16[1,16,4,64,256]{4,3,2,1,0:T(8,128)(2,1)} %param.4) | data formatting | bytes 4194304 | tf_op args[0]
  4.1 14.9 %all-to-all-start = ((bf16[64,4,16,256]{3,2,1,0:T(8,128)(2,1)}), bf16[64,4,16,256]{3,2,1,0:T(8,128)(2,1)S(1)}, u32[]{:S(2)}, u32[]{:S(2)}) async-start(bf16[64,4,16,256]{3,2,1,0:T(8,128)(2,1)} %bitcast.39), calls=%async_computation | async-start | bytes 4194304 | tf_op jit(solution)/shard_map/all_to_all | solution.py:270
  19.3 1.6 copy-done
  20.9 3.0 %shard_map.46 = (bf16[272,1024]{1,0:T(8,128)(2,1)S(1)}, bf16[2,272,1024]{2,1,0:T(8,128)(2,1)S(1)}, bf16[272,1024]{1,0:T(8,128)(2,1)S(1)}) custom-call(s32[3]{0:T(128)S(1)} %pad_add_fusion.where_ref, s32[4,2]{1,0:T(4,128)S(1)} %copy.10.sides_ref, s32[4,2]{1,0:T(4,128)S(1)} %copy.11.quarters_ref, bf16[32,2,16,1024]{3,2,1,0:T(8,128)(2,1)S(1)} %bitcast.35), custom_call_target="tpu_custom_call" | custom-call | flops 1 | bytes 1 | tf_op jit(solution)/shard_map/pallas_call | solution.py:92
  23.8 1.3 collective-permute-start
  25.2 2.4 %collective-permute-done = bf16[2,272,1024]{2,1,0:T(8,128)(2,1)S(1)} collective-permute-done((bf16[2,272,1024]{2,1,0:T(8,128)(2,1)S(1)}, bf16[2,272,1024]{2,1,0:T(8,128)(2,1)S(1)}, u32[]{:S(2)}, u32[]{:S(2)}) %collective-permute-start) | collective-permute-done | bytes 1114144 | tf_op jit(solution)/shard_map/ppermute | solution.py:273
  28.6 25.0 %collective-permute-done.1 = bf16[2,272,1024]{2,1,0:T(8,128)(2,1)S(1)} collective-permute-done((bf16[2,272,1024]{2,1,0:T(8,128)(2,1)S(1)}, bf16[2,272,1024]{2,1,0:T(8,128)(2,1)S(1)}, u32[]{:S(2)}, u32[]{:S(2)}) %collective-permute-start.1) | collective-permute-done | bytes 1114144 | tf_op jit(solution)/shard_map/ppermute | solution.py:274
  54.6 1.3 pad_maximum_fusion
  55.9 1.3 pad_maximum_fusion.1.own
  57.6 9.2 %all-to-all-done = bf16[64,4,16,256]{3,2,1,0:T(8,128)(2,1)S(1)} async-done(((bf16[64,4,16,256]{3,2,1,0:T(8,128)(2,1)}), bf16[64,4,16,256]{3,2,1,0:T(8,128)(2,1)S(1)}, u32[]{:S(2)}, u32[]{:S(2)}) %all-to-all-start) | async-done | bytes 2097184 | tf_op jit(solution)/shard_map/all_to_all | solution.py:270
  66.8 3.8 %collective-permute-start.7 = (bf16[64,4,16,256]{3,2,1,0:T(8,128)(2,1)S(1)}, bf16[64,4,16,256]{3,2,1,0:T(8,128)(2,1)S(1)}, u32[]{:S(2)}, u32[]{:S(2)}) collective-permute-start(bf16[64,4,16,256]{3,2,1,0:T(8,128)(2,1)S(1)} %all-to-all-done), channel_id=1, source_target_pairs={{0,1},{1,0},{2,3},{3,2},{4,5},{5,4},{6,7},{7,6},{8,9},{9,8},{10,11... | collective-permute-start | bytes 6291464 | tf_op jit(solution)/shard_map/ppermute | solution.py:289
  70.6 2.2 %collective-permute-start.4 = (bf16[3,256,1024]{2,1,0:T(8,128)(2,1)}, bf16[3,256,1024]{2,1,0:T(8,128)(2,1)S(1)}, u32[]{:S(2)}, u32[]{:S(2)}) collective-permute-start(bf16[3,256,1024]{2,1,0:T(8,128)(2,1)} %pad_maximum_fusion), channel_id=1, source_target_pairs={{0,6},{1,7},{2,4},{3,5},{4,2},{5,3},{6,0},{7,1},{8,14},{9,15},{10,... | collective-permute-start | bytes 4718600 | tf_op jit(solution)/shard_map/ppermute | solution.py:286
  72.8 0.9 collective-permute-start.5
  74.3 13.5 %collective-permute-done.8 = bf16[4,64,1024]{2,1,0:T(8,128)(2,1)S(1)} collective-permute-done((bf16[4,64,1024]{2,1,0:T(8,128)(2,1)S(1)}, bf16[4,64,1024]{2,1,0:T(8,128)(2,1)S(1)}, u32[]{:S(2)}, u32[]{:S(2)}) %collective-permute-start.8) | collective-permute-done | bytes 524320 | tf_op jit(solution)/shard_map/ppermute | solution.py:288
  87.8 13.2 %collective-permute-done.9 = bf16[4,64,1024]{2,1,0:T(8,128)(2,1)S(1)} collective-permute-done((bf16[4,64,1024]{2,1,0:T(8,128)(2,1)S(1)}, bf16[4,64,1024]{2,1,0:T(8,128)(2,1)S(1)}, u32[]{:S(2)}, u32[]{:S(2)}) %collective-permute-start.9) | collective-permute-done | bytes 524320 | tf_op jit(solution)/shard_map/ppermute | solution.py:288
  101.0 6.9 %collective-permute-done.4.cross123 = bf16[3,256,1024]{2,1,0:T(8,128)(2,1)S(1)} collective-permute-done((bf16[3,256,1024]{2,1,0:T(8,128)(2,1)}, bf16[3,256,1024]{2,1,0:T(8,128)(2,1)S(1)}, u32[]{:S(2)}, u32[]{:S(2)}) %collective-permute-start.4) | collective-permute-done | bytes 1572896 | tf_op jit(solution)/shard_map/ppermute | solution.py:286
  108.7 6.9 %shard_map.47.blend_ref.blend_a = bf16[16,192,1024]{2,1,0:T(8,128)(2,1)S(1)} custom-call(s32[3]{0:T(128)S(1)} %pad_add_fusion.where_ref, s32[4,16]{1,0:T(4,128)S(1)} %slice_convert_fusion.params_ref, bf16[272,1024]{1,0:T(8,128)(2,1)S(1)} %collective-permute-done.2.cross0, bf16[3,256,1024]{2,1,0:T(8,128)(2,1)S(1)} %collective-permute-done.4.cross123, ...), custom_call_target="tpu_custom_call" | custom-call | flops 1 | bytes 1 | tf_op jit(solution)/shard_map/pallas_call | solution.py:148
  115.6 2.0 %shard_map.48.part_a = f32[4,2,4,192,128]{4,3,2,1,0:T(8,128)S(1)} custom-call(bf16[16,192,1024]{2,1,0:T(8,128)(2,1)S(1)} %shard_map.47.blend_ref.blend_a, bf16[32,2,4,16,256]{4,3,2,1,0:T(8,128)(2,1)S(1)} %bitcast.30, bf16[32,2,4,16,256]{4,3,2,1,0:T(8,128)(2,1)S(1)} %bitcast.32), custom_call_target="tpu_custom_call" | custom-call | flops 1 | bytes 1 | tf_op jit(solution)/shard_map/pallas_call | solution.py:196
  117.9 1.0 collective-permute-start.11
  118.9 2.7 %shard_map.49.blend_ref.blend_b = bf16[16,64,1024]{2,1,0:T(8,128)(2,1)S(1)} custom-call(s32[3]{0:T(128)S(1)} %pad_add_fusion.where_ref, s32[4,16]{1,0:T(4,128)S(1)} %slice_convert_fusion.params_ref, bf16[272,1024]{1,0:T(8,128)(2,1)S(1)} %collective-permute-done.2.cross0, bf16[3,256,1024]{2,1,0:T(8,128)(2,1)S(1)} %collective-permute-done.4.cross123, ...), custom_call_target="tpu_custom_call" | custom-call | flops 1 | bytes 1 | tf_op jit(solution)/shard_map/pallas_call | solution.py:148
  121.6 1.0 shard_map.50.part_b
  122.7 3.7 %shard_map.51 = bf16[4,32,2,16,256]{4,3,2,1,0:T(8,128)(2,1)S(1)} custom-call(s32[3]{0:T(128)S(1)} %pad_add_fusion.where_ref, bf16[16,192,1024]{2,1,0:T(8,128)(2,1)S(1)} %shard_map.47.blend_ref.blend_a, bf16[16,64,1024]{2,1,0:T(8,128)(2,1)S(1)} %shard_map.49.blend_ref.blend_b, f32[4,2,4,192,128]{4,3,2,1,0:T(8,128)S(1)} %shard_map.48.part_a, ...), custom_call_target="tpu_custom_call" | custom-call | flops 1 | bytes 1 | tf_op jit(solution)/shard_map/pallas_call | solution.py:250
  126.4 62.4 %all_to_all.10 = bf16[256,16,256]{2,1,0:T(8,128)(2,1)S(1)} all-to-all(bf16[256,16,256]{2,1,0:T(8,128)(2,1)S(1)} %bitcast.34), channel_id=1, replica_groups={{6,0,14,8,22,16,30,24,38,32,46,40,54,48,62,56,70,64,78,72,86,80,94,88,1..., dimensions={0} | all-to-all | bytes 4194304 | tf_op jit(solution)/shard_map/all_to_all | solution.py:300
  188.7 2.1 %copy.12 = bf16[4,64,16,256]{3,1,2,0:T(8,128)(2,1)} copy(bf16[4,64,16,256]{3,2,1,0:T(8,128)(2,1)S(1)} %bitcast.40) | data formatting | bytes 4194304 | tf_op jit(solution)/shard_map/reshape | solution.py:303
  (42 shorter events, 4.4 us)
Async XLA Ops:
  4.1 14.9 %copy-start.2 = (s32[1,1,4,2]{2,3,1,0:T(2,128)S(1)}, s32[1,1,4,2]{2,3,1,0:T(2,128)}, u32[]{:S(2)}) copy-start(s32[1,1,4,2]{2,3,1,0:T(2,128)} %param.6) | copy-start | bytes 100
  4.1 15.0 %copy-start.3 = (s32[1,1,4,2]{2,3,1,0:T(2,128)S(1)}, s32[1,1,4,2]{2,3,1,0:T(2,128)}, u32[]{:S(2)}) copy-start(s32[1,1,4,2]{2,3,1,0:T(2,128)} %param.7) | copy-start | bytes 100
  4.1 62.7 %all-to-all-start = ((bf16[64,4,16,256]{3,2,1,0:T(8,128)(2,1)}), bf16[64,4,16,256]{3,2,1,0:T(8,128)(2,1)S(1)}, u32[]{:S(2)}, u32[]{:S(2)}) async-start(bf16[64,4,16,256]{3,2,1,0:T(8,128)(2,1)} %bitcast.39), calls=%async_computation | async-start | bytes 4194304 | tf_op jit(solution)/shard_map/all_to_all | solution.py:270
  19.3 1.6 copy-start
  23.8 3.7 %collective-permute-start = (bf16[2,272,1024]{2,1,0:T(8,128)(2,1)S(1)}, bf16[2,272,1024]{2,1,0:T(8,128)(2,1)S(1)}, u32[]{:S(2)}, u32[]{:S(2)}) collective-permute-start(bf16[2,272,1024]{2,1,0:T(8,128)(2,1)S(1)} %get-tuple-element.17), channel_id=1, source_target_pairs={{0,1},{1,0},{2,3},{3,2},{4,5},{5,4},{6,7},{7,6},{8,9},{9,8},{10,11... | collective-permute-start | bytes 3342344 | tf_op jit(solution)/shard_map/ppermute | solution.py:273
  27.7 25.9 %collective-permute-start.1 = (bf16[2,272,1024]{2,1,0:T(8,128)(2,1)S(1)}, bf16[2,272,1024]{2,1,0:T(8,128)(2,1)S(1)}, u32[]{:S(2)}, u32[]{:S(2)}) collective-permute-start(bf16[2,272,1024]{2,1,0:T(8,128)(2,1)S(1)} %pad_maximum_fusion.2), channel_id=1, source_target_pairs={{0,2},{1,3},{2,0},{3,1},{4,6},{5,7},{6,4},{7,5},{8,10},{9,11},{10,... | collective-permute-start | bytes 3342344 | tf_op jit(solution)/shard_map/ppermute | solution.py:274
  27.8 29.4 %collective-permute-start.2 = (bf16[272,1024]{1,0:T(8,128)(2,1)S(1)}, bf16[272,1024]{1,0:T(8,128)(2,1)S(1)}, u32[]{:S(2)}, u32[]{:S(2)}) collective-permute-start(bf16[272,1024]{1,0:T(8,128)(2,1)S(1)} %get-tuple-element.19), channel_id=1, source_target_pairs={{0,6},{1,7},{2,4},{3,5},{4,2},{5,3},{6,0},{7,1},{8,14},{9,15},{10,... | collective-permute-start | bytes 1671176 | tf_op jit(solution)/shard_map/ppermute | solution.py:275
  53.6 1.0 copy-start.1
  53.6 4.0 %collective-permute-start.3 = (bf16[4,128]{1,0:T(4,128)(2,1)S(1)}, bf16[4,128]{1,0:T(4,128)(2,1)S(1)}, u32[]{:S(2)}, u32[]{:S(2)}) collective-permute-start(bf16[4,128]{1,0:T(4,128)(2,1)S(1)} %pad_maximum_fusion.4), channel_id=1, source_target_pairs={{0,6},{1,7},{2,4},{3,5},{4,2},{5,3},{6,0},{7,1},{8,14},{9,15},{10,... | collective-permute-start | bytes 3080 | tf_op jit(solution)/shard_map/ppermute | solution.py:280
  55.9 1.3 slice-start
  66.8 48.8 %collective-permute-start.7 = (bf16[64,4,16,256]{3,2,1,0:T(8,128)(2,1)S(1)}, bf16[64,4,16,256]{3,2,1,0:T(8,128)(2,1)S(1)}, u32[]{:S(2)}, u32[]{:S(2)}) collective-permute-start(bf16[64,4,16,256]{3,2,1,0:T(8,128)(2,1)S(1)} %all-to-all-done), channel_id=1, source_target_pairs={{0,1},{1,0},{2,3},{3,2},{4,5},{5,4},{6,7},{7,6},{8,9},{9,8},{10,11... | collective-permute-start | bytes 6291464 | tf_op jit(solution)/shard_map/ppermute | solution.py:289
  70.6 47.3 %collective-permute-start.6 = (bf16[64,4,16,256]{3,2,1,0:T(8,128)(2,1)S(1)}, bf16[64,4,16,256]{3,2,1,0:T(8,128)(2,1)S(1)}, u32[]{:S(2)}, u32[]{:S(2)}) collective-permute-start(bf16[64,4,16,256]{3,2,1,0:T(8,128)(2,1)S(1)} %all-to-all-done), channel_id=1, source_target_pairs={{0,2},{1,3},{2,0},{3,1},{4,6},{5,7},{6,4},{7,5},{8,10},{9,11},{10,... | collective-permute-start | bytes 6291464 | tf_op jit(solution)/shard_map/ppermute | solution.py:285
  70.6 37.3 %collective-permute-start.4 = (bf16[3,256,1024]{2,1,0:T(8,128)(2,1)}, bf16[3,256,1024]{2,1,0:T(8,128)(2,1)S(1)}, u32[]{:S(2)}, u32[]{:S(2)}) collective-permute-start(bf16[3,256,1024]{2,1,0:T(8,128)(2,1)} %pad_maximum_fusion), channel_id=1, source_target_pairs={{0,6},{1,7},{2,4},{3,5},{4,2},{5,3},{6,0},{7,1},{8,14},{9,15},{10,... | collective-permute-start | bytes 4718600 | tf_op jit(solution)/shard_map/ppermute | solution.py:286
  72.8 35.9 %collective-permute-start.5 = (bf16[4,192,1024]{2,1,0:T(8,128)(2,1)}, bf16[4,192,1024]{2,1,0:T(8,128)(2,1)S(1)}, u32[]{:S(2)}, u32[]{:S(2)}) collective-permute-start(bf16[4,192,1024]{2,1,0:T(8,128)(2,1)} %pad_maximum_fusion.1.own), channel_id=1, source_target_pairs={{0,248},{1,249},{2,250},{3,251},{4,12},{5,13},{6,14},{7,15},{8,0},... | collective-permute-start | bytes 4718600 | tf_op jit(solution)/shard_map/ppermute | solution.py:287
  73.7 14.1 %collective-permute-start.8 = (bf16[4,64,1024]{2,1,0:T(8,128)(2,1)S(1)}, bf16[4,64,1024]{2,1,0:T(8,128)(2,1)S(1)}, u32[]{:S(2)}, u32[]{:S(2)}) collective-permute-start(bf16[4,64,1024]{2,1,0:T(8,128)(2,1)S(1)} %pad_maximum_fusion.3.own), channel_id=1, source_target_pairs={{0,8},{1,9},{2,10},{3,11},{4,28},{5,29},{6,30},{7,31},{8,16},{9,17... | collective-permute-start | bytes 1572872 | tf_op jit(solution)/shard_map/ppermute | solution.py:288
  87.8 13.2 %collective-permute-start.9 = (bf16[4,64,1024]{2,1,0:T(8,128)(2,1)S(1)}, bf16[4,64,1024]{2,1,0:T(8,128)(2,1)S(1)}, u32[]{:S(2)}, u32[]{:S(2)}) collective-permute-start(bf16[4,64,1024]{2,1,0:T(8,128)(2,1)S(1)} %collective-permute-done.8), channel_id=1, source_target_pairs={{0,8},{1,9},{2,10},{3,11},{4,28},{5,29},{6,30},{7,31},{8,16},{9,17... | collective-permute-start | bytes 1572872 | tf_op jit(solution)/shard_map/ppermute | solution.py:288
  101.0 16.7 %collective-permute-start.10 = (bf16[4,64,1024]{2,1,0:T(8,128)(2,1)S(1)}, bf16[4,64,1024]{2,1,0:T(8,128)(2,1)S(1)}, u32[]{:S(2)}, u32[]{:S(2)}) collective-permute-start(bf16[4,64,1024]{2,1,0:T(8,128)(2,1)S(1)} %collective-permute-done.9), channel_id=1, source_target_pairs={{0,8},{1,9},{2,10},{3,11},{4,28},{5,29},{6,30},{7,31},{8,16},{9,17... | collective-permute-start | bytes 1572872 | tf_op jit(solution)/shard_map/ppermute | solution.py:288
  117.9 4.8 %collective-permute-start.11 = (bf16[64,4,16,256]{3,2,1,0:T(8,128)(2,1)S(1)}, bf16[64,4,16,256]{3,2,1,0:T(8,128)(2,1)S(1)}, u32[]{:S(2)}, u32[]{:S(2)}) collective-permute-start(bf16[64,4,16,256]{3,2,1,0:T(8,128)(2,1)S(1)} %collective-permute-done.6), channel_id=1, source_target_pairs={{0,1},{1,0},{2,3},{3,2},{4,5},{5,4},{6,7},{7,6},{8,9},{9,8},{10,11... | collective-permute-start | bytes 6291464 | tf_op jit(solution)/shard_map/ppermute | solution.py:295

commit v8 on v7

--- a/solution.py
+++ b/solution.py
@@ -290,9 +290,9 @@
     params = params[:, :16].astype(jnp.int32)
     own_far = pltpu.with_memory_space_constraint(own_a, pltpu.HBM)
     blend_a = blend_centres(where, params, own_far, side_a, cross0, cross123, 0, CUT)
+    far, blend_a, side_b = lax.optimization_barrier((far, blend_a, side_b))
+    far_near = shift(far, perm=CORE)
     part_a = apply_here(blend_a, mine, near)
-    far, part_a, side_b = lax.optimization_barrier((far, part_a, side_b))
-    far_near = shift(far, perm=CORE)
     blend_b = blend_centres(where, params, own_b, side_b, cross0, cross123, CUT, JQ - CUT)
     part_b = apply_here(blend_b, mine, near)
     result = apply_transforms(where, blend_a, blend_b, part_a, part_b, (far, far_near))

time: 191 us -> 189 us (0.990)
  waiting for transfers between devices: 71.7 us -> 62 us
  starting transfers between devices: 25.6 us -> 33.3 us
    ppermute x3, waiting for transfers between devices: 26.7 us -> 20.5 us  [body(): side_b = shift(shift(shift(own_b, perm=BACK), perm=BACK), perm=BACK_END)]
    ppermute x1, waiting for transfers between devices: 6.88 us -> 1.51 us  [body(): cross123 = shift(own123, perm=CROSS)]
    ppermute x1, starting transfers between devices: 3.78 us -> 8.42 us  [body(): near = shift(mine, perm=CORE)]
    ppermute x1, starting transfers between devices: 1.02 us -> 4.7 us  [body(): far_near = shift(far, perm=CORE)]
    ppermute x1, waiting for transfers between devices: 0.18 us -> 3.01 us  [body(): far = shift(mine, perm=PAL)]
  transfers between devices with their start and end apart: 13 -> 13, of which waited for: 10 -> 8; matrix products, arithmetic and copies ran while one was open for 2% -> 2% of each run, Pallas kernels for 8% -> 8%
where the time goes in v8:
time: 189 us
  blocking collectives  62.3 us (33%)
  waiting for transfers between devices  62 us (33%)
  starting transfers between devices  33.3 us (18%)
  Pallas kernels  19.1 us (10%)
  local copies, waits for them, and re-layouts  8.86 us (5%)
  other arithmetic  2.85 us (2%)
    all_to_all x1, blocking collectives, body(): lax.all_to_all(result.reshape(MEM * GRP, 16, 256), AX, 0, 0, axis_index_g...  62.3 us
    ppermute x1, waiting for transfers between devices, body(): own23 = shift(jnp.stack([to_far, mate[1]]), perm=PAL)  25 us
    ppermute x3, waiting for transfers between devices, body(): side_b = shift(shift(shift(own_b, perm=BACK), perm=BACK), perm=BACK_END)  20.5 us
    all_to_all x1, starting transfers between devices, body(): lax.all_to_all(by_col, AX, 0, 0, axis_index_groups=FIELD_GROUPS, tiled=True)  14.9 us
    pallas_call x2, Pallas kernels, blend_centres(): pl.pallas_call(functools.partial(blend_kernel, first, count), out_shape=j...  9.58 us
    all_to_all x1, waiting for transfers between devices, body(): lax.all_to_all(by_col, AX, 0, 0, axis_index_groups=FIELD_GROUPS, tiled=True)  9.21 us
    ppermute x1, starting transfers between devices, body(): near = shift(mine, perm=CORE)  8.42 us
    unnamed x10, local copies, waits for them, and re-layouts  6.27 us
  transfers between devices with their start and end apart: 13, of which 8 were waited for; matrix products, arithmetic and copies ran while one was open for 2% of the time, Pallas kernels for 8%

profile of v8, /device:TPU:1, one launch (start us, length us, event | category | flops | bytes accessed | tf_op | source)
XLA Modules:
  0.0 188.6 jit_solution(16158647161633511264)
XLA Ops:
  0.0 4.1 %copy.16 = bf16[1,16,4,64,256]{4,1,2,3,0:T(8,128)(2,1)} copy(bf16[1,16,4,64,256]{4,3,2,1,0:T(8,128)(2,1)} %param.4) | data formatting | bytes 4194304 | tf_op args[0]
  4.1 14.9 %all-to-all-start = ((bf16[64,4,16,256]{3,2,1,0:T(8,128)(2,1)}), bf16[64,4,16,256]{3,2,1,0:T(8,128)(2,1)S(1)}, u32[]{:S(2)}, u32[]{:S(2)}) async-start(bf16[64,4,16,256]{3,2,1,0:T(8,128)(2,1)} %bitcast.39), calls=%async_computation | async-start | bytes 4194304 | tf_op jit(solution)/shard_map/all_to_all | solution.py:270
  19.3 1.6 copy-done
  20.9 3.0 %shard_map.46 = (bf16[272,1024]{1,0:T(8,128)(2,1)S(1)}, bf16[2,272,1024]{2,1,0:T(8,128)(2,1)S(1)}, bf16[272,1024]{1,0:T(8,128)(2,1)S(1)}) custom-call(s32[3]{0:T(128)S(1)} %pad_add_fusion.where_ref, s32[4,2]{1,0:T(4,128)S(1)} %copy.10.sides_ref, s32[4,2]{1,0:T(4,128)S(1)} %copy.11.quarters_ref, bf16[32,2,16,1024]{3,2,1,0:T(8,128)(2,1)S(1)} %bitcast.35), custom_call_target="tpu_custom_call" | custom-call | flops 1 | bytes 1 | tf_op jit(solution)/shard_map/pallas_call | solution.py:92
  23.8 1.3 collective-permute-start
  25.2 2.4 %collective-permute-done = bf16[2,272,1024]{2,1,0:T(8,128)(2,1)S(1)} collective-permute-done((bf16[2,272,1024]{2,1,0:T(8,128)(2,1)S(1)}, bf16[2,272,1024]{2,1,0:T(8,128)(2,1)S(1)}, u32[]{:S(2)}, u32[]{:S(2)}) %collective-permute-start) | collective-permute-done | bytes 1114144 | tf_op jit(solution)/shard_map/ppermute | solution.py:273
  28.6 25.0 %collective-permute-done.1 = bf16[2,272,1024]{2,1,0:T(8,128)(2,1)S(1)} collective-permute-done((bf16[2,272,1024]{2,1,0:T(8,128)(2,1)S(1)}, bf16[2,272,1024]{2,1,0:T(8,128)(2,1)S(1)}, u32[]{:S(2)}, u32[]{:S(2)}) %collective-permute-start.1) | collective-permute-done | bytes 1114144 | tf_op jit(solution)/shard_map/ppermute | solution.py:274
  54.6 1.3 pad_maximum_fusion
  55.9 1.3 pad_maximum_fusion.1.own
  57.6 9.2 %all-to-all-done = bf16[64,4,16,256]{3,2,1,0:T(8,128)(2,1)S(1)} async-done(((bf16[64,4,16,256]{3,2,1,0:T(8,128)(2,1)}), bf16[64,4,16,256]{3,2,1,0:T(8,128)(2,1)S(1)}, u32[]{:S(2)}, u32[]{:S(2)}) %all-to-all-start) | async-done | bytes 2097184 | tf_op jit(solution)/shard_map/all_to_all | solution.py:270
  66.8 1.2 collective-permute-start.5
  68.1 1.5 collective-permute-start.6
  69.8 9.7 %collective-permute-done.7 = bf16[4,64,1024]{2,1,0:T(8,128)(2,1)S(1)} collective-permute-done((bf16[4,64,1024]{2,1,0:T(8,128)(2,1)S(1)}, bf16[4,64,1024]{2,1,0:T(8,128)(2,1)S(1)}, u32[]{:S(2)}, u32[]{:S(2)}) %collective-permute-start.7) | collective-permute-done | bytes 524320 | tf_op jit(solution)/shard_map/ppermute | solution.py:288
  79.5 10.8 %collective-permute-done.8 = bf16[4,64,1024]{2,1,0:T(8,128)(2,1)S(1)} collective-permute-done((bf16[4,64,1024]{2,1,0:T(8,128)(2,1)S(1)}, bf16[4,64,1024]{2,1,0:T(8,128)(2,1)S(1)}, u32[]{:S(2)}, u32[]{:S(2)}) %collective-permute-start.8) | collective-permute-done | bytes 524320 | tf_op jit(solution)/shard_map/ppermute | solution.py:288
  90.3 8.4 %collective-permute-start.10 = (bf16[64,4,16,256]{3,2,1,0:T(8,128)(2,1)S(1)}, bf16[64,4,16,256]{3,2,1,0:T(8,128)(2,1)S(1)}, u32[]{:S(2)}, u32[]{:S(2)}) collective-permute-start(bf16[64,4,16,256]{3,2,1,0:T(8,128)(2,1)S(1)} %all-to-all-done), channel_id=1, source_target_pairs={{0,1},{1,0},{2,3},{3,2},{4,5},{5,4},{6,7},{7,6},{8,9},{9,8},{10,11... | collective-permute-start | bytes 6291464 | tf_op jit(solution)/shard_map/ppermute | solution.py:289
  98.7 1.5 collective-permute-done.5.cross123
  100.2 6.9 %shard_map.47.blend_ref.blend_a = bf16[16,192,1024]{2,1,0:T(8,128)(2,1)S(1)} custom-call(s32[3]{0:T(128)S(1)} %pad_add_fusion.where_ref, s32[4,16]{1,0:T(4,128)S(1)} %slice_convert_fusion.params_ref, bf16[272,1024]{1,0:T(8,128)(2,1)S(1)} %collective-permute-done.2.cross0, bf16[3,256,1024]{2,1,0:T(8,128)(2,1)S(1)} %collective-permute-done.5.cross123, ...), custom_call_target="tpu_custom_call" | custom-call | flops 1 | bytes 1 | tf_op jit(solution)/shard_map/pallas_call | solution.py:148
  107.2 3.0 %collective-permute-done.4 = bf16[64,4,16,256]{3,2,1,0:T(8,128)(2,1)S(1)} collective-permute-done((bf16[64,4,16,256]{3,2,1,0:T(8,128)(2,1)S(1)}, bf16[64,4,16,256]{3,2,1,0:T(8,128)(2,1)S(1)}, u32[]{:S(2)}, u32[]{:S(2)}) %collective-permute-start.4) | collective-permute-done | bytes 2097184 | tf_op jit(solution)/shard_map/ppermute | solution.py:285
  110.2 4.7 %collective-permute-start.11 = (bf16[64,4,16,256]{3,2,1,0:T(8,128)(2,1)S(1)}, bf16[64,4,16,256]{3,2,1,0:T(8,128)(2,1)S(1)}, u32[]{:S(2)}, u32[]{:S(2)}) collective-permute-start(bf16[64,4,16,256]{3,2,1,0:T(8,128)(2,1)S(1)} %collective-permute-done.4), channel_id=1, source_target_pairs={{0,1},{1,0},{2,3},{3,2},{4,5},{5,4},{6,7},{7,6},{8,9},{9,8},{10,11... | collective-permute-start | bytes 6291464 | tf_op jit(solution)/shard_map/ppermute | solution.py:294
  114.9 2.7 %shard_map.48.blend_ref.blend_b = bf16[16,64,1024]{2,1,0:T(8,128)(2,1)S(1)} custom-call(s32[3]{0:T(128)S(1)} %pad_add_fusion.where_ref, s32[4,16]{1,0:T(4,128)S(1)} %slice_convert_fusion.params_ref, bf16[272,1024]{1,0:T(8,128)(2,1)S(1)} %collective-permute-done.2.cross0, bf16[3,256,1024]{2,1,0:T(8,128)(2,1)S(1)} %collective-permute-done.5.cross123, ...), custom_call_target="tpu_custom_call" | custom-call | flops 1 | bytes 1 | tf_op jit(solution)/shard_map/pallas_call | solution.py:148
  118.5 2.0 %shard_map.49.part_a = f32[4,2,4,192,128]{4,3,2,1,0:T(8,128)S(1)} custom-call(bf16[16,192,1024]{2,1,0:T(8,128)(2,1)S(1)} %shard_map.47.blend_ref.blend_a, bf16[32,2,4,16,256]{4,3,2,1,0:T(8,128)(2,1)S(1)} %bitcast.31, bf16[32,2,4,16,256]{4,3,2,1,0:T(8,128)(2,1)S(1)} %bitcast.33), custom_call_target="tpu_custom_call" | custom-call | flops 1 | bytes 1 | tf_op jit(solution)/shard_map/pallas_call | solution.py:196
  120.6 3.6 %shard_map.51 = bf16[4,32,2,16,256]{4,3,2,1,0:T(8,128)(2,1)S(1)} custom-call(s32[3]{0:T(128)S(1)} %pad_add_fusion.where_ref, bf16[16,192,1024]{2,1,0:T(8,128)(2,1)S(1)} %shard_map.47.blend_ref.blend_a, bf16[16,64,1024]{2,1,0:T(8,128)(2,1)S(1)} %shard_map.48.blend_ref.blend_b, f32[4,2,4,192,128]{4,3,2,1,0:T(8,128)S(1)} %shard_map.49.part_a, ...), custom_call_target="tpu_custom_call" | custom-call | flops 1 | bytes 1 | tf_op jit(solution)/shard_map/pallas_call | solution.py:250
  124.1 62.3 %all_to_all.10 = bf16[256,16,256]{2,1,0:T(8,128)(2,1)S(1)} all-to-all(bf16[256,16,256]{2,1,0:T(8,128)(2,1)S(1)} %bitcast.34), channel_id=1, replica_groups={{6,0,14,8,22,16,30,24,38,32,46,40,54,48,62,56,70,64,78,72,86,80,94,88,1..., dimensions={0} | all-to-all | bytes 4194304 | tf_op jit(solution)/shard_map/all_to_all | solution.py:300
  186.4 2.1 %copy.12 = bf16[4,64,16,256]{3,1,2,0:T(8,128)(2,1)} copy(bf16[4,64,16,256]{3,2,1,0:T(8,128)(2,1)S(1)} %bitcast.40) | data formatting | bytes 4194304 | tf_op jit(solution)/shard_map/reshape | solution.py:303
  (42 shorter events, 3.9 us)
Async XLA Ops:
  4.1 14.9 %copy-start.2 = (s32[1,1,4,2]{2,3,1,0:T(2,128)S(1)}, s32[1,1,4,2]{2,3,1,0:T(2,128)}, u32[]{:S(2)}) copy-start(s32[1,1,4,2]{2,3,1,0:T(2,128)} %param.6) | copy-start | bytes 100
  4.1 15.0 %copy-start.3 = (s32[1,1,4,2]{2,3,1,0:T(2,128)S(1)}, s32[1,1,4,2]{2,3,1,0:T(2,128)}, u32[]{:S(2)}) copy-start(s32[1,1,4,2]{2,3,1,0:T(2,128)} %param.7) | copy-start | bytes 100
  4.1 62.7 %all-to-all-start = ((bf16[64,4,16,256]{3,2,1,0:T(8,128)(2,1)}), bf16[64,4,16,256]{3,2,1,0:T(8,128)(2,1)S(1)}, u32[]{:S(2)}, u32[]{:S(2)}) async-start(bf16[64,4,16,256]{3,2,1,0:T(8,128)(2,1)} %bitcast.39), calls=%async_computation | async-start | bytes 4194304 | tf_op jit(solution)/shard_map/all_to_all | solution.py:270
  19.3 1.6 copy-start
  23.8 3.7 %collective-permute-start = (bf16[2,272,1024]{2,1,0:T(8,128)(2,1)S(1)}, bf16[2,272,1024]{2,1,0:T(8,128)(2,1)S(1)}, u32[]{:S(2)}, u32[]{:S(2)}) collective-permute-start(bf16[2,272,1024]{2,1,0:T(8,128)(2,1)S(1)} %get-tuple-element.17), channel_id=1, source_target_pairs={{0,1},{1,0},{2,3},{3,2},{4,5},{5,4},{6,7},{7,6},{8,9},{9,8},{10,11... | collective-permute-start | bytes 3342344 | tf_op jit(solution)/shard_map/ppermute | solution.py:273
  27.7 25.9 %collective-permute-start.1 = (bf16[2,272,1024]{2,1,0:T(8,128)(2,1)S(1)}, bf16[2,272,1024]{2,1,0:T(8,128)(2,1)S(1)}, u32[]{:S(2)}, u32[]{:S(2)}) collective-permute-start(bf16[2,272,1024]{2,1,0:T(8,128)(2,1)S(1)} %pad_maximum_fusion.2), channel_id=1, source_target_pairs={{0,2},{1,3},{2,0},{3,1},{4,6},{5,7},{6,4},{7,5},{8,10},{9,11},{10,... | collective-permute-start | bytes 3342344 | tf_op jit(solution)/shard_map/ppermute | solution.py:274
  27.8 29.4 %collective-permute-start.2 = (bf16[272,1024]{1,0:T(8,128)(2,1)S(1)}, bf16[272,1024]{1,0:T(8,128)(2,1)S(1)}, u32[]{:S(2)}, u32[]{:S(2)}) collective-permute-start(bf16[272,1024]{1,0:T(8,128)(2,1)S(1)} %get-tuple-element.19), channel_id=1, source_target_pairs={{0,6},{1,7},{2,4},{3,5},{4,2},{5,3},{6,0},{7,1},{8,14},{9,15},{10,... | collective-permute-start | bytes 1671176 | tf_op jit(solution)/shard_map/ppermute | solution.py:275
  53.6 1.0 copy-start.1
  53.6 4.0 %collective-permute-start.3 = (bf16[4,128]{1,0:T(4,128)(2,1)S(1)}, bf16[4,128]{1,0:T(4,128)(2,1)S(1)}, u32[]{:S(2)}, u32[]{:S(2)}) collective-permute-start(bf16[4,128]{1,0:T(4,128)(2,1)S(1)} %pad_maximum_fusion.4), channel_id=1, source_target_pairs={{0,6},{1,7},{2,4},{3,5},{4,2},{5,3},{6,0},{7,1},{8,14},{9,15},{10,... | collective-permute-start | bytes 3080 | tf_op jit(solution)/shard_map/ppermute | solution.py:280
  55.9 1.3 slice-start
  66.8 43.3 %collective-permute-start.4 = (bf16[64,4,16,256]{3,2,1,0:T(8,128)(2,1)S(1)}, bf16[64,4,16,256]{3,2,1,0:T(8,128)(2,1)S(1)}, u32[]{:S(2)}, u32[]{:S(2)}) collective-permute-start(bf16[64,4,16,256]{3,2,1,0:T(8,128)(2,1)S(1)} %all-to-all-done), channel_id=1, source_target_pairs={{0,2},{1,3},{2,0},{3,1},{4,6},{5,7},{6,4},{7,5},{8,10},{9,11},{10,... | collective-permute-start | bytes 6291464 | tf_op jit(solution)/shard_map/ppermute | solution.py:285
  66.8 33.4 %collective-permute-start.5 = (bf16[3,256,1024]{2,1,0:T(8,128)(2,1)}, bf16[3,256,1024]{2,1,0:T(8,128)(2,1)S(1)}, u32[]{:S(2)}, u32[]{:S(2)}) collective-permute-start(bf16[3,256,1024]{2,1,0:T(8,128)(2,1)} %pad_maximum_fusion), channel_id=1, source_target_pairs={{0,6},{1,7},{2,4},{3,5},{4,2},{5,3},{6,0},{7,1},{8,14},{9,15},{10,... | collective-permute-start | bytes 4718600 | tf_op jit(solution)/shard_map/ppermute | solution.py:286
  68.1 32.2 %collective-permute-start.6 = (bf16[4,192,1024]{2,1,0:T(8,128)(2,1)}, bf16[4,192,1024]{2,1,0:T(8,128)(2,1)S(1)}, u32[]{:S(2)}, u32[]{:S(2)}) collective-permute-start(bf16[4,192,1024]{2,1,0:T(8,128)(2,1)} %pad_maximum_fusion.1.own), channel_id=1, source_target_pairs={{0,248},{1,249},{2,250},{3,251},{4,12},{5,13},{6,14},{7,15},{8,0},... | collective-permute-start | bytes 4718600 | tf_op jit(solution)/shard_map/ppermute | solution.py:287
  69.5 9.9 %collective-permute-start.7 = (bf16[4,64,1024]{2,1,0:T(8,128)(2,1)S(1)}, bf16[4,64,1024]{2,1,0:T(8,128)(2,1)S(1)}, u32[]{:S(2)}, u32[]{:S(2)}) collective-permute-start(bf16[4,64,1024]{2,1,0:T(8,128)(2,1)S(1)} %pad_maximum_fusion.3.own), channel_id=1, source_target_pairs={{0,8},{1,9},{2,10},{3,11},{4,28},{5,29},{6,30},{7,31},{8,16},{9,17... | collective-permute-start | bytes 1572872 | tf_op jit(solution)/shard_map/ppermute | solution.py:288
  79.5 10.8 %collective-permute-start.8 = (bf16[4,64,1024]{2,1,0:T(8,128)(2,1)S(1)}, bf16[4,64,1024]{2,1,0:T(8,128)(2,1)S(1)}, u32[]{:S(2)}, u32[]{:S(2)}) collective-permute-start(bf16[4,64,1024]{2,1,0:T(8,128)(2,1)S(1)} %collective-permute-done.7), channel_id=1, source_target_pairs={{0,8},{1,9},{2,10},{3,11},{4,28},{5,29},{6,30},{7,31},{8,16},{9,17... | collective-permute-start | bytes 1572872 | tf_op jit(solution)/shard_map/ppermute | solution.py:288
  90.3 16.9 %collective-permute-start.9 = (bf16[4,64,1024]{2,1,0:T(8,128)(2,1)S(1)}, bf16[4,64,1024]{2,1,0:T(8,128)(2,1)S(1)}, u32[]{:S(2)}, u32[]{:S(2)}) collective-permute-start(bf16[4,64,1024]{2,1,0:T(8,128)(2,1)S(1)} %collective-permute-done.8), channel_id=1, source_target_pairs={{0,8},{1,9},{2,10},{3,11},{4,28},{5,29},{6,30},{7,31},{8,16},{9,17... | collective-permute-start | bytes 1572872 | tf_op jit(solution)/shard_map/ppermute | solution.py:288
  90.3 27.3 %collective-permute-start.10 = (bf16[64,4,16,256]{3,2,1,0:T(8,128)(2,1)S(1)}, bf16[64,4,16,256]{3,2,1,0:T(8,128)(2,1)S(1)}, u32[]{:S(2)}, u32[]{:S(2)}) collective-permute-start(bf16[64,4,16,256]{3,2,1,0:T(8,128)(2,1)S(1)} %all-to-all-done), channel_id=1, source_target_pairs={{0,1},{1,0},{2,3},{3,2},{4,5},{5,4},{6,7},{7,6},{8,9},{9,8},{10,11... | collective-permute-start | bytes 6291464 | tf_op jit(solution)/shard_map/ppermute | solution.py:289
  110.2 10.4 %collective-permute-start.11 = (bf16[64,4,16,256]{3,2,1,0:T(8,128)(2,1)S(1)}, bf16[64,4,16,256]{3,2,1,0:T(8,128)(2,1)S(1)}, u32[]{:S(2)}, u32[]{:S(2)}) collective-permute-start(bf16[64,4,16,256]{3,2,1,0:T(8,128)(2,1)S(1)} %collective-permute-done.4), channel_id=1, source_target_pairs={{0,1},{1,0},{2,3},{3,2},{4,5},{5,4},{6,7},{7,6},{8,9},{9,8},{10,11... | collective-permute-start | bytes 6291464 | tf_op jit(solution)/shard_map/ppermute | solution.py:294

commit v9 on v8

--- a/solution.py
+++ b/solution.py
@@ -173,7 +173,7 @@
 def here_kernel(blend_ref, mine, near, out_ref):
     count = blend_ref.shape[1]
 
-    @pl.loop(0, 4, unroll=2)
+    @pl.loop(0, 4, unroll=4)
     def _(row):
         for pair in range(2):
             at = slice(pair * 128, pair * 128 + 128)
@@ -207,7 +207,7 @@
     quarter = where_ref[2]
     rest = JQ - CUT
 
-    @pl.loop(0, 4, unroll=2)
+    @pl.loop(0, 4, unroll=4)
     def _(row):
         for pair in range(2):
             at = slice(pair * 128, pair * 128 + 128)

time: 189 us -> 189 us (level)
  no operation moved by 1% of the time
where the time goes in v9:
time: 189 us; the launch traced here: 188 us
  blocking collectives  62.3 us (33%)
  waiting for transfers between devices  62 us (33%)
  starting transfers between devices  33.3 us (18%)
  Pallas kernels  18.8 us (10%)
  local copies, waits for them, and re-layouts  8.86 us (5%)
  other arithmetic  2.85 us (2%)
    all_to_all x1, blocking collectives, body(): lax.all_to_all(result.reshape(MEM * GRP, 16, 256), AX, 0, 0, axis_index_g...  62.3 us
    ppermute x1, waiting for transfers between devices, body(): own23 = shift(jnp.stack([to_far, mate[1]]), perm=PAL)  25 us
    ppermute x3, waiting for transfers between devices, body(): side_b = shift(shift(shift(own_b, perm=BACK), perm=BACK), perm=BACK_END)  20.5 us
    all_to_all x1, starting transfers between devices, body(): lax.all_to_all(by_col, AX, 0, 0, axis_index_groups=FIELD_GROUPS, tiled=True)  14.9 us
    pallas_call x2, Pallas kernels, blend_centres(): pl.pallas_call(functools.partial(blend_kernel, first, count), out_shape=j...  9.58 us
    all_to_all x1, waiting for transfers between devices, body(): lax.all_to_all(by_col, AX, 0, 0, axis_index_groups=FIELD_GROUPS, tiled=True)  9.21 us
    ppermute x1, starting transfers between devices, body(): near = shift(mine, perm=CORE)  8.42 us
    unnamed x10, local copies, waits for them, and re-layouts  6.27 us
  transfers between devices with their start and end apart: 13, of which 8 were waited for; matrix products, arithmetic and copies ran while one was open for 2% of the time, Pallas kernels for 8%

profile of v9, /device:TPU:1, one launch (start us, length us, event | category | flops | bytes accessed | tf_op | source)
XLA Modules:
  0.0 188.3 jit_solution(6576303914052410871)
XLA Ops:
  0.0 4.1 %copy.16 = bf16[1,16,4,64,256]{4,1,2,3,0:T(8,128)(2,1)} copy(bf16[1,16,4,64,256]{4,3,2,1,0:T(8,128)(2,1)} %param.4) | data formatting | bytes 4194304 | tf_op args[0]
  4.1 14.9 %all-to-all-start = ((bf16[64,4,16,256]{3,2,1,0:T(8,128)(2,1)}), bf16[64,4,16,256]{3,2,1,0:T(8,128)(2,1)S(1)}, u32[]{:S(2)}, u32[]{:S(2)}) async-start(bf16[64,4,16,256]{3,2,1,0:T(8,128)(2,1)} %bitcast.39), calls=%async_computation | async-start | bytes 4194304 | tf_op jit(solution)/shard_map/all_to_all | solution.py:270
  19.3 1.6 copy-done
  20.9 3.0 %shard_map.46 = (bf16[272,1024]{1,0:T(8,128)(2,1)S(1)}, bf16[2,272,1024]{2,1,0:T(8,128)(2,1)S(1)}, bf16[272,1024]{1,0:T(8,128)(2,1)S(1)}) custom-call(s32[3]{0:T(128)S(1)} %pad_add_fusion.where_ref, s32[4,2]{1,0:T(4,128)S(1)} %copy.10.sides_ref, s32[4,2]{1,0:T(4,128)S(1)} %copy.11.quarters_ref, bf16[32,2,16,1024]{3,2,1,0:T(8,128)(2,1)S(1)} %bitcast.35), custom_call_target="tpu_custom_call" | custom-call | flops 1 | bytes 1 | tf_op jit(solution)/shard_map/pallas_call | solution.py:92
  23.8 1.3 collective-permute-start
  25.2 2.4 %collective-permute-done = bf16[2,272,1024]{2,1,0:T(8,128)(2,1)S(1)} collective-permute-done((bf16[2,272,1024]{2,1,0:T(8,128)(2,1)S(1)}, bf16[2,272,1024]{2,1,0:T(8,128)(2,1)S(1)}, u32[]{:S(2)}, u32[]{:S(2)}) %collective-permute-start) | collective-permute-done | bytes 1114144 | tf_op jit(solution)/shard_map/ppermute | solution.py:273
  28.6 25.0 %collective-permute-done.1 = bf16[2,272,1024]{2,1,0:T(8,128)(2,1)S(1)} collective-permute-done((bf16[2,272,1024]{2,1,0:T(8,128)(2,1)S(1)}, bf16[2,272,1024]{2,1,0:T(8,128)(2,1)S(1)}, u32[]{:S(2)}, u32[]{:S(2)}) %collective-permute-start.1) | collective-permute-done | bytes 1114144 | tf_op jit(solution)/shard_map/ppermute | solution.py:274
  54.6 1.3 pad_maximum_fusion
  55.9 1.3 pad_maximum_fusion.1.own
  57.6 9.2 %all-to-all-done = bf16[64,4,16,256]{3,2,1,0:T(8,128)(2,1)S(1)} async-done(((bf16[64,4,16,256]{3,2,1,0:T(8,128)(2,1)}), bf16[64,4,16,256]{3,2,1,0:T(8,128)(2,1)S(1)}, u32[]{:S(2)}, u32[]{:S(2)}) %all-to-all-start) | async-done | bytes 2097184 | tf_op jit(solution)/shard_map/all_to_all | solution.py:270
  66.8 1.2 collective-permute-start.5
  68.1 1.5 collective-permute-start.6
  69.8 9.7 %collective-permute-done.7 = bf16[4,64,1024]{2,1,0:T(8,128)(2,1)S(1)} collective-permute-done((bf16[4,64,1024]{2,1,0:T(8,128)(2,1)S(1)}, bf16[4,64,1024]{2,1,0:T(8,128)(2,1)S(1)}, u32[]{:S(2)}, u32[]{:S(2)}) %collective-permute-start.7) | collective-permute-done | bytes 524320 | tf_op jit(solution)/shard_map/ppermute | solution.py:288
  79.5 10.8 %collective-permute-done.8 = bf16[4,64,1024]{2,1,0:T(8,128)(2,1)S(1)} collective-permute-done((bf16[4,64,1024]{2,1,0:T(8,128)(2,1)S(1)}, bf16[4,64,1024]{2,1,0:T(8,128)(2,1)S(1)}, u32[]{:S(2)}, u32[]{:S(2)}) %collective-permute-start.8) | collective-permute-done | bytes 524320 | tf_op jit(solution)/shard_map/ppermute | solution.py:288
  90.3 8.4 %collective-permute-start.10 = (bf16[64,4,16,256]{3,2,1,0:T(8,128)(2,1)S(1)}, bf16[64,4,16,256]{3,2,1,0:T(8,128)(2,1)S(1)}, u32[]{:S(2)}, u32[]{:S(2)}) collective-permute-start(bf16[64,4,16,256]{3,2,1,0:T(8,128)(2,1)S(1)} %all-to-all-done), channel_id=1, source_target_pairs={{0,1},{1,0},{2,3},{3,2},{4,5},{5,4},{6,7},{7,6},{8,9},{9,8},{10,11... | collective-permute-start | bytes 6291464 | tf_op jit(solution)/shard_map/ppermute | solution.py:289
  98.7 1.5 collective-permute-done.5.cross123
  100.2 6.9 %shard_map.47.blend_ref.blend_a = bf16[16,192,1024]{2,1,0:T(8,128)(2,1)S(1)} custom-call(s32[3]{0:T(128)S(1)} %pad_add_fusion.where_ref, s32[4,16]{1,0:T(4,128)S(1)} %slice_convert_fusion.params_ref, bf16[272,1024]{1,0:T(8,128)(2,1)S(1)} %collective-permute-done.2.cross0, bf16[3,256,1024]{2,1,0:T(8,128)(2,1)S(1)} %collective-permute-done.5.cross123, ...), custom_call_target="tpu_custom_call" | custom-call | flops 1 | bytes 1 | tf_op jit(solution)/shard_map/pallas_call | solution.py:148
  107.2 3.0 %collective-permute-done.4 = bf16[64,4,16,256]{3,2,1,0:T(8,128)(2,1)S(1)} collective-permute-done((bf16[64,4,16,256]{3,2,1,0:T(8,128)(2,1)S(1)}, bf16[64,4,16,256]{3,2,1,0:T(8,128)(2,1)S(1)}, u32[]{:S(2)}, u32[]{:S(2)}) %collective-permute-start.4) | collective-permute-done | bytes 2097184 | tf_op jit(solution)/shard_map/ppermute | solution.py:285
  110.2 4.7 %collective-permute-start.11 = (bf16[64,4,16,256]{3,2,1,0:T(8,128)(2,1)S(1)}, bf16[64,4,16,256]{3,2,1,0:T(8,128)(2,1)S(1)}, u32[]{:S(2)}, u32[]{:S(2)}) collective-permute-start(bf16[64,4,16,256]{3,2,1,0:T(8,128)(2,1)S(1)} %collective-permute-done.4), channel_id=1, source_target_pairs={{0,1},{1,0},{2,3},{3,2},{4,5},{5,4},{6,7},{7,6},{8,9},{9,8},{10,11... | collective-permute-start | bytes 6291464 | tf_op jit(solution)/shard_map/ppermute | solution.py:294
  114.9 2.7 %shard_map.48.blend_ref.blend_b = bf16[16,64,1024]{2,1,0:T(8,128)(2,1)S(1)} custom-call(s32[3]{0:T(128)S(1)} %pad_add_fusion.where_ref, s32[4,16]{1,0:T(4,128)S(1)} %slice_convert_fusion.params_ref, bf16[272,1024]{1,0:T(8,128)(2,1)S(1)} %collective-permute-done.2.cross0, bf16[3,256,1024]{2,1,0:T(8,128)(2,1)S(1)} %collective-permute-done.5.cross123, ...), custom_call_target="tpu_custom_call" | custom-call | flops 1 | bytes 1 | tf_op jit(solution)/shard_map/pallas_call | solution.py:148
  118.3 1.9 %shard_map.49.part_a = f32[4,2,4,192,128]{4,3,2,1,0:T(8,128)S(1)} custom-call(bf16[16,192,1024]{2,1,0:T(8,128)(2,1)S(1)} %shard_map.47.blend_ref.blend_a, bf16[32,2,4,16,256]{4,3,2,1,0:T(8,128)(2,1)S(1)} %bitcast.31, bf16[32,2,4,16,256]{4,3,2,1,0:T(8,128)(2,1)S(1)} %bitcast.33), custom_call_target="tpu_custom_call" | custom-call | flops 1 | bytes 1 | tf_op jit(solution)/shard_map/pallas_call | solution.py:196
  120.2 3.6 %shard_map.51 = bf16[4,32,2,16,256]{4,3,2,1,0:T(8,128)(2,1)S(1)} custom-call(s32[3]{0:T(128)S(1)} %pad_add_fusion.where_ref, bf16[16,192,1024]{2,1,0:T(8,128)(2,1)S(1)} %shard_map.47.blend_ref.blend_a, bf16[16,64,1024]{2,1,0:T(8,128)(2,1)S(1)} %shard_map.48.blend_ref.blend_b, f32[4,2,4,192,128]{4,3,2,1,0:T(8,128)S(1)} %shard_map.49.part_a, ...), custom_call_target="tpu_custom_call" | custom-call | flops 1 | bytes 1 | tf_op jit(solution)/shard_map/pallas_call | solution.py:250
  123.9 62.3 %all_to_all.10 = bf16[256,16,256]{2,1,0:T(8,128)(2,1)S(1)} all-to-all(bf16[256,16,256]{2,1,0:T(8,128)(2,1)S(1)} %bitcast.34), channel_id=1, replica_groups={{6,0,14,8,22,16,30,24,38,32,46,40,54,48,62,56,70,64,78,72,86,80,94,88,1..., dimensions={0} | all-to-all | bytes 4194304 | tf_op jit(solution)/shard_map/all_to_all | solution.py:300
  186.2 2.1 %copy.12 = bf16[4,64,16,256]{3,1,2,0:T(8,128)(2,1)} copy(bf16[4,64,16,256]{3,2,1,0:T(8,128)(2,1)S(1)} %bitcast.40) | data formatting | bytes 4194304 | tf_op jit(solution)/shard_map/reshape | solution.py:303
  (42 shorter events, 3.7 us)
Async XLA Ops:
  4.1 14.9 %copy-start.2 = (s32[1,1,4,2]{2,3,1,0:T(2,128)S(1)}, s32[1,1,4,2]{2,3,1,0:T(2,128)}, u32[]{:S(2)}) copy-start(s32[1,1,4,2]{2,3,1,0:T(2,128)} %param.6) | copy-start | bytes 100
  4.1 15.0 %copy-start.3 = (s32[1,1,4,2]{2,3,1,0:T(2,128)S(1)}, s32[1,1,4,2]{2,3,1,0:T(2,128)}, u32[]{:S(2)}) copy-start(s32[1,1,4,2]{2,3,1,0:T(2,128)} %param.7) | copy-start | bytes 100
  4.1 62.7 %all-to-all-start = ((bf16[64,4,16,256]{3,2,1,0:T(8,128)(2,1)}), bf16[64,4,16,256]{3,2,1,0:T(8,128)(2,1)S(1)}, u32[]{:S(2)}, u32[]{:S(2)}) async-start(bf16[64,4,16,256]{3,2,1,0:T(8,128)(2,1)} %bitcast.39), calls=%async_computation | async-start | bytes 4194304 | tf_op jit(solution)/shard_map/all_to_all | solution.py:270
  19.3 1.6 copy-start
  23.8 3.7 %collective-permute-start = (bf16[2,272,1024]{2,1,0:T(8,128)(2,1)S(1)}, bf16[2,272,1024]{2,1,0:T(8,128)(2,1)S(1)}, u32[]{:S(2)}, u32[]{:S(2)}) collective-permute-start(bf16[2,272,1024]{2,1,0:T(8,128)(2,1)S(1)} %get-tuple-element.17), channel_id=1, source_target_pairs={{0,1},{1,0},{2,3},{3,2},{4,5},{5,4},{6,7},{7,6},{8,9},{9,8},{10,11... | collective-permute-start | bytes 3342344 | tf_op jit(solution)/shard_map/ppermute | solution.py:273
  27.7 25.9 %collective-permute-start.1 = (bf16[2,272,1024]{2,1,0:T(8,128)(2,1)S(1)}, bf16[2,272,1024]{2,1,0:T(8,128)(2,1)S(1)}, u32[]{:S(2)}, u32[]{:S(2)}) collective-permute-start(bf16[2,272,1024]{2,1,0:T(8,128)(2,1)S(1)} %pad_maximum_fusion.2), channel_id=1, source_target_pairs={{0,2},{1,3},{2,0},{3,1},{4,6},{5,7},{6,4},{7,5},{8,10},{9,11},{10,... | collective-permute-start | bytes 3342344 | tf_op jit(solution)/shard_map/ppermute | solution.py:274
  27.8 29.4 %collective-permute-start.2 = (bf16[272,1024]{1,0:T(8,128)(2,1)S(1)}, bf16[272,1024]{1,0:T(8,128)(2,1)S(1)}, u32[]{:S(2)}, u32[]{:S(2)}) collective-permute-start(bf16[272,1024]{1,0:T(8,128)(2,1)S(1)} %get-tuple-element.19), channel_id=1, source_target_pairs={{0,6},{1,7},{2,4},{3,5},{4,2},{5,3},{6,0},{7,1},{8,14},{9,15},{10,... | collective-permute-start | bytes 1671176 | tf_op jit(solution)/shard_map/ppermute | solution.py:275
  53.6 1.0 copy-start.1
  53.6 4.0 %collective-permute-start.3 = (bf16[4,128]{1,0:T(4,128)(2,1)S(1)}, bf16[4,128]{1,0:T(4,128)(2,1)S(1)}, u32[]{:S(2)}, u32[]{:S(2)}) collective-permute-start(bf16[4,128]{1,0:T(4,128)(2,1)S(1)} %pad_maximum_fusion.4), channel_id=1, source_target_pairs={{0,6},{1,7},{2,4},{3,5},{4,2},{5,3},{6,0},{7,1},{8,14},{9,15},{10,... | collective-permute-start | bytes 3080 | tf_op jit(solution)/shard_map/ppermute | solution.py:280
  55.9 1.3 slice-start
  66.8 43.3 %collective-permute-start.4 = (bf16[64,4,16,256]{3,2,1,0:T(8,128)(2,1)S(1)}, bf16[64,4,16,256]{3,2,1,0:T(8,128)(2,1)S(1)}, u32[]{:S(2)}, u32[]{:S(2)}) collective-permute-start(bf16[64,4,16,256]{3,2,1,0:T(8,128)(2,1)S(1)} %all-to-all-done), channel_id=1, source_target_pairs={{0,2},{1,3},{2,0},{3,1},{4,6},{5,7},{6,4},{7,5},{8,10},{9,11},{10,... | collective-permute-start | bytes 6291464 | tf_op jit(solution)/shard_map/ppermute | solution.py:285
  66.8 33.4 %collective-permute-start.5 = (bf16[3,256,1024]{2,1,0:T(8,128)(2,1)}, bf16[3,256,1024]{2,1,0:T(8,128)(2,1)S(1)}, u32[]{:S(2)}, u32[]{:S(2)}) collective-permute-start(bf16[3,256,1024]{2,1,0:T(8,128)(2,1)} %pad_maximum_fusion), channel_id=1, source_target_pairs={{0,6},{1,7},{2,4},{3,5},{4,2},{5,3},{6,0},{7,1},{8,14},{9,15},{10,... | collective-permute-start | bytes 4718600 | tf_op jit(solution)/shard_map/ppermute | solution.py:286
  68.1 32.2 %collective-permute-start.6 = (bf16[4,192,1024]{2,1,0:T(8,128)(2,1)}, bf16[4,192,1024]{2,1,0:T(8,128)(2,1)S(1)}, u32[]{:S(2)}, u32[]{:S(2)}) collective-permute-start(bf16[4,192,1024]{2,1,0:T(8,128)(2,1)} %pad_maximum_fusion.1.own), channel_id=1, source_target_pairs={{0,248},{1,249},{2,250},{3,251},{4,12},{5,13},{6,14},{7,15},{8,0},... | collective-permute-start | bytes 4718600 | tf_op jit(solution)/shard_map/ppermute | solution.py:287
  69.5 9.9 %collective-permute-start.7 = (bf16[4,64,1024]{2,1,0:T(8,128)(2,1)S(1)}, bf16[4,64,1024]{2,1,0:T(8,128)(2,1)S(1)}, u32[]{:S(2)}, u32[]{:S(2)}) collective-permute-start(bf16[4,64,1024]{2,1,0:T(8,128)(2,1)S(1)} %pad_maximum_fusion.3.own), channel_id=1, source_target_pairs={{0,8},{1,9},{2,10},{3,11},{4,28},{5,29},{6,30},{7,31},{8,16},{9,17... | collective-permute-start | bytes 1572872 | tf_op jit(solution)/shard_map/ppermute | solution.py:288
  79.5 10.8 %collective-permute-start.8 = (bf16[4,64,1024]{2,1,0:T(8,128)(2,1)S(1)}, bf16[4,64,1024]{2,1,0:T(8,128)(2,1)S(1)}, u32[]{:S(2)}, u32[]{:S(2)}) collective-permute-start(bf16[4,64,1024]{2,1,0:T(8,128)(2,1)S(1)} %collective-permute-done.7), channel_id=1, source_target_pairs={{0,8},{1,9},{2,10},{3,11},{4,28},{5,29},{6,30},{7,31},{8,16},{9,17... | collective-permute-start | bytes 1572872 | tf_op jit(solution)/shard_map/ppermute | solution.py:288
  90.3 16.9 %collective-permute-start.9 = (bf16[4,64,1024]{2,1,0:T(8,128)(2,1)S(1)}, bf16[4,64,1024]{2,1,0:T(8,128)(2,1)S(1)}, u32[]{:S(2)}, u32[]{:S(2)}) collective-permute-start(bf16[4,64,1024]{2,1,0:T(8,128)(2,1)S(1)} %collective-permute-done.8), channel_id=1, source_target_pairs={{0,8},{1,9},{2,10},{3,11},{4,28},{5,29},{6,30},{7,31},{8,16},{9,17... | collective-permute-start | bytes 1572872 | tf_op jit(solution)/shard_map/ppermute | solution.py:288
  90.3 27.3 %collective-permute-start.10 = (bf16[64,4,16,256]{3,2,1,0:T(8,128)(2,1)S(1)}, bf16[64,4,16,256]{3,2,1,0:T(8,128)(2,1)S(1)}, u32[]{:S(2)}, u32[]{:S(2)}) collective-permute-start(bf16[64,4,16,256]{3,2,1,0:T(8,128)(2,1)S(1)} %all-to-all-done), channel_id=1, source_target_pairs={{0,1},{1,0},{2,3},{3,2},{4,5},{5,4},{6,7},{7,6},{8,9},{9,8},{10,11... | collective-permute-start | bytes 6291464 | tf_op jit(solution)/shard_map/ppermute | solution.py:289
  110.2 10.1 %collective-permute-start.11 = (bf16[64,4,16,256]{3,2,1,0:T(8,128)(2,1)S(1)}, bf16[64,4,16,256]{3,2,1,0:T(8,128)(2,1)S(1)}, u32[]{:S(2)}, u32[]{:S(2)}) collective-permute-start(bf16[64,4,16,256]{3,2,1,0:T(8,128)(2,1)S(1)} %collective-permute-done.4), channel_id=1, source_target_pairs={{0,1},{1,0},{2,3},{3,2},{4,5},{5,4},{6,7},{7,6},{8,9},{9,8},{10,11... | collective-permute-start | bytes 6291464 | tf_op jit(solution)/shard_map/ppermute | solution.py:294
